TPU v7x, 128 devices: a whole 4x4x4 slice. The times are simulated.
128 devices in a mesh: pool: 2 (over y_lo), ctx: 4 (over z), mp: 16 (over y_hi, x, core).
Axes of the slice: x: 4, y: 4 (y_hi: 2, y_lo: 2; y = y_hi * 2 + y_lo), z: 4, core: 2. Of those that a mesh axis runs over, the one named last changes fastest.
Arguments:
- tokens: bfloat16 [2, 2048, 4096], P('pool', 'ctx', 'mp'), may hold values from -2.5 to 2.5
- norm_gain: float32 [4096], replicated, may hold values from 0.5 to 1.5
- cross_gain: float32 [4096], replicated, may hold values from 0.1 to 1.9
- w_query: bfloat16 [4096, 4096], P(None, 'mp'), may hold values from -8 to 8
- w_key: bfloat16 [4096, 4096], P(None, 'mp'), may hold values from -0.09375 to 0.09375
- w_value: bfloat16 [4096, 4096], P(None, 'mp'), may hold values from -0.09375 to 0.09375
- w_out: bfloat16 [4096, 4096], P('mp'), may hold values from -0.125 to 0.125
- w_cross_query: bfloat16 [4096, 4096], P(None, 'mp'), may hold values from -8 to 8
- w_cross_kv: bfloat16 [2, 896, 4096], P(None, None, 'mp'), may hold values from -0.1875 to 0.1875
- w_cross_out: bfloat16 [4096, 4096], P('mp'), may hold values from -0.125 to 0.125
- encoded: bfloat16 [512, 128, 896], P(('pool', 'ctx'), 'mp'), may hold values from -6 to 6
- owners: int32 [2, 32, 2], replicated, may hold values from 0 to 7, all different within a row; in each aligned block of 8 rows (0 to 7, 8 to 15, ..., all dimensions but the last counted through in order) at most 4 rows name the same one
- slots: int32 [2, 32, 2], replicated, may hold values from 0 to 63
Outputs:
- layer_out: bfloat16 [2, 2048, 4096], P('pool', 'ctx', 'mp')
Inputs may be any that keep to these rules, and one draw needn't show every extreme that they name: The 2 neighbours of a span have different owners; among the spans of one index of pool and ctx (aligned blocks of 8 spans, sequence by sequence) no owner is named more than 4 times.
All inputs are finite; a program needn't handle non-finite values.
Results may differ from a plain program's by a relative error of at most 0.035.
Values may be sent and summed in bfloat16 or wider, within the bound.
No kernel may reach another device: no remote copies, remote signals or barrier semaphores. Data moves between devices by JAX's collectives and lax.ppermute only.
A program may use at most 128 MiB of HBM per device.

v0:
```python
import jax
import jax.numpy as jnp
from jax import lax
from jax.sharding import PartitionSpec as P

HEAD = 128
SPAN = 64
NB_TOK = 128
NB_PER = 2


norm_eps = 1e-05
mask_floor = -1e30


def from_behind(block, axis, distance):
    devices = range(lax.axis_size(axis))
    route = [(i - distance, i) for i in devices if i - distance in devices]
    return lax.ppermute(block, axis, route)


def fetch_neighbours(encoded, owners, slots, w_cross_kv):
    group_count = lax.axis_size(("pool", "ctx"))
    my_group = lax.axis_index(("pool", "ctx"))
    per_group = owners.size // group_count
    capacity = max(2, 2 * per_group // group_count)
    owner_table = owners.reshape(group_count, per_group)
    slot_table = slots.reshape(group_count, per_group)
    matched = (owner_table == my_group).astype(jnp.int32)
    order_rank = jnp.cumsum(matched, axis=1) - 1
    slot_index = jnp.arange(capacity, dtype=jnp.int32)
    picked = matched[:, None, :] * (order_rank[:, None, :] == slot_index[None, :, None]).astype(
        jnp.int32
    )
    source_rows = jnp.sum(picked * slot_table[:, None, :], axis=2).reshape(-1)
    filled = jnp.sum(picked, axis=2).reshape(-1)
    outgoing = jnp.where(
        filled[:, None, None] > 0, encoded[source_rows], jnp.zeros((), encoded.dtype)
    )
    outgoing = outgoing.reshape((group_count, capacity) + encoded.shape[1:])
    incoming = lax.all_to_all(outgoing, ("pool", "ctx"), split_axis=0, concat_axis=0, tiled=True)
    wanted = lax.dynamic_index_in_dim(owner_table, my_group, 0, keepdims=False)
    positions = jnp.arange(per_group, dtype=jnp.int32)
    same_owner = (wanted[:, None] == wanted[None, :]).astype(jnp.int32)
    before_this = (positions[None, :] < positions[:, None]).astype(jnp.int32)
    arrival = wanted * capacity + jnp.sum(same_owner * before_this, axis=1)
    arrived = incoming.reshape((group_count * capacity,) + encoded.shape[1:])[arrival]
    return jnp.einsum(
        "nrw,cwd->cnrd",
        lax.all_gather(arrived, "mp", axis=1, tiled=True),
        w_cross_kv,
        preferred_element_type=jnp.float32,
    ).astype(jnp.bfloat16)


def self_attention(queries, key_rows, value_rows, first_row):
    tok_rows, head_count, head_dim = queries.shape
    score_scale = head_dim ** (-0.5)
    query_pos = first_row + jnp.arange(tok_rows, dtype=jnp.int32)
    last_row = first_row + tok_rows - 1
    start_state = (
        jnp.full((head_count, tok_rows), mask_floor, jnp.float32),
        jnp.zeros((head_count, tok_rows), jnp.float32),
        jnp.zeros((head_count, tok_rows, head_dim), jnp.float32),
    )
    pieces = (
        lax.all_gather(key_rows, "ctx", axis=0, tiled=True),
        lax.all_gather(value_rows, "ctx", axis=0, tiled=True),
    )

    def update(state):
        running_max, running_sum, running_out = state
        keys_here, values_here = pieces
        key_pos = jnp.arange(keys_here.shape[0], dtype=jnp.int32)
        allowed = (key_pos[None, :] <= query_pos[:, None])[None]
        scores = (
            jnp.einsum("qhe,khe->hqk", queries, keys_here, preferred_element_type=jnp.float32)
            * score_scale
        )
        scores = jnp.where(allowed, scores, mask_floor)
        new_max = jnp.maximum(running_max, jnp.max(scores, axis=-1))
        weights = jnp.where(allowed, jnp.exp(scores - new_max[..., None]), 0.0)
        running_sum = jnp.sum(weights, axis=-1)
        running_out = jnp.einsum(
            "hqk,khe->hqe",
            weights.astype(jnp.bfloat16),
            values_here,
            preferred_element_type=jnp.float32,
        )
        return (new_max, running_sum, running_out)

    running_max, running_sum, running_out = lax.cond(
        jnp.int32(0) <= last_row, update, lambda state: state, start_state
    )
    attended = (running_out / running_sum[..., None]).astype(jnp.bfloat16)
    return jnp.transpose(attended, (1, 0, 2)).reshape(tok_rows, head_count * head_dim)


def cross_attention(queries, neighbour_kv):
    tok_rows, head_count, head_dim = queries.shape
    score_scale = head_dim ** (-0.5)
    span_count = neighbour_kv.shape[1] // NB_PER
    grouped = neighbour_kv.reshape(2, span_count, NB_PER * NB_TOK, head_count, head_dim)
    earlier = from_behind(grouped[:, -1:], "ctx", 1)
    extended = jnp.concatenate([earlier, grouped], axis=1)
    padded = jnp.concatenate(
        [
            jnp.zeros((1, head_count, head_dim), jnp.bfloat16),
            queries,
            jnp.zeros((SPAN - 1, head_count, head_dim), jnp.bfloat16),
        ],
        axis=0,
    )
    padded = padded.reshape(span_count + 1, SPAN, head_count, head_dim)
    scores = (
        jnp.einsum("cmhe,cnhe->chmn", padded, extended[0], preferred_element_type=jnp.float32)
        * score_scale
    )
    peak = jnp.max(scores, axis=-1, keepdims=True)
    weights = jnp.exp(scores - peak)
    totals = jnp.sum(weights, axis=-1)
    mixed_out = jnp.einsum(
        "chmn,cnhe->cmhe",
        weights.astype(jnp.bfloat16),
        extended[1],
        preferred_element_type=jnp.float32,
    )
    mixed_out = (mixed_out / jnp.transpose(totals, (0, 2, 1))[..., None]).astype(jnp.bfloat16)
    mixed_out = mixed_out.reshape((span_count + 1) * SPAN, head_count * head_dim)
    return mixed_out[1 : tok_rows + 1]


def per_device(
    tokens,
    norm_gain,
    cross_gain,
    w_query,
    w_key,
    w_value,
    w_out,
    w_cross_query,
    w_cross_kv,
    w_cross_out,
    encoded,
    owners,
    slots,
):
    tok_rows = tokens.shape[1]
    head_count = w_query.shape[1] // HEAD
    whole_rows = lax.all_gather(tokens[0], "mp", axis=1, tiled=True)
    whole_float = whole_rows.astype(jnp.float32)
    normed = (
        whole_float
        * lax.rsqrt(jnp.mean(whole_float * whole_float, axis=-1, keepdims=True) + norm_eps)
        * norm_gain
    ).astype(jnp.bfloat16)
    queries = (
        jnp.dot(normed, w_query, preferred_element_type=jnp.float32)
        .astype(jnp.bfloat16)
        .reshape(tok_rows, head_count, HEAD)
    )
    key_rows = (
        jnp.dot(normed, w_key, preferred_element_type=jnp.float32)
        .astype(jnp.bfloat16)
        .reshape(tok_rows, head_count, HEAD)
    )
    value_rows = (
        jnp.dot(normed, w_value, preferred_element_type=jnp.float32)
        .astype(jnp.bfloat16)
        .reshape(tok_rows, head_count, HEAD)
    )
    attended = self_attention(queries, key_rows, value_rows, lax.axis_index("ctx") * tok_rows)
    branch_terms = jnp.dot(attended, w_out, preferred_element_type=jnp.float32)
    share = lax.psum_scatter(
        branch_terms.astype(jnp.bfloat16), "mp", scatter_dimension=1, tiled=True
    ).astype(jnp.float32)
    residual_part = (tokens[0].astype(jnp.float32) + share).astype(jnp.bfloat16)
    mixed_rows = lax.all_gather(residual_part, "mp", axis=1, tiled=True)
    mixed_float = mixed_rows.astype(jnp.float32)
    cross_in = (
        mixed_float
        * lax.rsqrt(jnp.mean(mixed_float * mixed_float, axis=-1, keepdims=True) + norm_eps)
        * cross_gain
    ).astype(jnp.bfloat16)
    cross_queries = (
        jnp.dot(cross_in, w_cross_query, preferred_element_type=jnp.float32)
        .astype(jnp.bfloat16)
        .reshape(tok_rows, head_count, HEAD)
    )
    neighbour_kv = fetch_neighbours(encoded, owners, slots, w_cross_kv)
    crossed = cross_attention(cross_queries, neighbour_kv)
    cross_terms = jnp.dot(crossed, w_cross_out, preferred_element_type=jnp.float32)
    cross_part = lax.psum_scatter(
        cross_terms.astype(jnp.bfloat16), "mp", scatter_dimension=1, tiled=True
    ).astype(jnp.float32)
    return (residual_part.astype(jnp.float32) + cross_part).astype(jnp.bfloat16)[None]


def solution(mesh):
    placed = (
        P("pool", "ctx", "mp"),
        P(),
        P(),
        P(None, "mp"),
        P(None, "mp"),
        P(None, "mp"),
        P("mp", None),
        P(None, "mp"),
        P(None, None, "mp"),
        P("mp", None),
        P(("pool", "ctx"), "mp", None),
        P(),
        P(),
    )
    return jax.shard_map(
        per_device, mesh=mesh, in_specs=placed, out_specs=P("pool", "ctx", "mp"), check_vma=False
    )
```

profile of v0, /device:TPU:2, one launch (start us, length us, event | category | flops | bytes accessed | tf_op | source)
XLA Modules:
  0.0 438.7 jit_solution(675896711523024793)
XLA Ops:
  6.5 0.7 all-gather.14.cloned.1.call-update
  7.3 0.0 all-gather.10.cloned.1.call-start
  7.3 63.4 %all-gather.14.cloned.1.call-done = bf16[1,512,4096]{2,1,0:T(8,128)(2,1)} async-done(((bf16[1,512,256]{2,1,0:T(8,128)(2,1)}), bf16[1,512,4096]{2,1,0:T(8,128)(2,1)}) %all-gather.14.cloned.1.call-update) | async-done | bytes 4194320 | tf_op jit(solution)/shard_map/all_gather | solution.py:150
  70.8 3.2 fusion.15
  74.0 0.2 copy-done.2
  74.2 3.2 convolution_convert_fusion.2
  77.4 0.8 copy.33
  78.2 0.0 all-gather.8.cloned.1.call-start
  78.3 4.4 %convolution_convert_fusion.3 = bf16[512,256]{0,1:T(8,128)(2,1)S(1)} fusion(bf16[4096,256]{1,0:T(8,128)(2,1)} %param.19, bf16[1,512,4096]{2,1,0:T(8,128)(2,1)} %all-gather.14.cloned.1.call-done, f32[4096]{0:T(1024)S(1)} %copy-done.10, f32[512]{0:T(512)S(1)} %add_rsqrt_fusion.1), kind=kOutput, calls=%fused_computation.44 | convolution fusion | flops 1082261504 | bytes 6572032 | tf_op jit(solution)/shard_map/dot_general | solution.py:163
  82.7 0.8 copy.32
  83.6 0.2 reduce-scatter.3.cloned.1.call-start
  83.9 4.2 convolution_convert_fusion.4
  88.1 13.5 %all-gather.10.cloned.1.call-done = bf16[2048,2,128]{2,0,1:T(8,128)(2,1)} async-done(((bf16[512,2,128]{2,0,1:T(8,128)(2,1)}), bf16[2048,2,128]{2,0,1:T(8,128)(2,1)}) %all-gather.10.cloned.1.call-update) | async-done | bytes 1048592 | tf_op jit(solution)/shard_map/all_gather | solution.py:68
  101.6 26.3 %all-gather.8.cloned.1.call-done = bf16[2048,2,128]{2,0,1:T(8,128)(2,1)} async-done(((bf16[512,2,128]{2,0,1:T(8,128)(2,1)}), bf16[2048,2,128]{2,0,1:T(8,128)(2,1)}) %all-gather.8.cloned.1.call-update) | async-done | bytes 1048592 | tf_op jit(solution)/shard_map/all_gather | solution.py:67
  127.9 9.6 %conditional.1 = (f32[2,512]{1,0:T(2,128)S(1)}, f32[2,512,128]{1,2,0:T(8,128)S(1)}) conditional(s32[]{:T(128)} %convert_element_type.86, () %tuple.13, (s32[]{:T(128)}, s32[512]{0:T(512)S(1)}, bf16[512,256]{1,0:T(8,128)(2,1)S(1)}, bf16[2048,2,128]{2,0,1:T(8,128)(2,1)}, bf16[2048,2,128]{2,0,1:T(8,128)(2,1)}) %tuple.14), branch_computations={%region_1.0_spmd, %region_2.5_spmd} | conditional | flops 1102052864 | bytes 36468784 | solution.py:92
  127.9 0.7 iota_compare_fusion
  128.5 3.4 fusion
  132.0 2.6 fusion.3
  134.6 2.9 fusion.2
  137.5 0.1 divide_convert_fusion
  137.6 3.2 convolution_convert_fusion.1
  140.8 0.0 reduce-scatter.3.cloned.1.call-update
  140.8 0.1 copy.35
  140.9 0.1 reshape.166
  141.0 0.2 reduce_window_sum.11
  141.2 0.1 copy.37
  141.3 0.1 mul.96
  141.4 0.2 select_reduce_fusion
  141.6 0.1 copy.38
  141.7 0.1 reshape.167
  141.8 0.1 copy.36
  141.9 1.8 gather_fusion
  143.7 0.9 broadcast_select_fusion
  144.6 4.5 %all-to-all-start = ((bf16[8,4,8,896]{3,2,1,0:T(8,128)(2,1)}), bf16[8,4,8,896]{3,2,1,0:T(8,128)(2,1)S(1)}, u32[]{:S(2)}, u32[]{:S(2)}) async-start(bf16[8,4,8,896]{3,2,1,0:T(8,128)(2,1)} %broadcast_select_fusion), calls=%async_computation.1 | async-start | bytes 917504 | tf_op jit(solution)/shard_map/all_to_all | solution.py:41
  149.1 0.0 all-gather.16.cloned.1.call-start
  149.1 0.2 select_reduce_fusion.1
  149.4 7.7 %all-to-all-done = bf16[8,4,8,896]{3,2,1,0:T(8,128)(2,1)S(1)} async-done(((bf16[8,4,8,896]{3,2,1,0:T(8,128)(2,1)}), bf16[8,4,8,896]{3,2,1,0:T(8,128)(2,1)S(1)}, u32[]{:S(2)}, u32[]{:S(2)}) %all-to-all-start) | async-done | bytes 458784 | tf_op jit(solution)/shard_map/all_to_all | solution.py:41
  157.1 1.3 gather_fusion.1
  158.4 0.0 all-gather.12.cloned.1.call-start
  158.5 63.0 %reduce-scatter.3.cloned.1.call-done = bf16[512,256]{1,0:T(8,128)(2,1)} async-done(((bf16[512,4096]{1,0:T(8,128)(2,1)}), bf16[512,256]{1,0:T(8,128)(2,1)}) %reduce-scatter.3.cloned.1.call-update) | async-done | bytes 262160 | tf_op jit(solution)/shard_map/reduce_scatter | solution.py:174
  221.5 1.7 fusion.42
  223.2 0.0 reduce-scatter.5.cloned.1.call-start
  223.3 0.1 pad.4.clone
  223.3 53.4 %all-gather.16.cloned.1.call-done = bf16[16,128,896]{2,1,0:T(8,128)(2,1)} async-done(((bf16[16,8,896]{2,1,0:T(8,128)(2,1)}), bf16[16,128,896]{2,1,0:T(8,128)(2,1)}) %all-gather.16.cloned.1.call-update) | async-done | bytes 3670032 | tf_op jit(solution)/shard_map/all_gather | solution.py:50
  276.7 6.0 %convert_bitcast_fusion = bf16[2,16,128,256]{3,2,0,1:T(8,128)(2,1)} fusion(bf16[16,128,896]{2,1,0:T(8,128)(2,1)} %all-gather.16.cloned.1.call-done, bf16[2,896,256]{2,1,0:T(8,128)(2,1)} %param.23), kind=kOutput, calls=%fused_computation.37 | convolution fusion | flops 1880096768 | bytes 6684672 | tf_op jit(solution)/shard_map/nrw,cwd->cnrd/dot_general | solution.py:48
  282.8 4.5 %copy.39 = bf16[2,16,128,256]{2,1,3,0:T(8,128)(2,1)} copy(bf16[2,16,128,256]{3,2,0,1:T(8,128)(2,1)} %convert_bitcast_fusion) | data formatting | bytes 4194304 | tf_op jit(solution)/shard_map/convert_element_type | solution.py:53
  287.3 4.1 reshape.169
  291.4 4.6 %copy.40 = bf16[2,8,256,2,128]{4,2,3,1,0:T(8,128)(2,1)} copy(bf16[2,8,256,2,128]{2,1,4,3,0:T(8,128)(2,1)} %reshape.169) | data formatting | bytes 4194304 | tf_op jit(solution)/shard_map/reshape | solution.py:103
  295.9 1.0 slice.20
  296.9 3.7 collective-permute-start
  300.6 36.4 %all-gather.12.cloned.1.call-done = bf16[512,4096]{1,0:T(8,128)(2,1)} async-done(((bf16[512,256]{1,0:T(8,128)(2,1)}), bf16[512,4096]{1,0:T(8,128)(2,1)}) %all-gather.12.cloned.1.call-update) | async-done | bytes 4194320 | tf_op jit(solution)/shard_map/all_gather | solution.py:178
  337.0 3.2 fusion.12
  340.2 0.2 copy-done.3
  340.4 3.2 fusion.28
  343.6 0.2 copy.42
  343.8 0.2 maximum_maximum_fusion
  344.0 2.0 fusion.55
  346.0 0.4 fusion.37
  346.5 0.5 fusion.27
  346.9 0.3 copy.44
  347.3 0.3 copy-done.5
  347.6 3.2 convolution_convert_fusion
  350.8 79.3 %reduce-scatter.5.cloned.1.call-done = bf16[512,256]{1,0:T(8,128)(2,1)} async-done(((bf16[512,4096]{1,0:T(8,128)(2,1)}), bf16[512,256]{1,0:T(8,128)(2,1)}) %reduce-scatter.5.cloned.1.call-update) | async-done | bytes 262160 | tf_op jit(solution)/shard_map/reduce_scatter | solution.py:193
  430.1 1.7 fusion.44
  (44 shorter events, 0.3 us)
Async XLA Ops:
  6.5 131.0 %copy-start = (bf16[256,4096]{1,0:T(8,128)(2,1)S(1)}, bf16[256,4096]{1,0:T(8,128)(2,1)}, u32[]{:S(2)}) copy-start(bf16[256,4096]{1,0:T(8,128)(2,1)} %param.21) | copy-start | bytes 6291460
  6.5 67.5 %copy-start.10 = (f32[4096]{0:T(1024)S(1)}, f32[4096]{0:T(1024)}, u32[]{:S(2)}) copy-start(f32[4096]{0:T(1024)} %param.16) | copy-start | bytes 49156
  6.5 64.2 %all-gather.14.cloned.1.call-start = ((), (), s32[]{:S(2)}) async-start(), calls=%async_computation.8 | async-start | bytes 4456448 | tf_op jit(solution)/shard_map/all_gather | solution.py:150
  7.3 94.3 %all-gather.10.cloned.1.call-start = ((), (), s32[]{:S(2)}) async-start(), calls=%async_computation.4 | async-start | bytes 1310720 | tf_op jit(solution)/shard_map/all_gather | solution.py:68
  70.8 3.4 copy-start.2
  78.2 49.6 %all-gather.8.cloned.1.call-start = ((), (), s32[]{:S(2)}) async-start(), calls=%async_computation.3 | async-start | bytes 1310720 | tf_op jit(solution)/shard_map/all_gather | solution.py:67
  83.6 137.8 %reduce-scatter.3.cloned.1.call-start = ((), (), s32[]{:S(2)}) async-start(), calls=%async_computation.5 | async-start | bytes 4456448 | tf_op jit(solution)/shard_map/reduce_scatter | solution.py:174
  128.5 3.4 copy-start.9
  137.5 3.3 copy-start.7
  137.6 3.6 copy-start.8
  140.8 80.7 %copy-start.6 = (bf16[1,512,256]{2,1,0:T(8,128)(2,1)S(1)}, bf16[1,512,256]{2,1,0:T(8,128)(2,1)}, u32[]{:S(2)}) copy-start(bf16[1,512,256]{2,1,0:T(8,128)(2,1)} %param.15) | copy-start | bytes 786436
  144.6 12.5 %all-to-all-start = ((bf16[8,4,8,896]{3,2,1,0:T(8,128)(2,1)}), bf16[8,4,8,896]{3,2,1,0:T(8,128)(2,1)S(1)}, u32[]{:S(2)}, u32[]{:S(2)}) async-start(bf16[8,4,8,896]{3,2,1,0:T(8,128)(2,1)} %broadcast_select_fusion), calls=%async_computation.1 | async-start | bytes 917504 | tf_op jit(solution)/shard_map/all_to_all | solution.py:41
  149.1 127.6 %all-gather.16.cloned.1.call-start = ((), (), s32[]{:S(2)}) async-start(), calls=%async_computation.9 | async-start | bytes 3899392 | tf_op jit(solution)/shard_map/all_gather | solution.py:50
  158.4 178.5 %all-gather.12.cloned.1.call-start = ((), (), s32[]{:S(2)}) async-start(), calls=%async_computation.6 | async-start | bytes 4456448 | tf_op jit(solution)/shard_map/all_gather | solution.py:178
  223.2 206.9 %reduce-scatter.5.cloned.1.call-start = ((), (), s32[]{:S(2)}) async-start(), calls=%async_computation.7 | async-start | bytes 4456448 | tf_op jit(solution)/shard_map/reduce_scatter | solution.py:193
  291.4 48.8 %copy-start.11 = (f32[4096]{0:T(1024)S(1)}, f32[4096]{0:T(1024)}, u32[]{:S(2)}) copy-start(f32[4096]{0:T(1024)} %param.17) | copy-start | bytes 49156
  296.9 47.1 %collective-permute-start = (bf16[2,1,256,2,128]{4,2,3,1,0:T(8,128)(2,1)S(1)}, bf16[2,1,256,2,128]{4,2,3,1,0:T(8,128)(2,1)S(1)}, u32[]{:S(2)}, u32[]{:S(2)}) collective-permute-start(bf16[2,1,256,2,128]{4,2,3,1,0:T(8,128)(2,1)S(1)} %slice.20), channel_id=1, source_target_pairs={{0,16},{16,32},{32,48},{1,17},{17,33},{33,49},{2,18},{18,34},{34,5... | collective-permute-start | bytes 786440 | tf_op jit(solution)/shard_map/ppermute | solution.py:19
  337.0 3.4 copy-start.3
  343.8 2.7 copy-start.1
  346.0 1.6 copy-start.5
  347.6 82.5 %copy-start.4 = (bf16[512,256]{1,0:T(8,128)(2,1)S(1)}, bf16[512,256]{1,0:T(8,128)(2,1)}, u32[]{:S(2)}) copy-start(bf16[512,256]{1,0:T(8,128)(2,1)} %fusion.42) | copy-start | bytes 786436
Sparse Core Ops, SparseCore 0:
  9.6 61.0 all-gather.13
  78.4 23.1 all-gather.9
  103.2 24.5 all-gather.7
  140.9 80.4 reduce-scatter.2
  224.1 52.5 all-gather.15
  279.1 57.8 all-gather.11
  351.0 79.1 reduce-scatter.4
where the time goes:
time: 440 us; the launch traced here: 439 us
  waiting for transfers between devices  344 us (78%)
  matrix products  35.9 us (8%)
  local copies, waits for them, and re-layouts  20.9 us (5%)
  other arithmetic  15.7 us (4%)
  between operations  13.7 us (3%)
  starting transfers between devices  8.6 us (2%)
    reduce_scatter x1, waiting for transfers between devices, per_device(): lax.psum_scatter(cross_terms.astype(jnp.bfloat16), 'mp', scatter_dimensio...  79.3 us
    all_gather x1, waiting for transfers between devices, per_device(): whole_rows = lax.all_gather(tokens[0], 'mp', axis=1, tiled=True)  63.4 us
    reduce_scatter x1, waiting for transfers between devices, per_device(): lax.psum_scatter(branch_terms.astype(jnp.bfloat16), 'mp', scatter_dimensi...  63 us
    all_gather x1, waiting for transfers between devices, fetch_neighbours(): lax.all_gather(arrived, 'mp', axis=1, tiled=True)  53.4 us
    all_gather x1, waiting for transfers between devices, per_device(): mixed_rows = lax.all_gather(residual_part, 'mp', axis=1, tiled=True)  36.4 us
    all_gather x1, waiting for transfers between devices, self_attention(): lax.all_gather(key_rows, 'ctx', axis=0, tiled=True)  26.3 us
    all_gather x1, waiting for transfers between devices, self_attention(): lax.all_gather(value_rows, 'ctx', axis=0, tiled=True)  13.5 us
  transfers between devices with their start and end apart: 9, of which 8 were waited for; matrix products, arithmetic and copies ran while one was open for 10% of the time, Pallas kernels for 0%

commit v1 on v0

v1 whole, which is shorter than its diff:
```python
import jax
import jax.numpy as jnp
from jax import lax
from jax.experimental import pallas as pl
from jax.experimental.pallas import tpu as pltpu
from jax.sharding import PartitionSpec as P

HEAD = 128
SPAN = 64
NB_TOK = 128
NB_PER = 2
LOG2E = 1.4426950408889634
norm_eps = 1e-05
mask_floor = -1e30

CHIPS = ((0, 0), (0, -1), (0, 1), (1, 0), (0, 2), (1, -1), (1, 1), (1, 2))


def route(dy, dx, dc):
    return [
        (y * 8 + x * 2 + c, ((y + dy) % 2) * 8 + ((x + dx) % 4) * 2 + (c + dc) % 2)
        for y in range(2)
        for x in range(4)
        for c in range(2)
    ]


TO_RIGHT, TO_LEFT, TO_Y, TO_CORE = route(0, 1, 0), route(0, -1, 0), route(1, 0, 0), route(0, 0, 1)


def mp_send(block, pairs):
    return lax.ppermute(block, "mp", pairs)


def relative_ids():
    me = lax.axis_index("mp")
    y, x, c = me // 8, (me // 2) % 4, me % 2
    return jnp.stack(
        [
            ((y + dy) % 2) * 8 + ((x + dx) % 4) * 2 + (c + dc) % 2
            for dc in range(2)
            for dy, dx in CHIPS
        ]
    ).astype(jnp.int32)


def gather_mp(shard):
    half = shard.shape[0] // 2
    from_left, from_right, from_y = (
        mp_send(shard, TO_RIGHT),
        mp_send(shard, TO_LEFT),
        mp_send(shard, TO_Y),
    )
    left2 = mp_send(jnp.concatenate([from_left[:half], from_y[:half]]), TO_RIGHT)
    right2 = mp_send(jnp.concatenate([from_right[half:], from_y[half:]]), TO_LEFT)
    across = mp_send(jnp.concatenate([from_left[half:], from_right[:half]]), TO_Y)
    far_top = mp_send(left2[half:], TO_RIGHT)
    far_low = mp_send(right2[half:], TO_LEFT)
    mine = jnp.stack(
        [
            shard,
            from_left,
            from_right,
            from_y,
            jnp.concatenate([left2[:half], right2[:half]]),
            jnp.concatenate([left2[half:], across[:half]]),
            jnp.concatenate([across[half:], right2[half:]]),
            jnp.concatenate([far_top, far_low]),
        ]
    )
    return mine, mp_send(mine, TO_CORE)


def scatter_mp(mine, partner):
    partner = mp_send(partner, TO_CORE)

    def part(i, rows):
        return mine[i, rows].astype(jnp.float32) + partner[i, rows].astype(jnp.float32)

    half = mine.shape[1] // 2
    top, low = slice(0, half), slice(half, 2 * half)
    b16 = jnp.bfloat16
    own, left, right, y, x2, y_left, y_right, y2 = range(8)
    from_left = mp_send(jnp.concatenate([part(x2, top), part(y2, top)]).astype(b16), TO_RIGHT)
    from_right = mp_send(jnp.concatenate([part(x2, low), part(y2, low)]).astype(b16), TO_LEFT)
    from_y = mp_send(jnp.concatenate([part(y_right, low), part(y_left, top)]).astype(b16), TO_Y)
    via_left = mp_send((part(y_right, top) + from_left[half:].astype(jnp.float32)).astype(b16), TO_RIGHT)
    via_right = mp_send((part(y_left, low) + from_right[half:].astype(jnp.float32)).astype(b16), TO_LEFT)
    to_right = jnp.concatenate(
        [
            part(right, top) + from_left[:half].astype(jnp.float32),
            part(right, low) + from_y[:half].astype(jnp.float32),
        ]
    ).astype(b16)
    to_left = jnp.concatenate(
        [
            part(left, top) + from_y[half:].astype(jnp.float32),
            part(left, low) + from_right[:half].astype(jnp.float32),
        ]
    ).astype(b16)
    to_y = (
        part(y, slice(0, 2 * half))
        + jnp.concatenate([via_left, via_right]).astype(jnp.float32)
    ).astype(b16)
    a, b, c = mp_send(to_right, TO_RIGHT), mp_send(to_left, TO_LEFT), mp_send(to_y, TO_Y)
    return (
        part(own, slice(0, 2 * half))
        + a.astype(jnp.float32)
        + b.astype(jnp.float32)
        + c.astype(jnp.float32)
    )


VMEM_ROOM = 48 * 1024 * 1024


def call(kernel, **kw):
    return pl.pallas_call(
        kernel,
        compiler_params=pltpu.CompilerParams(vmem_limit_bytes=VMEM_ROOM),
        **kw,
    )


def normed_projection(ids, mine, partner, gain, weights):
    count = len(weights)
    shards, rows, feats = mine.shape
    steps = 2 * shards
    width = weights[0].shape[1]

    def kernel(ids_ref, mine_ref, partner_ref, gain_ref, *refs):
        w_refs, out_refs = refs[:count], refs[count : 2 * count]
        inv_ref, acc_ref = refs[2 * count :]
        k = pl.program_id(0)

        @pl.when(k == 0)
        def _():
            total = jnp.zeros((rows, feats), jnp.float32)
            for i in range(shards):
                a = mine_ref[i].astype(jnp.float32)
                b = partner_ref[i].astype(jnp.float32)
                total = total + a * a + b * b
            mean = jnp.sum(total, axis=1, keepdims=True) * (1.0 / (steps * feats))
            inv_ref[...] = jnp.broadcast_to(lax.rsqrt(mean + norm_eps), inv_ref.shape)

        def step(x):
            normed = (
                x.astype(jnp.float32) * inv_ref[:, :1] * gain_ref[ids_ref[k]]
            ).astype(jnp.bfloat16)
            for i in range(count):
                part = jnp.dot(normed, w_refs[i][...], preferred_element_type=jnp.float32)
                acc_ref[i] = jnp.where(k == 0, part, acc_ref[i] + part)

        @pl.when(k < shards)
        def _():
            step(mine_ref[jnp.minimum(k, shards - 1)])

        @pl.when(k >= shards)
        def _():
            step(partner_ref[jnp.maximum(k - shards, 0)])

        @pl.when(k == steps - 1)
        def _():
            for i in range(count):
                out_refs[i][...] = acc_ref[i].astype(jnp.bfloat16)

    whole = pl.BlockSpec((shards, rows, feats), lambda k, ids: (0, 0, 0))
    return call(
        kernel,
        grid_spec=pltpu.PrefetchScalarGridSpec(
            num_scalar_prefetch=1,
            grid=(steps,),
            in_specs=[
                whole,
                whole,
                pl.BlockSpec((steps, 1, feats), lambda k, ids: (0, 0, 0)),
            ]
            + [pl.BlockSpec((feats, width), lambda k, ids: (ids[k], 0))] * count,
            out_specs=[pl.BlockSpec((rows, width), lambda k, ids: (0, 0))] * count,
            scratch_shapes=[
                pltpu.VMEM((rows, 128), jnp.float32),
                pltpu.VMEM((count, rows, width), jnp.float32),
            ],
        ),
        out_shape=[jax.ShapeDtypeStruct((rows, width), jnp.bfloat16)] * count,
    )(ids, mine, partner, gain.reshape(steps, 1, feats), *weights)


def self_attention(queries, kv_own, kv_back1, kv_back2, kv_back3):
    rows, width = queries.shape
    heads = width // HEAD
    chunk = rows // 2
    scale = HEAD ** (-0.5) * LOG2E

    def kernel(ctx_ref, q_ref, own_ref, b1_ref, b2_ref, b3_ref, out_ref):
        c = pl.program_id(0)
        kv = (own_ref, b1_ref, b2_ref, b3_ref)
        for back in range(4):

            @pl.when(ctx_ref[0] == back)
            def _(back=back):
                pos = c * chunk + lax.broadcasted_iota(jnp.int32, (chunk, rows), 0)
                allowed = lax.broadcasted_iota(jnp.int32, (chunk, rows), 1) <= pos
                for h in range(heads):
                    cols = slice(h * HEAD, (h + 1) * HEAD)
                    q = q_ref[:, cols]
                    scores = []
                    for d in range(back + 1):
                        s = lax.dot_general(
                            q,
                            kv[d][0, :, cols],
                            (((1,), (1,)), ((), ())),
                            preferred_element_type=jnp.float32,
                        ) * scale
                        scores.append(jnp.where(allowed, s, mask_floor) if d == 0 else s)
                    peak = jnp.max(scores[0], axis=1, keepdims=True)
                    for s in scores[1:]:
                        peak = jnp.maximum(peak, jnp.max(s, axis=1, keepdims=True))
                    total, mixed = 0.0, 0.0
                    for d in range(back + 1):
                        weights = jnp.exp2(scores[d] - peak)
                        total = total + jnp.sum(weights, axis=1, keepdims=True)
                        mixed = mixed + jnp.dot(
                            weights.astype(jnp.bfloat16),
                            kv[d][1, :, cols],
                            preferred_element_type=jnp.float32,
                        )
                    out_ref[:, cols] = (mixed / total).astype(jnp.bfloat16)

    whole = pl.BlockSpec((2, rows, width), lambda c, ctx: (0, 0, 0))
    block = pl.BlockSpec((chunk, width), lambda c, ctx: (c, 0))
    return call(
        kernel,
        grid_spec=pltpu.PrefetchScalarGridSpec(
            num_scalar_prefetch=1, grid=(2,), in_specs=[block] + [whole] * 4, out_specs=block
        ),
        out_shape=jax.ShapeDtypeStruct((rows, width), jnp.bfloat16),
    )(lax.axis_index("ctx").reshape(1).astype(jnp.int32), queries, kv_own, kv_back1, kv_back2, kv_back3)


def output_blocks(ids, inputs, weight):
    rows, depth = inputs.shape
    blocks = ids.shape[0]
    width = 256

    def kernel(ids_ref, in_ref, w_ref, out_ref):
        out_ref[0] = jnp.dot(in_ref[...], w_ref[...], preferred_element_type=jnp.float32).astype(
            jnp.bfloat16
        )

    return call(
        kernel,
        grid_spec=pltpu.PrefetchScalarGridSpec(
            num_scalar_prefetch=1,
            grid=(blocks,),
            in_specs=[
                pl.BlockSpec((rows, depth), lambda k, ids: (0, 0)),
                pl.BlockSpec((depth, width), lambda k, ids: (0, ids[k])),
            ],
            out_specs=pl.BlockSpec((1, rows, width), lambda k, ids: (k, 0, 0)),
        ),
        out_shape=jax.ShapeDtypeStruct((blocks, rows, width), jnp.bfloat16),
    )(ids, inputs, weight)


def neighbour_projection(mine, partner, w_cross_kv):
    shards, rows, depth = mine.shape
    width = w_cross_kv.shape[2]
    spans = rows // 16

    def kernel(mine_ref, partner_ref, w_ref, out_ref):
        for core, x_ref in enumerate((mine_ref, partner_ref)):
            for part in range(2):
                res = jnp.dot(x_ref[0], w_ref[part], preferred_element_type=jnp.float32)
                out_ref[part, :, 0, core] = res.astype(jnp.bfloat16).reshape(spans, 16, width)

    block = pl.BlockSpec((1, rows, depth), lambda k: (k, 0, 0))
    return call(
        kernel,
        grid=(shards,),
        in_specs=[block, block, pl.BlockSpec((2, depth, width), lambda k: (0, 0, 0))],
        out_specs=pl.BlockSpec((2, spans, 1, 2, 16, width), lambda k: (0, 0, k, 0, 0, 0)),
        out_shape=jax.ShapeDtypeStruct((2, spans, shards, 2, 16, width), jnp.bfloat16),
    )(mine, partner, w_cross_kv).reshape(2, spans, shards * 32, width)


def cross_attention(queries, neighbour_kv, earlier):
    rows, width = queries.shape
    heads = width // HEAD
    spans = neighbour_kv.shape[1]
    scale = HEAD ** (-0.5) * LOG2E

    def attend(q, k, v):
        s = (
            lax.dot_general(q, k, (((1,), (1,)), ((), ())), preferred_element_type=jnp.float32)
            * scale
        )
        weights = jnp.exp2(s - jnp.max(s, axis=1, keepdims=True))
        total = jnp.sum(weights, axis=1, keepdims=True)
        return jnp.dot(weights.astype(jnp.bfloat16), v, preferred_element_type=jnp.float32) / total

    def kernel(q_ref, kv_ref, earlier_ref, out_ref, shifted_ref):
        row = lax.broadcasted_iota(jnp.int32, (rows, HEAD), 0)
        for h in range(heads):
            cols = slice(h * HEAD, (h + 1) * HEAD)
            shifted = pltpu.roll(q_ref[:, cols].astype(jnp.float32), 1, 0).astype(jnp.bfloat16)
            for g in range(spans):
                k, v = (
                    (earlier_ref[0, :, cols], earlier_ref[1, :, cols])
                    if g == 0
                    else (kv_ref[0, g - 1, :, cols], kv_ref[1, g - 1, :, cols])
                )
                shifted_ref[g * SPAN : (g + 1) * SPAN] = attend(
                    shifted[g * SPAN : (g + 1) * SPAN], k, v
                )
            last = attend(
                q_ref[rows - 16 :, cols], kv_ref[0, spans - 1, :, cols], kv_ref[1, spans - 1, :, cols]
            )
            back = pltpu.roll(shifted_ref[...], rows - 1, 0)
            final = jnp.where(row == rows - 1, last[15:16], back)
            out_ref[:, cols] = final.astype(jnp.bfloat16)

    return call(
        kernel,
        out_shape=jax.ShapeDtypeStruct((rows, width), jnp.bfloat16),
        scratch_shapes=[pltpu.VMEM((rows, HEAD), jnp.float32)],
    )(queries, neighbour_kv, earlier)


def fetch_neighbours(encoded, owners, slots):
    group_count = lax.axis_size(("pool", "ctx"))
    my_group = lax.axis_index(("pool", "ctx"))
    per_group = owners.size // group_count
    capacity = max(2, 2 * per_group // group_count)
    owner_table = owners.reshape(group_count, per_group)
    slot_table = slots.reshape(group_count, per_group)
    matched = (owner_table == my_group).astype(jnp.int32)
    earlier = jnp.arange(per_group)[None, :] < jnp.arange(per_group)[:, None]
    order_rank = jnp.sum(matched[:, None, :] * earlier.astype(jnp.int32)[None], axis=2)
    slot_index = jnp.arange(capacity, dtype=jnp.int32)
    picked = matched[:, None, :] * (order_rank[:, None, :] == slot_index[None, :, None]).astype(
        jnp.int32
    )
    source_rows = jnp.sum(picked * slot_table[:, None, :], axis=2).reshape(-1)
    outgoing = encoded[source_rows]
    outgoing = outgoing.reshape((group_count, capacity) + encoded.shape[1:])
    incoming = lax.all_to_all(outgoing, ("pool", "ctx"), split_axis=0, concat_axis=0, tiled=True)
    wanted = lax.dynamic_index_in_dim(owner_table, my_group, 0, keepdims=False)
    same_owner = (wanted[:, None] == wanted[None, :]).astype(jnp.int32)
    arrival = wanted * capacity + jnp.sum(same_owner * earlier.astype(jnp.int32), axis=1)
    return incoming.reshape((group_count * capacity,) + encoded.shape[1:])[arrival]


def ctx_send(block, pairs):
    return lax.ppermute(block, "ctx", pairs)


def relay_kv(kv):
    half = kv.shape[1] // 2
    back1 = ctx_send(kv, [(0, 1), (1, 2), (2, 3)])
    other = ctx_send(kv, [(0, 3), (1, 0)])
    top = ctx_send(back1[:, :half], [(1, 2), (2, 3)])
    low = ctx_send(other[:, half:], [(3, 2), (0, 3)])
    return back1, jnp.concatenate([top, low], axis=1), other


def per_device(
    tokens,
    norm_gain,
    cross_gain,
    w_query,
    w_key,
    w_value,
    w_out,
    w_cross_query,
    w_cross_kv,
    w_cross_out,
    encoded,
    owners,
    slots,
):
    ids = relative_ids()
    half = ids.shape[0] // 2
    mine, partner = gather_mp(tokens[0])
    fetched = fetch_neighbours(encoded, owners, slots)
    keys, values = normed_projection(ids, mine, partner, norm_gain, (w_key, w_value))
    kv = jnp.stack([keys, values])
    back1, back2, back3 = relay_kv(kv)
    (queries,) = normed_projection(ids, mine, partner, norm_gain, (w_query,))
    nb_mine, nb_partner = gather_mp(fetched.reshape(-1, fetched.shape[-1]))
    neighbour_kv = neighbour_projection(nb_mine, nb_partner, w_cross_kv)
    earlier = ctx_send(neighbour_kv[:, -1], [(0, 1), (1, 2), (2, 3)])
    attended = self_attention(queries, kv, back1, back2, back3)
    for_partner = output_blocks(ids[half:], attended, w_out)
    for_mine = output_blocks(ids[:half], attended, w_out)
    share = scatter_mp(for_mine, for_partner)
    residual = (tokens[0].astype(jnp.float32) + share).astype(jnp.bfloat16)
    mine, partner = gather_mp(residual)
    (cross_queries,) = normed_projection(ids, mine, partner, cross_gain, (w_cross_query,))
    crossed = cross_attention(cross_queries, neighbour_kv, earlier)
    for_partner = output_blocks(ids[half:], crossed, w_cross_out)
    for_mine = output_blocks(ids[:half], crossed, w_cross_out)
    share = scatter_mp(for_mine, for_partner)
    return (residual.astype(jnp.float32) + share).astype(jnp.bfloat16)[None]


def solution(mesh):
    placed = (
        P("pool", "ctx", "mp"),
        P(),
        P(),
        P(None, "mp"),
        P(None, "mp"),
        P(None, "mp"),
        P("mp", None),
        P(None, "mp"),
        P(None, None, "mp"),
        P("mp", None),
        P(("pool", "ctx"), "mp", None),
        P(),
        P(),
    )
    return jax.shard_map(
        per_device, mesh=mesh, in_specs=placed, out_specs=P("pool", "ctx", "mp"), check_vma=False
    )
```

time: 440 us -> 249 us (0.57)
  waiting for transfers between devices: 344 us -> 71 us
  starting transfers between devices: 8.6 us -> 84.4 us
  Pallas kernels: 0 us -> 62.4 us
  matrix products: 35.9 us -> 0 us
  between operations: 13.7 us -> 1.09 us
  local copies, waits for them, and re-layouts: 20.9 us -> 15.5 us
    all_gather x5 -> x0, waiting for transfers between devices: 193 us -> none  [the longest x1 63.4 us: per_device(): whole_rows = lax.all_gather(tokens[0], 'mp', axis=1, tiled=True)]
    reduce_scatter x2 -> x0, waiting for transfers between devices: 142 us -> none  [the longest x1 79.3 us: per_device(): lax.psum_scatter(cross_terms.astype(jnp.bfloat16), 'mp', scatter_dimensio...]
    ppermute x1 -> x50, starting transfers between devices: 3.69 us -> 80.2 us  [the longest x45 63.8 us: mp_send(): return lax.ppermute(block, 'mp', pairs)]
    ppermute x1 -> x50, waiting for transfers between devices: 0.01 us -> 71 us  [the longest x45 69 us: mp_send(): return lax.ppermute(block, 'mp', pairs)]
    pallas_call x0 -> x10, Pallas kernels: none -> 62.4 us  [the longest x3 37.4 us: normed_projection(): call(kernel, grid_spec=pltpu.PrefetchScalarGridSpec(num_scalar_prefetch=1...]
    dot_general x10 -> x0, matrix products: 33.3 us -> none  [the longest x1 6.03 us: fetch_neighbours(): jnp.einsum('nrw,cwd->cnrd', lax.all_gather(arrived, 'mp', axis=1, tiled=T...]
    reshape x5 -> x0, local copies, waits for them, and re-layouts: 10.5 us -> none  [the longest x2 8.68 us: cross_attention(): neighbour_kv.reshape(2, span_count, NB_PER * NB_TOK, head_count, head_dim)]
    reduce_sum x6 -> x3, other arithmetic: 10.2 us -> 1.13 us  [the longest x1 0.74 us: fetch_neighbours(): source_rows = jnp.sum(picked * slot_table[:, None, :], axis=2).reshape(-1)]
  transfers between devices with their start and end apart: 9 -> 51, of which waited for: 8 -> 29; matrix products, arithmetic and copies ran while one was open for 10% -> 10% of each run, Pallas kernels for 0% -> 17%
where the time goes in v1:
time: 249 us; the launch traced here: 246 us
  starting transfers between devices  84.4 us (34%)
  waiting for transfers between devices  71 us (29%)
  Pallas kernels  62.4 us (25%)
  local copies, waits for them, and re-layouts  15.5 us (6%)
  other arithmetic  11.6 us (5%)
    ppermute x45, waiting for transfers between devices, mp_send(): return lax.ppermute(block, 'mp', pairs)  69 us
    ppermute x45, starting transfers between devices, mp_send(): return lax.ppermute(block, 'mp', pairs)  63.8 us
    pallas_call x3, Pallas kernels, normed_projection(): call(kernel, grid_spec=pltpu.PrefetchScalarGridSpec(num_scalar_prefetch=1...  37.4 us
    ppermute x5, starting transfers between devices, ctx_send(): return lax.ppermute(block, 'ctx', pairs)  16.4 us
    pallas_call x4, Pallas kernels, output_blocks(): call(kernel, grid_spec=pltpu.PrefetchScalarGridSpec(num_scalar_prefetch=1...  12.6 us
    pallas_call x1, Pallas kernels, neighbour_projection(): call(kernel, grid=(shards,), in_specs=[block, block, pl.BlockSpec((2, dep...  5.15 us
  transfers between devices with their start and end apart: 51, of which 29 were waited for; matrix products, arithmetic and copies ran while one was open for 10% of the time, Pallas kernels for 17%

profile of v1, /device:TPU:2, one launch (start us, length us, event | category | flops | bytes accessed | tf_op | source)
XLA Modules:
  0.0 245.8 jit_solution(12725335604445752266)
XLA Ops:
  0.0 3.2 %collective-permute-start.2 = (bf16[512,256]{1,0:T(8,128)(2,1)}, bf16[512,256]{1,0:T(8,128)(2,1)S(1)}, u32[]{:S(2)}, u32[]{:S(2)}) collective-permute-start(bf16[512,256]{1,0:T(8,128)(2,1)} %bitcast.226), channel_id=1, source_target_pairs={{0,8},{1,9},{2,10},{3,11},{4,12},{5,13},{6,14},{7,15},{8,0},{9,1},... | collective-permute-start | bytes 786440 | tf_op jit(solution)/shard_map/ppermute | solution.py:32
  3.2 1.5 collective-permute-start
  6.2 3.5 %collective-permute-done.2 = bf16[512,256]{1,0:T(8,128)(2,1)S(1)} collective-permute-done((bf16[512,256]{1,0:T(8,128)(2,1)}, bf16[512,256]{1,0:T(8,128)(2,1)S(1)}, u32[]{:S(2)}, u32[]{:S(2)}) %collective-permute-start.2) | collective-permute-done | bytes 262176 | tf_op jit(solution)/shard_map/ppermute | solution.py:32
  9.8 2.6 %collective-permute-done.1 = bf16[512,256]{1,0:T(8,128)(2,1)S(1)} collective-permute-done((bf16[512,256]{1,0:T(8,128)(2,1)}, bf16[512,256]{1,0:T(8,128)(2,1)S(1)}, u32[]{:S(2)}, u32[]{:S(2)}) %collective-permute-start.1) | collective-permute-done | bytes 262176 | tf_op jit(solution)/shard_map/ppermute | solution.py:32
  13.1 1.6 collective-permute-start.3
  15.5 3.6 %collective-permute-done.4 = bf16[512,256]{1,0:T(8,128)(2,1)S(1)} collective-permute-done((bf16[512,256]{1,0:T(8,128)(2,1)S(1)}, bf16[512,256]{1,0:T(8,128)(2,1)S(1)}, u32[]{:S(2)}, u32[]{:S(2)}) %collective-permute-start.4) | collective-permute-done | bytes 262176 | tf_op jit(solution)/shard_map/ppermute | solution.py:32
  22.7 1.4 collective-permute-done.7
  24.1 2.8 %collective-permute-done.6 = bf16[256,256]{1,0:T(8,128)(2,1)S(1)} collective-permute-done((bf16[256,256]{1,0:T(8,128)(2,1)S(1)}, bf16[256,256]{1,0:T(8,128)(2,1)S(1)}, u32[]{:S(2)}, u32[]{:S(2)}) %collective-permute-start.6) | collective-permute-done | bytes 131104 | tf_op jit(solution)/shard_map/ppermute | solution.py:32
  28.5 2.8 %collective-permute-done.8.partner_ref = bf16[8,512,256]{2,1,0:T(8,128)(2,1)} collective-permute-done((bf16[8,512,256]{2,1,0:T(8,128)(2,1)S(1)}, bf16[8,512,256]{2,1,0:T(8,128)(2,1)}, u32[]{:S(2)}, u32[]{:S(2)}) %collective-permute-start.8) | collective-permute-done | bytes 2097184 | tf_op jit(solution)/shard_map/ppermute | solution.py:32
  31.3 13.6 %shard_map.128 = (bf16[512,256]{1,0:T(8,128)(2,1)S(1)}, bf16[512,256]{1,0:T(8,128)(2,1)S(1)}) custom-call(s32[16]{0:T(128)S(1)} %stack.156.ids_ref, bf16[8,512,256]{2,1,0:T(8,128)(2,1)S(1)} %fusion.14.mine_ref, bf16[8,512,256]{2,1,0:T(8,128)(2,1)} %collective-permute-done.8.partner_ref, f32[16,1,256]{2,1,0:T(1,128)S(1)} %bitcast.221, ...), custom_call_target="tpu_custom_call" | custom-call | tf_op jit(solution)/shard_map/pallas_call | solution.py:168
  45.0 4.6 %collective-permute-start.9 = (bf16[2,512,256]{2,1,0:T(8,128)(2,1)S(1)}, bf16[2,512,256]{2,1,0:T(8,128)(2,1)}, u32[]{:S(2)}, u32[]{:S(2)}) collective-permute-start(bf16[2,512,256]{2,1,0:T(8,128)(2,1)S(1)} %pad_maximum_fusion.own_ref), channel_id=1, source_target_pairs={{0,16},{16,32},{32,48},{1,17},{17,33},{33,49},{2,18},{18,34},{34,5... | collective-permute-start | bytes 1572872 | tf_op jit(solution)/shard_map/ppermute | solution.py:355
  49.7 2.6 %collective-permute-start.11 = (bf16[2,512,256]{2,1,0:T(8,128)(2,1)S(1)}, bf16[2,512,256]{2,1,0:T(8,128)(2,1)}, u32[]{:S(2)}, u32[]{:S(2)}) collective-permute-start(bf16[2,512,256]{2,1,0:T(8,128)(2,1)S(1)} %pad_maximum_fusion.own_ref), channel_id=1, source_target_pairs={{0,48},{16,0},{1,49},{17,1},{2,50},{18,2},{3,51},{19,3},{4,52},{20... | collective-permute-start | bytes 1572872 | tf_op jit(solution)/shard_map/ppermute | solution.py:355
  53.1 1.3 copy.24
  54.4 1.3 reshape.207
  57.0 1.5 gather_fusion
  58.5 4.1 %all-to-all-start = ((bf16[8,4,8,896]{3,2,1,0:T(8,128)(2,1)}), bf16[8,4,8,896]{3,2,1,0:T(8,128)(2,1)}, u32[]{:S(2)}, u32[]{:S(2)}) async-start(bf16[8,4,8,896]{3,2,1,0:T(8,128)(2,1)} %bitcast.225), calls=%async_computation | async-start | bytes 917504 | tf_op jit(solution)/shard_map/all_to_all | solution.py:347
  63.3 2.0 collective-permute-done.11.b3_ref
  66.3 6.5 %collective-permute-start.12 = (bf16[2,256,256]{2,1,0:T(8,128)(2,1)S(1)}, bf16[2,256,256]{2,1,0:T(8,128)(2,1)}, u32[]{:S(2)}, u32[]{:S(2)}) collective-permute-start(bf16[2,256,256]{2,1,0:T(8,128)(2,1)S(1)} %slice.457), channel_id=1, source_target_pairs={{48,32},{0,48},{49,33},{1,49},{50,34},{2,50},{51,35},{3,51},{52,36... | collective-permute-start | bytes 786440 | tf_op jit(solution)/shard_map/ppermute | solution.py:355
  72.8 1.7 slice.456
  74.4 1.4 collective-permute-start.10
  77.5 12.3 %shard_map.127.q_ref = bf16[512,256]{1,0:T(8,128)(2,1)S(1)} custom-call(s32[16]{0:T(128)S(1)} %copy-done.11, bf16[8,512,256]{2,1,0:T(8,128)(2,1)S(1)} %fusion.14.mine_ref, bf16[8,512,256]{2,1,0:T(8,128)(2,1)} %collective-permute-done.8.partner_ref, f32[16,1,256]{2,1,0:T(1,128)S(1)} %bitcast.222, bf16[4096,256]{1,0:T(8,128)(2,1)} %refs_0_.3), custom_call_target="tpu_custom_call" | custom-call | tf_op jit(solution)/shard_map/pallas_call | solution.py:168
  92.1 2.8 %shard_map.129.in_ref = bf16[512,256]{1,0:T(8,128)(2,1)S(1)} custom-call(s32[1]{0:T(128)} %bitcast.9.ctx_ref, bf16[512,256]{1,0:T(8,128)(2,1)S(1)} %shard_map.127.q_ref, bf16[2,512,256]{2,1,0:T(8,128)(2,1)S(1)} %copy-done.6, bf16[2,512,256]{2,1,0:T(8,128)(2,1)} %collective-permute-done.9.b1_ref, bf16[2,512,256]{2,1,0:T(8,128)(2,1)S(1)} %pad_maximum_fusion.1.b2_ref, ...), custom_call_target="tpu_custom_call" | custom-call | tf_op jit(solution)/shard_map/pallas_call | solution.py:232
  94.9 4.6 %shard_map.131 = bf16[8,512,256]{2,1,0:T(8,128)(2,1)} custom-call(s32[8]{0:T(128)S(1)} %stack.168.ids_ref, bf16[512,256]{1,0:T(8,128)(2,1)S(1)} %shard_map.129.in_ref, bf16[256,4096]{1,0:T(8,128)(2,1)S(1)} %copy-done.3), custom_call_target="tpu_custom_call" | custom-call | tf_op jit(solution)/shard_map/pallas_call | solution.py:251
  99.6 1.6 gather_fusion.1
  101.3 3.3 %collective-permute-start.32 = (bf16[128,896]{1,0:T(8,128)(2,1)S(1)}, bf16[128,896]{1,0:T(8,128)(2,1)S(1)}, u32[]{:S(2)}, u32[]{:S(2)}) collective-permute-start(bf16[128,896]{1,0:T(8,128)(2,1)S(1)} %bitcast.230), channel_id=1, source_target_pairs={{0,6},{1,7},{2,0},{3,1},{4,2},{5,3},{6,4},{7,5},{8,14},{9,15},{10,... | collective-permute-start | bytes 688136 | tf_op jit(solution)/shard_map/ppermute | solution.py:32
  105.6 8.2 %collective-permute-done.33 = bf16[128,896]{1,0:T(8,128)(2,1)S(1)} collective-permute-done((bf16[128,896]{1,0:T(8,128)(2,1)S(1)}, bf16[128,896]{1,0:T(8,128)(2,1)S(1)}, u32[]{:S(2)}, u32[]{:S(2)}) %collective-permute-start.33) | collective-permute-done | bytes 229408 | tf_op jit(solution)/shard_map/ppermute | solution.py:32
  113.9 2.9 %collective-permute-start.35 = (bf16[128,896]{1,0:T(8,128)(2,1)S(1)}, bf16[128,896]{1,0:T(8,128)(2,1)S(1)}, u32[]{:S(2)}, u32[]{:S(2)}) collective-permute-start(bf16[128,896]{1,0:T(8,128)(2,1)S(1)} %pad_maximum_fusion.19), channel_id=1, source_target_pairs={{0,6},{1,7},{2,0},{3,1},{4,2},{5,3},{6,4},{7,5},{8,14},{9,15},{10,... | collective-permute-start | bytes 688136 | tf_op jit(solution)/shard_map/ppermute | solution.py:32
  118.2 2.7 %shard_map.130 = bf16[8,512,256]{2,1,0:T(8,128)(2,1)S(1)} custom-call(s32[8]{0:T(128)S(1)} %stack.147.ids_ref, bf16[512,256]{1,0:T(8,128)(2,1)S(1)} %shard_map.129.in_ref, bf16[256,4096]{1,0:T(8,128)(2,1)S(1)} %copy-done.3), custom_call_target="tpu_custom_call" | custom-call | tf_op jit(solution)/shard_map/pallas_call | solution.py:251
  120.9 1.4 fusion.37
  122.4 2.1 collective-permute-start.17
  124.6 2.6 %collective-permute-start.15 = (bf16[512,256]{1,0:T(8,128)(2,1)S(1)}, bf16[512,256]{1,0:T(8,128)(2,1)S(1)}, u32[]{:S(2)}, u32[]{:S(2)}) collective-permute-start(bf16[512,256]{1,0:T(8,128)(2,1)S(1)} %pad_maximum_fusion.6), channel_id=1, source_target_pairs={{0,8},{1,9},{2,10},{3,11},{4,12},{5,13},{6,14},{7,15},{8,0},{9,1},... | collective-permute-start | bytes 786440 | tf_op jit(solution)/shard_map/ppermute | solution.py:32
  127.2 3.3 %collective-permute-start.38 = (bf16[64,896]{1,0:T(8,128)(2,1)S(1)}, bf16[64,896]{1,0:T(8,128)(2,1)S(1)}, u32[]{:S(2)}, u32[]{:S(2)}) collective-permute-start(bf16[64,896]{1,0:T(8,128)(2,1)S(1)} %get-tuple-element.69), channel_id=1, source_target_pairs={{0,6},{1,7},{2,0},{3,1},{4,2},{5,3},{6,4},{7,5},{8,14},{9,15},{10,... | collective-permute-start | bytes 344072 | tf_op jit(solution)/shard_map/ppermute | solution.py:32
  132.5 1.5 fusion.30
  134.0 3.3 %collective-permute-start.20 = (bf16[256,256]{1,0:T(8,128)(2,1)S(1)}, bf16[256,256]{1,0:T(8,128)(2,1)S(1)}, u32[]{:S(2)}, u32[]{:S(2)}) collective-permute-start(bf16[256,256]{1,0:T(8,128)(2,1)S(1)} %get-tuple-element.33), channel_id=1, source_target_pairs={{0,6},{1,7},{2,0},{3,1},{4,2},{5,3},{6,4},{7,5},{8,14},{9,15},{10,... | collective-permute-start | bytes 393224 | tf_op jit(solution)/shard_map/ppermute | solution.py:32
  137.3 2.1 collective-permute-start.18
  143.7 3.2 %collective-permute-start.21 = (bf16[512,256]{1,0:T(8,128)(2,1)S(1)}, bf16[512,256]{1,0:T(8,128)(2,1)S(1)}, u32[]{:S(2)}, u32[]{:S(2)}) collective-permute-start(bf16[512,256]{1,0:T(8,128)(2,1)S(1)} %fusion.5), channel_id=1, source_target_pairs={{0,8},{1,9},{2,10},{3,11},{4,12},{5,13},{6,14},{7,15},{8,0},{9,1},... | collective-permute-start | bytes 786440 | tf_op jit(solution)/shard_map/ppermute | solution.py:32
  147.0 1.7 collective-permute-start.37
  148.7 4.1 %collective-permute-done.21 = bf16[512,256]{1,0:T(8,128)(2,1)S(1)} collective-permute-done((bf16[512,256]{1,0:T(8,128)(2,1)S(1)}, bf16[512,256]{1,0:T(8,128)(2,1)S(1)}, u32[]{:S(2)}, u32[]{:S(2)}) %collective-permute-start.21) | collective-permute-done | bytes 262176 | tf_op jit(solution)/shard_map/ppermute | solution.py:32
  153.9 3.9 %collective-permute-start.24 = (bf16[512,256]{1,0:T(8,128)(2,1)S(1)}, bf16[512,256]{1,0:T(8,128)(2,1)S(1)}, u32[]{:S(2)}, u32[]{:S(2)}) collective-permute-start(bf16[512,256]{1,0:T(8,128)(2,1)S(1)} %get-tuple-element.10), channel_id=1, source_target_pairs={{0,8},{1,9},{2,10},{3,11},{4,12},{5,13},{6,14},{7,15},{8,0},{9,1},... | collective-permute-start | bytes 786440 | tf_op jit(solution)/shard_map/ppermute | solution.py:32
  157.9 2.0 collective-permute-start.23
  160.2 2.0 collective-permute-done.24
  162.2 3.1 %collective-permute-done.23 = bf16[512,256]{1,0:T(8,128)(2,1)S(1)} collective-permute-done((bf16[512,256]{1,0:T(8,128)(2,1)S(1)}, bf16[512,256]{1,0:T(8,128)(2,1)S(1)}, u32[]{:S(2)}, u32[]{:S(2)}) %collective-permute-start.23) | collective-permute-done | bytes 262176 | tf_op jit(solution)/shard_map/ppermute | solution.py:32
  165.4 2.2 collective-permute-start.26
  169.1 1.8 collective-permute-start.27
  171.8 2.2 collective-permute-start.29
  174.0 2.7 %collective-permute-done.25 = bf16[512,256]{1,0:T(8,128)(2,1)S(1)} collective-permute-done((bf16[512,256]{1,0:T(8,128)(2,1)S(1)}, bf16[512,256]{1,0:T(8,128)(2,1)S(1)}, u32[]{:S(2)}, u32[]{:S(2)}) %collective-permute-start.25) | collective-permute-done | bytes 262176 | tf_op jit(solution)/shard_map/ppermute | solution.py:32
  178.6 3.6 %collective-permute-done.28 = bf16[256,256]{1,0:T(8,128)(2,1)S(1)} collective-permute-done((bf16[256,256]{1,0:T(8,128)(2,1)S(1)}, bf16[256,256]{1,0:T(8,128)(2,1)S(1)}, u32[]{:S(2)}, u32[]{:S(2)}) %collective-permute-start.28) | collective-permute-done | bytes 131104 | tf_op jit(solution)/shard_map/ppermute | solution.py:32
  182.3 5.2 %shard_map.133 = bf16[2,8,8,2,16,256]{5,4,3,2,1,0:T(8,128)(2,1)} custom-call(bf16[8,128,896]{2,1,0:T(8,128)(2,1)S(1)} %fusion.34.mine_ref, bf16[8,128,896]{2,1,0:T(8,128)(2,1)S(1)} %collective-permute-done.39.partner_ref, bf16[2,896,256]{2,1,0:T(8,128)(2,1)S(1)} %copy-done.7), custom_call_target="tpu_custom_call" | custom-call | tf_op jit(solution)/shard_map/pallas_call | solution.py:278
  187.5 1.8 copy.25
  190.7 11.5 %shard_map.132.q_ref = bf16[512,256]{1,0:T(8,128)(2,1)S(1)} custom-call(s32[16]{0:T(128)S(1)} %copy-done.12, bf16[8,512,256]{2,1,0:T(8,128)(2,1)S(1)} %fusion.18.mine_ref, bf16[8,512,256]{2,1,0:T(8,128)(2,1)S(1)} %collective-permute-done.30.partner_ref, f32[16,1,256]{2,1,0:T(1,128)S(1)} %bitcast.223, bf16[4096,256]{1,0:T(8,128)(2,1)} %refs_0_.5), custom_call_target="tpu_custom_call" | custom-call | tf_op jit(solution)/shard_map/pallas_call | solution.py:168
  202.3 4.4 %shard_map.134.in_ref = bf16[512,256]{1,0:T(8,128)(2,1)S(1)} custom-call(bf16[512,256]{1,0:T(8,128)(2,1)S(1)} %shard_map.132.q_ref, bf16[2,8,256,256]{3,2,1,0:T(8,128)(2,1)S(1)} %bitcast.218, bf16[2,256,256]{2,1,0:T(8,128)(2,1)S(1)} %collective-permute-done.40.earlier_ref), custom_call_target="tpu_custom_call" | custom-call | tf_op jit(solution)/shard_map/pallas_call | solution.py:323
  206.7 2.6 %shard_map.136 = bf16[8,512,256]{2,1,0:T(8,128)(2,1)S(1)} custom-call(s32[8]{0:T(128)S(1)} %copy-done.14, bf16[512,256]{1,0:T(8,128)(2,1)S(1)} %shard_map.134.in_ref, bf16[256,4096]{1,0:T(8,128)(2,1)S(1)} %copy-done.4), custom_call_target="tpu_custom_call" | custom-call | tf_op jit(solution)/shard_map/pallas_call | solution.py:251
  209.9 2.6 %shard_map.135 = bf16[8,512,256]{2,1,0:T(8,128)(2,1)S(1)} custom-call(s32[8]{0:T(128)S(1)} %copy-done.16, bf16[512,256]{1,0:T(8,128)(2,1)S(1)} %shard_map.134.in_ref, bf16[256,4096]{1,0:T(8,128)(2,1)S(1)} %copy-done.4), custom_call_target="tpu_custom_call" | custom-call | tf_op jit(solution)/shard_map/pallas_call | solution.py:251
  214.1 3.3 %collective-permute-start.45 = (bf16[512,256]{1,0:T(8,128)(2,1)S(1)}, bf16[512,256]{1,0:T(8,128)(2,1)S(1)}, u32[]{:S(2)}, u32[]{:S(2)}) collective-permute-start(bf16[512,256]{1,0:T(8,128)(2,1)S(1)} %pad_maximum_fusion.16), channel_id=1, source_target_pairs={{0,6},{1,7},{2,0},{3,1},{4,2},{5,3},{6,4},{7,5},{8,14},{9,15},{10,... | collective-permute-start | bytes 786440 | tf_op jit(solution)/shard_map/ppermute | solution.py:32
  217.4 1.8 collective-permute-start.43
  219.1 4.9 %collective-permute-done.42 = bf16[512,256]{1,0:T(8,128)(2,1)S(1)} collective-permute-done((bf16[512,256]{1,0:T(8,128)(2,1)S(1)}, bf16[512,256]{1,0:T(8,128)(2,1)S(1)}, u32[]{:S(2)}, u32[]{:S(2)}) %collective-permute-start.42) | collective-permute-done | bytes 262176 | tf_op jit(solution)/shard_map/ppermute | solution.py:32
  224.1 3.2 %collective-permute-done.43 = bf16[512,256]{1,0:T(8,128)(2,1)S(1)} collective-permute-done((bf16[512,256]{1,0:T(8,128)(2,1)S(1)}, bf16[512,256]{1,0:T(8,128)(2,1)S(1)}, u32[]{:S(2)}, u32[]{:S(2)}) %collective-permute-start.43) | collective-permute-done | bytes 262176 | tf_op jit(solution)/shard_map/ppermute | solution.py:32
  227.5 3.0 %collective-permute-start.48 = (bf16[256,256]{1,0:T(8,128)(2,1)S(1)}, bf16[256,256]{1,0:T(8,128)(2,1)S(1)}, u32[]{:S(2)}, u32[]{:S(2)}) collective-permute-start(bf16[256,256]{1,0:T(8,128)(2,1)S(1)} %get-tuple-element.23), channel_id=1, source_target_pairs={{0,6},{1,7},{2,0},{3,1},{4,2},{5,3},{6,4},{7,5},{8,14},{9,15},{10,... | collective-permute-start | bytes 393224 | tf_op jit(solution)/shard_map/ppermute | solution.py:32
  230.6 2.1 collective-permute-start.46
  232.8 1.6 collective-permute-done.48
  234.4 2.5 %collective-permute-done.47 = bf16[256,256]{1,0:T(8,128)(2,1)S(1)} collective-permute-done((bf16[256,256]{1,0:T(8,128)(2,1)S(1)}, bf16[256,256]{1,0:T(8,128)(2,1)S(1)}, u32[]{:S(2)}, u32[]{:S(2)}) %collective-permute-start.47) | collective-permute-done | bytes 131104 | tf_op jit(solution)/shard_map/ppermute | solution.py:32
  237.0 1.8 collective-permute-start.49
  238.8 1.8 collective-permute-done.44
  240.5 4.4 %collective-permute-done.49 = bf16[512,256]{1,0:T(8,128)(2,1)S(1)} collective-permute-done((bf16[512,256]{1,0:T(8,128)(2,1)S(1)}, bf16[512,256]{1,0:T(8,128)(2,1)S(1)}, u32[]{:S(2)}, u32[]{:S(2)}) %collective-permute-start.49) | collective-permute-done | bytes 262176 | tf_op jit(solution)/shard_map/ppermute | solution.py:32
  (187 shorter events, 35.6 us)
Async XLA Ops:
  0.0 57.0 %copy-start = (bf16[64,8,896]{2,1,0:T(8,128)(2,1)S(1)}, bf16[64,8,896]{2,1,0:T(8,128)(2,1)}, u32[]{:S(2)}) copy-start(bf16[64,8,896]{2,1,0:T(8,128)(2,1)} %param.23) | copy-start | bytes 2752516
  0.0 9.8 %collective-permute-start.2 = (bf16[512,256]{1,0:T(8,128)(2,1)}, bf16[512,256]{1,0:T(8,128)(2,1)S(1)}, u32[]{:S(2)}, u32[]{:S(2)}) collective-permute-start(bf16[512,256]{1,0:T(8,128)(2,1)} %bitcast.226), channel_id=1, source_target_pairs={{0,8},{1,9},{2,10},{3,11},{4,12},{5,13},{6,14},{7,15},{8,0},{9,1},... | collective-permute-start | bytes 786440 | tf_op jit(solution)/shard_map/ppermute | solution.py:32
  3.2 9.8 %collective-permute-start = (bf16[512,256]{1,0:T(8,128)(2,1)}, bf16[512,256]{1,0:T(8,128)(2,1)S(1)}, u32[]{:S(2)}, u32[]{:S(2)}) collective-permute-start(bf16[512,256]{1,0:T(8,128)(2,1)} %bitcast.227), channel_id=1, source_target_pairs={{0,2},{1,3},{2,4},{3,5},{4,6},{5,7},{6,0},{7,1},{8,10},{9,11},{10,... | collective-permute-start | bytes 786440 | tf_op jit(solution)/shard_map/ppermute | solution.py:32
  4.7 7.7 %collective-permute-start.1 = (bf16[512,256]{1,0:T(8,128)(2,1)}, bf16[512,256]{1,0:T(8,128)(2,1)S(1)}, u32[]{:S(2)}, u32[]{:S(2)}) collective-permute-start(bf16[512,256]{1,0:T(8,128)(2,1)} %bitcast.228), channel_id=1, source_target_pairs={{0,6},{1,7},{2,0},{3,1},{4,2},{5,3},{6,4},{7,5},{8,14},{9,15},{10,... | collective-permute-start | bytes 786440 | tf_op jit(solution)/shard_map/ppermute | solution.py:32
  12.4 6.6 %collective-permute-start.4 = (bf16[512,256]{1,0:T(8,128)(2,1)S(1)}, bf16[512,256]{1,0:T(8,128)(2,1)S(1)}, u32[]{:S(2)}, u32[]{:S(2)}) collective-permute-start(bf16[512,256]{1,0:T(8,128)(2,1)S(1)} %pad_maximum_fusion.3), channel_id=1, source_target_pairs={{0,6},{1,7},{2,0},{3,1},{4,2},{5,3},{6,4},{7,5},{8,14},{9,15},{10,... | collective-permute-start | bytes 786440 | tf_op jit(solution)/shard_map/ppermute | solution.py:32
  13.1 7.6 %collective-permute-start.3 = (bf16[512,256]{1,0:T(8,128)(2,1)S(1)}, bf16[512,256]{1,0:T(8,128)(2,1)S(1)}, u32[]{:S(2)}, u32[]{:S(2)}) collective-permute-start(bf16[512,256]{1,0:T(8,128)(2,1)S(1)} %pad_maximum_fusion.2), channel_id=1, source_target_pairs={{0,2},{1,3},{2,4},{3,5},{4,6},{5,7},{6,0},{7,1},{8,10},{9,11},{10,... | collective-permute-start | bytes 786440 | tf_op jit(solution)/shard_map/ppermute | solution.py:32
  14.7 8.0 %collective-permute-start.5 = (bf16[512,256]{1,0:T(8,128)(2,1)S(1)}, bf16[512,256]{1,0:T(8,128)(2,1)S(1)}, u32[]{:S(2)}, u32[]{:S(2)}) collective-permute-start(bf16[512,256]{1,0:T(8,128)(2,1)S(1)} %pad_maximum_fusion.4), channel_id=1, source_target_pairs={{0,8},{1,9},{2,10},{3,11},{4,12},{5,13},{6,14},{7,15},{8,0},{9,1},... | collective-permute-start | bytes 786440 | tf_op jit(solution)/shard_map/ppermute | solution.py:32
  15.4 11.8 %copy-start.20 = (s32[2,32,2]{1,2,0:T(2,128)S(1)}, s32[2,32,2]{1,2,0:T(2,128)}, u32[]{:S(2)}) copy-start(s32[2,32,2]{1,2,0:T(2,128)} %param.25) | copy-start | bytes 1540
  15.5 12.5 %copy-start.21 = (s32[2,32,2]{1,2,0:T(2,128)S(1)}, s32[2,32,2]{1,2,0:T(2,128)}, u32[]{:S(2)}) copy-start(s32[2,32,2]{1,2,0:T(2,128)} %param.24) | copy-start | bytes 1540
  15.5 15.8 %copy-start.8 = (f32[4096]{0:T(1024)S(1)}, f32[4096]{0:T(1024)}, u32[]{:S(2)}) copy-start(f32[4096]{0:T(1024)} %param.14) | copy-start | bytes 49156
  19.1 5.0 %collective-permute-start.7 = (bf16[256,256]{1,0:T(8,128)(2,1)S(1)}, bf16[256,256]{1,0:T(8,128)(2,1)S(1)}, u32[]{:S(2)}, u32[]{:S(2)}) collective-permute-start(bf16[256,256]{1,0:T(8,128)(2,1)S(1)} %get-tuple-element.57), channel_id=1, source_target_pairs={{0,6},{1,7},{2,0},{3,1},{4,2},{5,3},{6,4},{7,5},{8,14},{9,15},{10,... | collective-permute-start | bytes 393224 | tf_op jit(solution)/shard_map/ppermute | solution.py:32
  20.7 6.2 %collective-permute-start.6 = (bf16[256,256]{1,0:T(8,128)(2,1)S(1)}, bf16[256,256]{1,0:T(8,128)(2,1)S(1)}, u32[]{:S(2)}, u32[]{:S(2)}) collective-permute-start(bf16[256,256]{1,0:T(8,128)(2,1)S(1)} %get-tuple-element.59), channel_id=1, source_target_pairs={{0,2},{1,3},{2,4},{3,5},{4,6},{5,7},{6,0},{7,1},{8,10},{9,11},{10,... | collective-permute-start | bytes 393224 | tf_op jit(solution)/shard_map/ppermute | solution.py:32
  26.9 4.4 %collective-permute-start.8 = (bf16[8,512,256]{2,1,0:T(8,128)(2,1)S(1)}, bf16[8,512,256]{2,1,0:T(8,128)(2,1)}, u32[]{:S(2)}, u32[]{:S(2)}) collective-permute-start(bf16[8,512,256]{2,1,0:T(8,128)(2,1)S(1)} %fusion.14.mine_ref), channel_id=1, source_target_pairs={{0,1},{1,0},{2,3},{3,2},{4,5},{5,4},{6,7},{7,6},{8,9},{9,8},{10,11... | collective-permute-start | bytes 6291464 | tf_op jit(solution)/shard_map/ppermute | solution.py:32
  28.1 16.8 %copy-start.18 = (s32[8,16]{1,0:T(8,128)}, s32[8,16]{1,0:T(8,128)S(1)}, u32[]{:S(2)}) copy-start(s32[8,16]{1,0:T(8,128)S(1)} %reshape.206) | copy-start | bytes 1540
  28.2 16.7 %copy-start.10 = (s32[16]{0:T(128)}, s32[16]{0:T(128)S(1)}, u32[]{:S(2)}) copy-start(s32[16]{0:T(128)S(1)} %stack.156.ids_ref) | copy-start | bytes 196
  31.3 21.0 %copy-start.19 = (s32[8,16]{1,0:T(8,128)S(1)}, s32[8,16]{1,0:T(8,128)}, u32[]{:S(2)}) copy-start(s32[8,16]{1,0:T(8,128)} %mul.106) | copy-start | bytes 1540
  45.0 44.7 %copy-start.5 = (bf16[2,512,256]{2,1,0:T(8,128)(2,1)}, bf16[2,512,256]{2,1,0:T(8,128)(2,1)S(1)}, u32[]{:S(2)}) copy-start(bf16[2,512,256]{2,1,0:T(8,128)(2,1)S(1)} %pad_maximum_fusion.own_ref) | copy-start | bytes 1572868
  45.0 27.7 %collective-permute-start.9 = (bf16[2,512,256]{2,1,0:T(8,128)(2,1)S(1)}, bf16[2,512,256]{2,1,0:T(8,128)(2,1)}, u32[]{:S(2)}, u32[]{:S(2)}) collective-permute-start(bf16[2,512,256]{2,1,0:T(8,128)(2,1)S(1)} %pad_maximum_fusion.own_ref), channel_id=1, source_target_pairs={{0,16},{16,32},{32,48},{1,17},{17,33},{33,49},{2,18},{18,34},{34,5... | collective-permute-start | bytes 1572872 | tf_op jit(solution)/shard_map/ppermute | solution.py:355
  49.7 15.7 %collective-permute-start.11 = (bf16[2,512,256]{2,1,0:T(8,128)(2,1)S(1)}, bf16[2,512,256]{2,1,0:T(8,128)(2,1)}, u32[]{:S(2)}, u32[]{:S(2)}) collective-permute-start(bf16[2,512,256]{2,1,0:T(8,128)(2,1)S(1)} %pad_maximum_fusion.own_ref), channel_id=1, source_target_pairs={{0,48},{16,0},{1,49},{17,1},{2,50},{18,2},{3,51},{19,3},{4,52},{20... | collective-permute-start | bytes 1572872 | tf_op jit(solution)/shard_map/ppermute | solution.py:355
  58.5 41.1 %all-to-all-start = ((bf16[8,4,8,896]{3,2,1,0:T(8,128)(2,1)}), bf16[8,4,8,896]{3,2,1,0:T(8,128)(2,1)}, u32[]{:S(2)}, u32[]{:S(2)}) async-start(bf16[8,4,8,896]{3,2,1,0:T(8,128)(2,1)} %bitcast.225), calls=%async_computation | async-start | bytes 917504 | tf_op jit(solution)/shard_map/all_to_all | solution.py:347
  66.3 23.5 %collective-permute-start.12 = (bf16[2,256,256]{2,1,0:T(8,128)(2,1)S(1)}, bf16[2,256,256]{2,1,0:T(8,128)(2,1)}, u32[]{:S(2)}, u32[]{:S(2)}) collective-permute-start(bf16[2,256,256]{2,1,0:T(8,128)(2,1)S(1)} %slice.457), channel_id=1, source_target_pairs={{48,32},{0,48},{49,33},{1,49},{50,34},{2,50},{51,35},{3,51},{52,36... | collective-permute-start | bytes 786440 | tf_op jit(solution)/shard_map/ppermute | solution.py:355
  74.4 15.4 %collective-permute-start.10 = (bf16[2,256,256]{2,1,0:T(8,128)(2,1)}, bf16[2,256,256]{2,1,0:T(8,128)(2,1)}, u32[]{:S(2)}, u32[]{:S(2)}) collective-permute-start(bf16[2,256,256]{2,1,0:T(8,128)(2,1)} %slice.456), channel_id=1, source_target_pairs={{16,32},{32,48},{17,33},{33,49},{18,34},{34,50},{19,35},{35,51},{2... | collective-permute-start | bytes 786440 | tf_op jit(solution)/shard_map/ppermute | solution.py:355
  76.1 18.8 %copy-start.13 = (s32[8]{0:T(128)}, s32[8]{0:T(128)S(1)}, u32[]{:S(2)}) copy-start(s32[8]{0:T(128)S(1)} %stack.168.ids_ref) | copy-start | bytes 100
  76.2 42.1 %copy-start.15 = (s32[8]{0:T(128)}, s32[8]{0:T(128)S(1)}, u32[]{:S(2)}) copy-start(s32[8]{0:T(128)S(1)} %stack.147.ids_ref) | copy-start | bytes 100
  99.6 21.3 %collective-permute-start.13 = (bf16[8,512,256]{2,1,0:T(8,128)(2,1)}, bf16[8,512,256]{2,1,0:T(8,128)(2,1)}, u32[]{:S(2)}, u32[]{:S(2)}) collective-permute-start(bf16[8,512,256]{2,1,0:T(8,128)(2,1)} %shard_map.131), channel_id=1, source_target_pairs={{0,1},{1,0},{2,3},{3,2},{4,5},{5,4},{6,7},{7,6},{8,9},{9,8},{10,11... | collective-permute-start | bytes 6291464 | tf_op jit(solution)/shard_map/ppermute | solution.py:32
  101.2 15.7 %collective-permute-start.31 = (bf16[128,896]{1,0:T(8,128)(2,1)S(1)}, bf16[128,896]{1,0:T(8,128)(2,1)S(1)}, u32[]{:S(2)}, u32[]{:S(2)}) collective-permute-start(bf16[128,896]{1,0:T(8,128)(2,1)S(1)} %bitcast.229), channel_id=1, source_target_pairs={{0,2},{1,3},{2,4},{3,5},{4,6},{5,7},{6,0},{7,1},{8,10},{9,11},{10,... | collective-permute-start | bytes 688136 | tf_op jit(solution)/shard_map/ppermute | solution.py:32
  101.3 12.6 %collective-permute-start.32 = (bf16[128,896]{1,0:T(8,128)(2,1)S(1)}, bf16[128,896]{1,0:T(8,128)(2,1)S(1)}, u32[]{:S(2)}, u32[]{:S(2)}) collective-permute-start(bf16[128,896]{1,0:T(8,128)(2,1)S(1)} %bitcast.230), channel_id=1, source_target_pairs={{0,6},{1,7},{2,0},{3,1},{4,2},{5,3},{6,4},{7,5},{8,14},{9,15},{10,... | collective-permute-start | bytes 688136 | tf_op jit(solution)/shard_map/ppermute | solution.py:32
  104.6 9.2 %collective-permute-start.33 = (bf16[128,896]{1,0:T(8,128)(2,1)S(1)}, bf16[128,896]{1,0:T(8,128)(2,1)S(1)}, u32[]{:S(2)}, u32[]{:S(2)}) collective-permute-start(bf16[128,896]{1,0:T(8,128)(2,1)S(1)} %bitcast.231), channel_id=1, source_target_pairs={{0,8},{1,9},{2,10},{3,11},{4,12},{5,13},{6,14},{7,15},{8,0},{9,1},... | collective-permute-start | bytes 688136 | tf_op jit(solution)/shard_map/ppermute | solution.py:32
  113.9 10.6 %collective-permute-start.35 = (bf16[128,896]{1,0:T(8,128)(2,1)S(1)}, bf16[128,896]{1,0:T(8,128)(2,1)S(1)}, u32[]{:S(2)}, u32[]{:S(2)}) collective-permute-start(bf16[128,896]{1,0:T(8,128)(2,1)S(1)} %pad_maximum_fusion.19), channel_id=1, source_target_pairs={{0,6},{1,7},{2,0},{3,1},{4,2},{5,3},{6,4},{7,5},{8,14},{9,15},{10,... | collective-permute-start | bytes 688136 | tf_op jit(solution)/shard_map/ppermute | solution.py:32
  116.9 10.3 %collective-permute-start.34 = (bf16[128,896]{1,0:T(8,128)(2,1)S(1)}, bf16[128,896]{1,0:T(8,128)(2,1)S(1)}, u32[]{:S(2)}, u32[]{:S(2)}) collective-permute-start(bf16[128,896]{1,0:T(8,128)(2,1)S(1)} %pad_maximum_fusion.18), channel_id=1, source_target_pairs={{0,2},{1,3},{2,4},{3,5},{4,6},{5,7},{6,0},{7,1},{8,10},{9,11},{10,... | collective-permute-start | bytes 688136 | tf_op jit(solution)/shard_map/ppermute | solution.py:32
  117.0 29.9 %collective-permute-start.36 = (bf16[128,896]{1,0:T(8,128)(2,1)S(1)}, bf16[128,896]{1,0:T(8,128)(2,1)S(1)}, u32[]{:S(2)}, u32[]{:S(2)}) collective-permute-start(bf16[128,896]{1,0:T(8,128)(2,1)S(1)} %pad_maximum_fusion.20), channel_id=1, source_target_pairs={{0,8},{1,9},{2,10},{3,11},{4,12},{5,13},{6,14},{7,15},{8,0},{9,1},... | collective-permute-start | bytes 688136 | tf_op jit(solution)/shard_map/ppermute | solution.py:32
  122.3 8.1 %collective-permute-start.14 = (bf16[512,256]{1,0:T(8,128)(2,1)S(1)}, bf16[512,256]{1,0:T(8,128)(2,1)S(1)}, u32[]{:S(2)}, u32[]{:S(2)}) collective-permute-start(bf16[512,256]{1,0:T(8,128)(2,1)S(1)} %pad_maximum_fusion.5), channel_id=1, source_target_pairs={{0,2},{1,3},{2,4},{3,5},{4,6},{5,7},{6,0},{7,1},{8,10},{9,11},{10,... | collective-permute-start | bytes 786440 | tf_op jit(solution)/shard_map/ppermute | solution.py:32
  122.4 8.9 %collective-permute-start.17 = (bf16[512,256]{1,0:T(8,128)(2,1)S(1)}, bf16[512,256]{1,0:T(8,128)(2,1)S(1)}, u32[]{:S(2)}, u32[]{:S(2)}) collective-permute-start(bf16[512,256]{1,0:T(8,128)(2,1)S(1)} %pad_maximum_fusion.8), channel_id=1, source_target_pairs={{0,6},{1,7},{2,0},{3,1},{4,2},{5,3},{6,4},{7,5},{8,14},{9,15},{10,... | collective-permute-start | bytes 786440 | tf_op jit(solution)/shard_map/ppermute | solution.py:32
  124.6 8.0 %collective-permute-start.15 = (bf16[512,256]{1,0:T(8,128)(2,1)S(1)}, bf16[512,256]{1,0:T(8,128)(2,1)S(1)}, u32[]{:S(2)}, u32[]{:S(2)}) collective-permute-start(bf16[512,256]{1,0:T(8,128)(2,1)S(1)} %pad_maximum_fusion.6), channel_id=1, source_target_pairs={{0,8},{1,9},{2,10},{3,11},{4,12},{5,13},{6,14},{7,15},{8,0},{9,1},... | collective-permute-start | bytes 786440 | tf_op jit(solution)/shard_map/ppermute | solution.py:32
  127.2 32.7 %collective-permute-start.38 = (bf16[64,896]{1,0:T(8,128)(2,1)S(1)}, bf16[64,896]{1,0:T(8,128)(2,1)S(1)}, u32[]{:S(2)}, u32[]{:S(2)}) collective-permute-start(bf16[64,896]{1,0:T(8,128)(2,1)S(1)} %get-tuple-element.69), channel_id=1, source_target_pairs={{0,6},{1,7},{2,0},{3,1},{4,2},{5,3},{6,4},{7,5},{8,14},{9,15},{10,... | collective-permute-start | bytes 344072 | tf_op jit(solution)/shard_map/ppermute | solution.py:32
  134.0 18.8 %copy-start.17 = (bf16[1,512,256]{2,1,0:T(8,128)(2,1)S(1)}, bf16[1,512,256]{2,1,0:T(8,128)(2,1)}, u32[]{:S(2)}) copy-start(bf16[1,512,256]{2,1,0:T(8,128)(2,1)} %param.13) | copy-start | bytes 786436
  134.0 6.4 %collective-permute-start.20 = (bf16[256,256]{1,0:T(8,128)(2,1)S(1)}, bf16[256,256]{1,0:T(8,128)(2,1)S(1)}, u32[]{:S(2)}, u32[]{:S(2)}) collective-permute-start(bf16[256,256]{1,0:T(8,128)(2,1)S(1)} %get-tuple-element.33), channel_id=1, source_target_pairs={{0,6},{1,7},{2,0},{3,1},{4,2},{5,3},{6,4},{7,5},{8,14},{9,15},{10,... | collective-permute-start | bytes 393224 | tf_op jit(solution)/shard_map/ppermute | solution.py:32
  137.3 5.4 %collective-permute-start.19 = (bf16[256,256]{1,0:T(8,128)(2,1)S(1)}, bf16[256,256]{1,0:T(8,128)(2,1)S(1)}, u32[]{:S(2)}, u32[]{:S(2)}) collective-permute-start(bf16[256,256]{1,0:T(8,128)(2,1)S(1)} %get-tuple-element.18), channel_id=1, source_target_pairs={{0,2},{1,3},{2,4},{3,5},{4,6},{5,7},{6,0},{7,1},{8,10},{9,11},{10,... | collective-permute-start | bytes 393224 | tf_op jit(solution)/shard_map/ppermute | solution.py:32
  137.3 11.4 %collective-permute-start.18 = (bf16[512,256]{1,0:T(8,128)(2,1)S(1)}, bf16[512,256]{1,0:T(8,128)(2,1)S(1)}, u32[]{:S(2)}, u32[]{:S(2)}) collective-permute-start(bf16[512,256]{1,0:T(8,128)(2,1)S(1)} %pad_maximum_fusion.9), channel_id=1, source_target_pairs={{0,6},{1,7},{2,0},{3,1},{4,2},{5,3},{6,4},{7,5},{8,14},{9,15},{10,... | collective-permute-start | bytes 786440 | tf_op jit(solution)/shard_map/ppermute | solution.py:32
  140.4 8.3 %collective-permute-start.16 = (bf16[512,256]{1,0:T(8,128)(2,1)S(1)}, bf16[512,256]{1,0:T(8,128)(2,1)S(1)}, u32[]{:S(2)}, u32[]{:S(2)}) collective-permute-start(bf16[512,256]{1,0:T(8,128)(2,1)S(1)} %pad_maximum_fusion.7), channel_id=1, source_target_pairs={{0,2},{1,3},{2,4},{3,5},{4,6},{5,7},{6,0},{7,1},{8,10},{9,11},{10,... | collective-permute-start | bytes 786440 | tf_op jit(solution)/shard_map/ppermute | solution.py:32
  143.7 9.1 %collective-permute-start.21 = (bf16[512,256]{1,0:T(8,128)(2,1)S(1)}, bf16[512,256]{1,0:T(8,128)(2,1)S(1)}, u32[]{:S(2)}, u32[]{:S(2)}) collective-permute-start(bf16[512,256]{1,0:T(8,128)(2,1)S(1)} %fusion.5), channel_id=1, source_target_pairs={{0,8},{1,9},{2,10},{3,11},{4,12},{5,13},{6,14},{7,15},{8,0},{9,1},... | collective-permute-start | bytes 786440 | tf_op jit(solution)/shard_map/ppermute | solution.py:32
  147.0 12.9 %collective-permute-start.37 = (bf16[64,896]{1,0:T(8,128)(2,1)S(1)}, bf16[64,896]{1,0:T(8,128)(2,1)S(1)}, u32[]{:S(2)}, u32[]{:S(2)}) collective-permute-start(bf16[64,896]{1,0:T(8,128)(2,1)S(1)} %get-tuple-element.71), channel_id=1, source_target_pairs={{0,2},{1,3},{2,4},{3,5},{4,6},{5,7},{6,0},{7,1},{8,10},{9,11},{10,... | collective-permute-start | bytes 344072 | tf_op jit(solution)/shard_map/ppermute | solution.py:32
  153.9 8.2 %collective-permute-start.24 = (bf16[512,256]{1,0:T(8,128)(2,1)S(1)}, bf16[512,256]{1,0:T(8,128)(2,1)S(1)}, u32[]{:S(2)}, u32[]{:S(2)}) collective-permute-start(bf16[512,256]{1,0:T(8,128)(2,1)S(1)} %get-tuple-element.10), channel_id=1, source_target_pairs={{0,8},{1,9},{2,10},{3,11},{4,12},{5,13},{6,14},{7,15},{8,0},{9,1},... | collective-permute-start | bytes 786440 | tf_op jit(solution)/shard_map/ppermute | solution.py:32
  157.9 7.4 %collective-permute-start.23 = (bf16[512,256]{1,0:T(8,128)(2,1)S(1)}, bf16[512,256]{1,0:T(8,128)(2,1)S(1)}, u32[]{:S(2)}, u32[]{:S(2)}) collective-permute-start(bf16[512,256]{1,0:T(8,128)(2,1)S(1)} %get-tuple-element.10), channel_id=1, source_target_pairs={{0,6},{1,7},{2,0},{3,1},{4,2},{5,3},{6,4},{7,5},{8,14},{9,15},{10,... | collective-permute-start | bytes 786440 | tf_op jit(solution)/shard_map/ppermute | solution.py:32
  159.9 22.4 %collective-permute-start.39 = (bf16[8,128,896]{2,1,0:T(8,128)(2,1)S(1)}, bf16[8,128,896]{2,1,0:T(8,128)(2,1)S(1)}, u32[]{:S(2)}, u32[]{:S(2)}) collective-permute-start(bf16[8,128,896]{2,1,0:T(8,128)(2,1)S(1)} %fusion.34.mine_ref), channel_id=1, source_target_pairs={{0,1},{1,0},{2,3},{3,2},{4,5},{5,4},{6,7},{7,6},{8,9},{9,8},{10,11... | collective-permute-start | bytes 5505032 | tf_op jit(solution)/shard_map/ppermute | solution.py:32
  160.0 8.7 %collective-permute-start.22 = (bf16[512,256]{1,0:T(8,128)(2,1)S(1)}, bf16[512,256]{1,0:T(8,128)(2,1)S(1)}, u32[]{:S(2)}, u32[]{:S(2)}) collective-permute-start(bf16[512,256]{1,0:T(8,128)(2,1)S(1)} %get-tuple-element.10), channel_id=1, source_target_pairs={{0,2},{1,3},{2,4},{3,5},{4,6},{5,7},{6,0},{7,1},{8,10},{9,11},{10,... | collective-permute-start | bytes 786440 | tf_op jit(solution)/shard_map/ppermute | solution.py:32
  165.4 6.4 %collective-permute-start.26 = (bf16[512,256]{1,0:T(8,128)(2,1)S(1)}, bf16[512,256]{1,0:T(8,128)(2,1)S(1)}, u32[]{:S(2)}, u32[]{:S(2)}) collective-permute-start(bf16[512,256]{1,0:T(8,128)(2,1)S(1)} %pad_maximum_fusion.11), channel_id=1, source_target_pairs={{0,6},{1,7},{2,0},{3,1},{4,2},{5,3},{6,4},{7,5},{8,14},{9,15},{10,... | collective-permute-start | bytes 786440 | tf_op jit(solution)/shard_map/ppermute | solution.py:32
  168.8 7.9 %collective-permute-start.25 = (bf16[512,256]{1,0:T(8,128)(2,1)S(1)}, bf16[512,256]{1,0:T(8,128)(2,1)S(1)}, u32[]{:S(2)}, u32[]{:S(2)}) collective-permute-start(bf16[512,256]{1,0:T(8,128)(2,1)S(1)} %pad_maximum_fusion.10), channel_id=1, source_target_pairs={{0,2},{1,3},{2,4},{3,5},{4,6},{5,7},{6,0},{7,1},{8,10},{9,11},{10,... | collective-permute-start | bytes 786440 | tf_op jit(solution)/shard_map/ppermute | solution.py:32
  169.1 9.4 %collective-permute-start.27 = (bf16[512,256]{1,0:T(8,128)(2,1)S(1)}, bf16[512,256]{1,0:T(8,128)(2,1)S(1)}, u32[]{:S(2)}, u32[]{:S(2)}) collective-permute-start(bf16[512,256]{1,0:T(8,128)(2,1)S(1)} %pad_maximum_fusion.12), channel_id=1, source_target_pairs={{0,8},{1,9},{2,10},{3,11},{4,12},{5,13},{6,14},{7,15},{8,0},{9,1},... | collective-permute-start | bytes 786440 | tf_op jit(solution)/shard_map/ppermute | solution.py:32
  171.8 6.8 %collective-permute-start.29 = (bf16[256,256]{1,0:T(8,128)(2,1)S(1)}, bf16[256,256]{1,0:T(8,128)(2,1)S(1)}, u32[]{:S(2)}, u32[]{:S(2)}) collective-permute-start(bf16[256,256]{1,0:T(8,128)(2,1)S(1)} %get-tuple-element.45), channel_id=1, source_target_pairs={{0,6},{1,7},{2,0},{3,1},{4,2},{5,3},{6,4},{7,5},{8,14},{9,15},{10,... | collective-permute-start | bytes 393224 | tf_op jit(solution)/shard_map/ppermute | solution.py:32
  176.7 5.5 %collective-permute-start.28 = (bf16[256,256]{1,0:T(8,128)(2,1)S(1)}, bf16[256,256]{1,0:T(8,128)(2,1)S(1)}, u32[]{:S(2)}, u32[]{:S(2)}) collective-permute-start(bf16[256,256]{1,0:T(8,128)(2,1)S(1)} %get-tuple-element.47), channel_id=1, source_target_pairs={{0,2},{1,3},{2,4},{3,5},{4,6},{5,7},{6,0},{7,1},{8,10},{9,11},{10,... | collective-permute-start | bytes 393224 | tf_op jit(solution)/shard_map/ppermute | solution.py:32
  182.2 8.5 %collective-permute-start.30 = (bf16[8,512,256]{2,1,0:T(8,128)(2,1)S(1)}, bf16[8,512,256]{2,1,0:T(8,128)(2,1)S(1)}, u32[]{:S(2)}, u32[]{:S(2)}) collective-permute-start(bf16[8,512,256]{2,1,0:T(8,128)(2,1)S(1)} %fusion.18.mine_ref), channel_id=1, source_target_pairs={{0,1},{1,0},{2,3},{3,2},{4,5},{5,4},{6,7},{7,6},{8,9},{9,8},{10,11... | collective-permute-start | bytes 6291464 | tf_op jit(solution)/shard_map/ppermute | solution.py:32
  189.4 12.9 %collective-permute-start.40 = (bf16[2,256,256]{2,1,0:T(8,128)(2,1)S(1)}, bf16[2,256,256]{2,1,0:T(8,128)(2,1)S(1)}, u32[]{:S(2)}, u32[]{:S(2)}) collective-permute-start(bf16[2,256,256]{2,1,0:T(8,128)(2,1)S(1)} %slice_bitcast_fusion), channel_id=1, source_target_pairs={{0,16},{16,32},{32,48},{1,17},{17,33},{33,49},{2,18},{18,34},{34,5... | collective-permute-start | bytes 786440 | tf_op jit(solution)/shard_map/ppermute | solution.py:355
  190.7 11.6 %copy-start.2 = (bf16[2,8,8,2,16,256]{5,4,3,2,1,0:T(8,128)(2,1)S(1)}, bf16[2,8,8,2,16,256]{5,4,3,2,1,0:T(8,128)(2,1)}, u32[]{:S(2)}) copy-start(bf16[2,8,8,2,16,256]{5,4,3,2,1,0:T(8,128)(2,1)} %shard_map.133) | copy-start | bytes 6291460
  209.4 4.3 %collective-permute-start.41 = (bf16[8,512,256]{2,1,0:T(8,128)(2,1)S(1)}, bf16[8,512,256]{2,1,0:T(8,128)(2,1)S(1)}, u32[]{:S(2)}, u32[]{:S(2)}) collective-permute-start(bf16[8,512,256]{2,1,0:T(8,128)(2,1)S(1)} %shard_map.136), channel_id=1, source_target_pairs={{0,1},{1,0},{2,3},{3,2},{4,5},{5,4},{6,7},{7,6},{8,9},{9,8},{10,11... | collective-permute-start | bytes 6291464 | tf_op jit(solution)/shard_map/ppermute | solution.py:32
  213.9 10.1 %collective-permute-start.42 = (bf16[512,256]{1,0:T(8,128)(2,1)S(1)}, bf16[512,256]{1,0:T(8,128)(2,1)S(1)}, u32[]{:S(2)}, u32[]{:S(2)}) collective-permute-start(bf16[512,256]{1,0:T(8,128)(2,1)S(1)} %pad_maximum_fusion.13), channel_id=1, source_target_pairs={{0,2},{1,3},{2,4},{3,5},{4,6},{5,7},{6,0},{7,1},{8,10},{9,11},{10,... | collective-permute-start | bytes 786440 | tf_op jit(solution)/shard_map/ppermute | solution.py:32
  214.1 10.0 %collective-permute-start.45 = (bf16[512,256]{1,0:T(8,128)(2,1)S(1)}, bf16[512,256]{1,0:T(8,128)(2,1)S(1)}, u32[]{:S(2)}, u32[]{:S(2)}) collective-permute-start(bf16[512,256]{1,0:T(8,128)(2,1)S(1)} %pad_maximum_fusion.16), channel_id=1, source_target_pairs={{0,6},{1,7},{2,0},{3,1},{4,2},{5,3},{6,4},{7,5},{8,14},{9,15},{10,... | collective-permute-start | bytes 786440 | tf_op jit(solution)/shard_map/ppermute | solution.py:32
  217.4 9.9 %collective-permute-start.43 = (bf16[512,256]{1,0:T(8,128)(2,1)S(1)}, bf16[512,256]{1,0:T(8,128)(2,1)S(1)}, u32[]{:S(2)}, u32[]{:S(2)}) collective-permute-start(bf16[512,256]{1,0:T(8,128)(2,1)S(1)} %pad_maximum_fusion.14), channel_id=1, source_target_pairs={{0,8},{1,9},{2,10},{3,11},{4,12},{5,13},{6,14},{7,15},{8,0},{9,1},... | collective-permute-start | bytes 786440 | tf_op jit(solution)/shard_map/ppermute | solution.py:32
  227.2 18.6 %copy-start.1 = (bf16[64,8,896]{2,1,0:T(8,128)(2,1)S(1)}, bf16[64,8,896]{2,1,0:T(8,128)(2,1)}, u32[]{:S(2)}) copy-start(bf16[64,8,896]{2,1,0:T(8,128)(2,1)} %param.23) | copy-start | bytes 2752516
  227.5 6.8 %collective-permute-start.48 = (bf16[256,256]{1,0:T(8,128)(2,1)S(1)}, bf16[256,256]{1,0:T(8,128)(2,1)S(1)}, u32[]{:S(2)}, u32[]{:S(2)}) collective-permute-start(bf16[256,256]{1,0:T(8,128)(2,1)S(1)} %get-tuple-element.23), channel_id=1, source_target_pairs={{0,6},{1,7},{2,0},{3,1},{4,2},{5,3},{6,4},{7,5},{8,14},{9,15},{10,... | collective-permute-start | bytes 393224 | tf_op jit(solution)/shard_map/ppermute | solution.py:32
  230.6 6.3 %collective-permute-start.47 = (bf16[256,256]{1,0:T(8,128)(2,1)S(1)}, bf16[256,256]{1,0:T(8,128)(2,1)S(1)}, u32[]{:S(2)}, u32[]{:S(2)}) collective-permute-start(bf16[256,256]{1,0:T(8,128)(2,1)S(1)} %get-tuple-element.12), channel_id=1, source_target_pairs={{0,2},{1,3},{2,4},{3,5},{4,6},{5,7},{6,0},{7,1},{8,10},{9,11},{10,... | collective-permute-start | bytes 393224 | tf_op jit(solution)/shard_map/ppermute | solution.py:32
  230.6 8.2 %collective-permute-start.46 = (bf16[512,256]{1,0:T(8,128)(2,1)S(1)}, bf16[512,256]{1,0:T(8,128)(2,1)S(1)}, u32[]{:S(2)}, u32[]{:S(2)}) collective-permute-start(bf16[512,256]{1,0:T(8,128)(2,1)S(1)} %pad_maximum_fusion.17), channel_id=1, source_target_pairs={{0,6},{1,7},{2,0},{3,1},{4,2},{5,3},{6,4},{7,5},{8,14},{9,15},{10,... | collective-permute-start | bytes 786440 | tf_op jit(solution)/shard_map/ppermute | solution.py:32
  232.7 7.9 %collective-permute-start.44 = (bf16[512,256]{1,0:T(8,128)(2,1)S(1)}, bf16[512,256]{1,0:T(8,128)(2,1)S(1)}, u32[]{:S(2)}, u32[]{:S(2)}) collective-permute-start(bf16[512,256]{1,0:T(8,128)(2,1)S(1)} %pad_maximum_fusion.15), channel_id=1, source_target_pairs={{0,2},{1,3},{2,4},{3,5},{4,6},{5,7},{6,0},{7,1},{8,10},{9,11},{10,... | collective-permute-start | bytes 786440 | tf_op jit(solution)/shard_map/ppermute | solution.py:32
  237.0 8.0 %collective-permute-start.49 = (bf16[512,256]{1,0:T(8,128)(2,1)S(1)}, bf16[512,256]{1,0:T(8,128)(2,1)S(1)}, u32[]{:S(2)}, u32[]{:S(2)}) collective-permute-start(bf16[512,256]{1,0:T(8,128)(2,1)S(1)} %fusion), channel_id=1, source_target_pairs={{0,8},{1,9},{2,10},{3,11},{4,12},{5,13},{6,14},{7,15},{8,0},{9,1},... | collective-permute-start | bytes 786440 | tf_op jit(solution)/shard_map/ppermute | solution.py:32
  (9 other events, 36.6 us)

commit v2 on v1

v2 whole, which is shorter than its diff:
```python
import jax
import jax.numpy as jnp
from jax import lax
from jax.experimental import pallas as pl
from jax.experimental.pallas import tpu as pltpu
from jax.sharding import PartitionSpec as P

HEAD = 128
SPAN = 64
NB_TOK = 128
NB_PER = 2
LOG2E = 1.4426950408889634
norm_eps = 1e-05
mask_floor = -1e30

CHIPS = ((0, 0), (0, -1), (0, 1), (1, 0), (0, 2), (1, -1), (1, 1), (1, 2))


def route(dy, dx, dc):
    return [
        (y * 8 + x * 2 + c, ((y + dy) % 2) * 8 + ((x + dx) % 4) * 2 + (c + dc) % 2)
        for y in range(2)
        for x in range(4)
        for c in range(2)
    ]


TO_RIGHT, TO_LEFT, TO_X2 = route(0, 1, 0), route(0, -1, 0), route(0, 2, 0)
TO_Y, TO_CORE = route(1, 0, 0), route(0, 0, 1)


def mp_send(block, pairs):
    return lax.ppermute(block, "mp", pairs)


def relative_ids():
    me = lax.axis_index("mp")
    y, x, c = me // 8, (me // 2) % 4, me % 2
    return jnp.stack(
        [
            ((y + dy) % 2) * 8 + ((x + dx) % 4) * 2 + (c + dc) % 2
            for dc in range(2)
            for dy, dx in CHIPS
        ]
    ).astype(jnp.int32)


def corner(block):
    return block[(0,) * (block.ndim - 2) + (slice(0, 16), slice(0, 128))]


def gather_mp(shard, during_first=None, during_second=None, all_first=False):
    tie = lax.optimization_barrier
    from_y, from_x2 = mp_send(shard, TO_Y), mp_send(shard, TO_X2)
    from_left, from_right = mp_send(shard, TO_RIGHT), mp_send(shard, TO_LEFT)
    if all_first:
        (from_y, from_x2, from_left, from_right), during_first = tie(
            ((from_y, from_x2, from_left, from_right), during_first)
        )
    else:
        (from_y, from_x2), during_first = tie(((from_y, from_x2), during_first))
    left_y, right_y = mp_send(from_y, TO_RIGHT), mp_send(from_y, TO_LEFT)
    y_x2 = mp_send(from_x2, TO_Y)
    near = jnp.stack([shard, from_left, from_right, from_y])
    near_partner = mp_send(near, TO_CORE)
    if callable(during_second):
        during_second = during_second(during_first)
    far, during_second, _ = tie(
        (jnp.stack([from_x2, left_y, right_y, y_x2]), during_second, corner(near))
    )
    return (near, far, near_partner, mp_send(far, TO_CORE)), during_first, during_second


def scatter_mp(mine, partner, during_first=None):
    partner = mp_send(partner, TO_CORE)

    def part(i):
        return mine[i].astype(jnp.float32) + partner[i].astype(jnp.float32)

    b16, f32 = jnp.bfloat16, jnp.float32
    _, left, right, y, x2, y_left, y_right, y2 = range(8)
    far = mp_send(part(y2).astype(b16), TO_Y)
    from_left = mp_send(part(y_right).astype(b16), TO_RIGHT)
    from_right = mp_send(part(y_left).astype(b16), TO_LEFT)
    near_left = mp_send(part(right).astype(b16), TO_RIGHT)
    near_right = mp_send(part(left).astype(b16), TO_LEFT)
    (far, from_left, from_right), during_first = lax.optimization_barrier(
        ((far, from_left, from_right), during_first)
    )
    from_x2 = mp_send((part(x2) + far.astype(f32)).astype(b16), TO_X2)
    from_y = mp_send((part(y) + from_left.astype(f32) + from_right.astype(f32)).astype(b16), TO_Y)
    return [mine, partner, near_left, near_right, from_x2, from_y], during_first


IN_VMEM = pl.BlockSpec(memory_space=pltpu.VMEM)
MIB = 1024 * 1024


def call(kernel, room, **kw):
    return pl.pallas_call(
        kernel,
        compiler_params=pltpu.CompilerParams(vmem_limit_bytes=room * MIB),
        **kw,
    )


STAT_ROWS = 16


def shard_to_send(ids, gain, summands):
    rows, feats = summands[0].shape[-2:]
    pick = [s.ndim == 3 for s in summands]

    def kernel(ids_ref, gain_ref, *refs):
        in_refs, (plain_ref, out_ref) = refs[:-2], refs[-2:]
        total = jnp.zeros((rows, feats), jnp.float32)
        for ref, leading in zip(in_refs, pick):
            total = total + (ref[0] if leading else ref[...]).astype(jnp.float32)
        plain = total.astype(jnp.bfloat16)
        plain_ref[...] = plain
        x = plain.astype(jnp.float32)
        out_ref[:rows] = (x * gain_ref[ids_ref[0]]).astype(jnp.bfloat16)
        squares = jnp.broadcast_to(jnp.sum(x * x, axis=1, keepdims=True), (rows, 128)).T
        line = jnp.concatenate(
            [squares[:1, i * feats : (i + 1) * feats] for i in range(rows // feats)]
        )
        high = line.astype(jnp.bfloat16).astype(jnp.float32)
        block = jnp.concatenate(
            [high, line - high, jnp.zeros((STAT_ROWS - 2 * (rows // feats), feats), jnp.float32)]
        )
        out_ref[rows:] = block.astype(jnp.bfloat16)

    return call(
        kernel,
        8,
        in_specs=[pl.BlockSpec(memory_space=pltpu.SMEM)] + [IN_VMEM] * (1 + len(summands)),
        out_specs=[IN_VMEM] * 2,
        out_shape=[
            jax.ShapeDtypeStruct((rows, feats), jnp.bfloat16),
            jax.ShapeDtypeStruct((rows + STAT_ROWS, feats), jnp.bfloat16),
        ],
    )(ids[:1], gain.reshape(-1, 1, feats), *summands)


def normed_projection(ids, stacks, weights):
    each, rows, feats = stacks[0].shape
    rows = rows - STAT_ROWS
    depth = each * len(stacks) * feats
    count = len(weights)
    width = weights[0].shape[1]
    lines = rows // feats

    def kernel(ids_ref, *refs):
        x_refs, w_refs = refs[: len(stacks)], refs[len(stacks) : -1]
        out_ref = refs[-1]
        stat = jnp.zeros((STAT_ROWS, feats), jnp.float32)
        for x_ref in x_refs:
            for i in range(each):
                stat = stat + x_ref[i, rows:].astype(jnp.float32)
        stat = stat[:lines] + stat[lines : 2 * lines]
        inv_line = lax.rsqrt(stat * (1.0 / depth) + norm_eps)
        inv = jnp.concatenate(
            [jnp.broadcast_to(inv_line[i : i + 1], (128, feats)).T for i in range(lines)]
        )
        inv = jnp.concatenate([inv] * (width // 128), axis=1)
        x = jnp.concatenate([x_ref[i, :rows] for x_ref in x_refs for i in range(each)], axis=1)
        for i, w_ref in enumerate(w_refs):
            w = jnp.concatenate(
                [
                    w_ref[pl.ds(pl.multiple_of(ids_ref[k] * feats, feats), feats)]
                    for k in range(each * len(stacks))
                ]
            )
            product = jnp.dot(x, w, preferred_element_type=jnp.float32)
            out_ref[i] = (product * inv).astype(jnp.bfloat16)

    return call(
        kernel,
        12,
        in_specs=[pl.BlockSpec(memory_space=pltpu.SMEM)] + [IN_VMEM] * (len(stacks) + count),
        out_specs=IN_VMEM,
        out_shape=jax.ShapeDtypeStruct((count, rows, width), jnp.bfloat16),
        cost_estimate=pl.CostEstimate(
            flops=2 * rows * depth * width * count,
            bytes_accessed=2 * (rows + width * count) * depth,
            transcendentals=0,
        ),
    )(ids, *stacks, *weights)


def self_attention(queries, kv_own, kv_back1, kv_back2, kv_back3):
    rows, width = queries.shape
    heads = width // HEAD
    chunk = rows // 2
    scale = HEAD ** (-0.5) * LOG2E

    def kernel(ctx_ref, q_ref, own_ref, b1_ref, b2_ref, b3_ref, out_ref):
        kv = (own_ref, b1_ref, b2_ref, b3_ref)
        start = pl.program_id(0) * chunk
        for back in range(4):

            @pl.when(ctx_ref[0] == back)
            def _(back=back):
                pos = start + lax.broadcasted_iota(jnp.int32, (chunk, rows), 0)
                allowed = lax.broadcasted_iota(jnp.int32, (chunk, rows), 1) <= pos
                for h in range(heads):
                    cols = slice(h * HEAD, (h + 1) * HEAD)
                    q = q_ref[:, cols]
                    scores = []
                    for d in range(back + 1):
                        s = lax.dot_general(
                            q,
                            kv[d][0, :, cols],
                            (((1,), (1,)), ((), ())),
                            preferred_element_type=jnp.float32,
                        ) * scale
                        scores.append(jnp.where(allowed, s, mask_floor) if d == 0 else s)
                    peak = jnp.max(scores[0], axis=1, keepdims=True)
                    for s in scores[1:]:
                        peak = jnp.maximum(peak, jnp.max(s, axis=1, keepdims=True))
                    total, mixed = 0.0, 0.0
                    for d in range(back + 1):
                        weights = jnp.exp2(scores[d] - peak)
                        total = total + jnp.sum(weights, axis=1, keepdims=True)
                        mixed = mixed + jnp.dot(
                            weights.astype(jnp.bfloat16),
                            kv[d][1, :, cols],
                            preferred_element_type=jnp.float32,
                        )
                    out_ref[:, cols] = (mixed / total).astype(jnp.bfloat16)

    whole = pl.BlockSpec((2, rows, width), lambda c: (0, 0, 0))
    block = pl.BlockSpec((chunk, width), lambda c: (c, 0))
    return call(
        kernel,
        16,
        grid=(rows // chunk,),
        in_specs=[pl.BlockSpec(memory_space=pltpu.SMEM), block] + [whole] * 4,
        out_specs=block,
        out_shape=jax.ShapeDtypeStruct((rows, width), jnp.bfloat16),
        cost_estimate=pl.CostEstimate(
            flops=16 * rows * rows * width,
            bytes_accessed=10 * rows * width,
            transcendentals=8 * rows * rows,
        ),
    )(lax.axis_index("ctx").reshape(1).astype(jnp.int32), queries, kv_own, kv_back1, kv_back2, kv_back3)


def output_blocks(ids, inputs, weight):
    rows = inputs.shape[0]
    blocks = ids.shape[0]
    width = 256

    def kernel(ids_ref, in_ref, w_ref, out_ref):
        for k in range(blocks):
            start = pl.multiple_of(ids_ref[k] * width, width)
            out_ref[k] = jnp.dot(
                in_ref[...], w_ref[:, pl.ds(start, width)], preferred_element_type=jnp.float32
            ).astype(jnp.bfloat16)

    return call(
        kernel,
        12,
        in_specs=[pl.BlockSpec(memory_space=pltpu.SMEM), IN_VMEM, IN_VMEM],
        out_specs=IN_VMEM,
        out_shape=jax.ShapeDtypeStruct((blocks, rows, width), jnp.bfloat16),
        cost_estimate=pl.CostEstimate(
            flops=2 * rows * inputs.shape[1] * width * blocks,
            bytes_accessed=2 * rows * width * blocks,
            transcendentals=0,
        ),
    )(ids, inputs, weight)


def neighbour_projection(stacks, w_cross_kv):
    each, rows, depth = stacks[0].shape
    width = w_cross_kv.shape[2]
    spans = rows // 16

    def kernel(*refs):
        x_refs, w_ref, out_ref = refs[:-2], refs[-2], refs[-1]
        for n, x_ref in enumerate(x_refs):
            x = x_ref[...].reshape(each * rows, depth)
            for part in range(2):
                res = jnp.dot(x, w_ref[part], preferred_element_type=jnp.float32)
                res = res.astype(jnp.bfloat16).reshape(each, spans, 16, width)
                for i in range(each):
                    out_ref[part, :, n * each + i] = res[i]

    return call(
        kernel,
        16,
        in_specs=[IN_VMEM] * (len(stacks) + 1),
        out_specs=IN_VMEM,
        out_shape=jax.ShapeDtypeStruct((2, spans, each * len(stacks), 16, width), jnp.bfloat16),
        cost_estimate=pl.CostEstimate(
            flops=4 * rows * each * len(stacks) * depth * width,
            bytes_accessed=2 * rows * each * len(stacks) * depth,
            transcendentals=0,
        ),
    )(*stacks, w_cross_kv)


def cross_attention(queries, neighbour_kv, earlier):
    rows, width = queries.shape
    heads = width // HEAD
    spans = neighbour_kv.shape[1]
    tokens = NB_PER * NB_TOK
    scale = HEAD ** (-0.5) * LOG2E

    def kernel(q_ref, kv_ref, earlier_ref, out_ref):
        row = lax.broadcasted_iota(jnp.int32, (rows, HEAD), 0)

        def span(part, g, cols):
            ref = earlier_ref.at[part] if g == 0 else kv_ref.at[part, g - 1]
            return ref[:, :, cols].reshape(tokens, HEAD)

        for h in range(heads):
            cols = slice(h * HEAD, (h + 1) * HEAD)
            q = q_ref[:, cols]
            shifted = pltpu.roll(q.astype(jnp.float32), 1, 0).astype(jnp.bfloat16)
            groups = [shifted[g * SPAN : (g + 1) * SPAN] for g in range(spans)] + [q[rows - 16 :]]
            s = jnp.concatenate(
                [
                    lax.dot_general(
                        groups[g],
                        span(0, g, cols),
                        (((1,), (1,)), ((), ())),
                        preferred_element_type=jnp.float32,
                    )
                    for g in range(spans + 1)
                ]
            )
            s = s * scale
            weights = jnp.exp2(s - jnp.max(s, axis=1, keepdims=True))
            total = jnp.sum(weights, axis=1, keepdims=True)
            weights = weights.astype(jnp.bfloat16)
            mixed = jnp.concatenate(
                [
                    jnp.dot(
                        weights[g * SPAN : min((g + 1) * SPAN, rows + 16)],
                        span(1, g, cols),
                        preferred_element_type=jnp.float32,
                    )
                    for g in range(spans + 1)
                ]
            )
            mixed = mixed / total
            back = pltpu.roll(mixed[:rows], rows - 1, 0)
            final = jnp.where(row == rows - 1, mixed[rows + 15 :], back)
            out_ref[:, cols] = final.astype(jnp.bfloat16)

    return call(
        kernel,
        12,
        in_specs=[IN_VMEM] * 3,
        out_specs=IN_VMEM,
        out_shape=jax.ShapeDtypeStruct((rows, width), jnp.bfloat16),
    )(queries, neighbour_kv, earlier)


def pick_neighbours(encoded, owners, slots):
    group_count = lax.axis_size(("pool", "ctx"))
    my_group = lax.axis_index(("pool", "ctx"))
    per_group = owners.size // group_count
    capacity = max(2, 2 * per_group // group_count)
    owner_table = owners.reshape(group_count, per_group)
    slot_table = slots.reshape(group_count, per_group)
    matched = (owner_table == my_group).astype(jnp.int32)
    earlier = jnp.arange(per_group)[None, :] < jnp.arange(per_group)[:, None]
    order_rank = jnp.sum(matched[:, None, :] * earlier.astype(jnp.int32)[None], axis=2)
    slot_index = jnp.arange(capacity, dtype=jnp.int32)
    picked = matched[:, None, :] * (order_rank[:, None, :] == slot_index[None, :, None]).astype(
        jnp.int32
    )
    source_rows = jnp.sum(picked * slot_table[:, None, :], axis=2).reshape(-1)
    outgoing = encoded[source_rows]
    outgoing = outgoing.reshape((group_count, capacity) + encoded.shape[1:])
    wanted = lax.dynamic_index_in_dim(owner_table, my_group, 0, keepdims=False)
    same_owner = (wanted[:, None] == wanted[None, :]).astype(jnp.int32)
    arrival = wanted * capacity + jnp.sum(same_owner * earlier.astype(jnp.int32), axis=1)
    return outgoing, arrival


def exchange_neighbours(outgoing, arrival):
    incoming = lax.all_to_all(outgoing, ("pool", "ctx"), split_axis=0, concat_axis=0, tiled=True)
    return incoming.reshape((-1,) + outgoing.shape[2:])[arrival]


def ctx_send(block, pairs):
    return lax.ppermute(block, "ctx", pairs)


def send_kv(kv):
    return ctx_send(kv, [(0, 1), (1, 2), (2, 3)]), ctx_send(kv, [(0, 3), (1, 0)])


def per_device(
    tokens,
    norm_gain,
    cross_gain,
    w_query,
    w_key,
    w_value,
    w_out,
    w_cross_query,
    w_cross_kv,
    w_cross_out,
    encoded,
    owners,
    slots,
):
    ids = relative_ids()
    half = ids.shape[0] // 2
    tie = lax.optimization_barrier
    _, shard = shard_to_send(ids, norm_gain, [tokens[0]])
    picked = pick_neighbours(encoded, owners, slots)
    fetched = exchange_neighbours(*picked)
    stacks, _, fetched = gather_mp(shard, picked, fetched)
    kv = normed_projection(ids, stacks, (w_key, w_value))
    kv, fetched = tie((kv, fetched))
    back1, back3 = send_kv(kv)
    queries = normed_projection(ids, stacks, (w_query,))[0]
    nb_stacks, _, attended = gather_mp(
        fetched.reshape(-1, fetched.shape[-1]),
        (corner(queries), corner(back3), corner(back1)),
        lambda _: self_attention(
            queries, kv, back1, ctx_send(back3, [(3, 2), (0, 3)]), back3
        ),
        all_first=True,
    )
    for_partner = output_blocks(ids[half:], attended, w_out)
    for_mine = output_blocks(ids[:half], attended, w_out)
    neighbour_kv = neighbour_projection(nb_stacks, w_cross_kv)
    summands, neighbour_kv = scatter_mp(for_mine, for_partner, neighbour_kv)
    earlier = ctx_send(neighbour_kv[:, -1], [(0, 1), (1, 2), (2, 3)])
    residual, shard = shard_to_send(ids, cross_gain, [tokens[0]] + summands)
    stacks, earlier, _ = gather_mp(shard, earlier)
    cross_queries = normed_projection(ids, stacks, (w_cross_query,))[0]
    crossed = cross_attention(cross_queries, neighbour_kv, earlier)
    for_partner = output_blocks(ids[half:], crossed, w_cross_out)
    for_mine = output_blocks(ids[:half], crossed, w_cross_out)
    summands, _ = scatter_mp(for_mine, for_partner)
    total = residual.astype(jnp.float32)
    for s in summands:
        total = total + (s[0] if s.ndim == 3 else s).astype(jnp.float32)
    return total.astype(jnp.bfloat16)[None]


def solution(mesh):
    placed = (
        P("pool", "ctx", "mp"),
        P(),
        P(),
        P(None, "mp"),
        P(None, "mp"),
        P(None, "mp"),
        P("mp", None),
        P(None, "mp"),
        P(None, None, "mp"),
        P("mp", None),
        P(("pool", "ctx"), "mp", None),
        P(),
        P(),
    )
    return jax.shard_map(
        per_device, mesh=mesh, in_specs=placed, out_specs=P("pool", "ctx", "mp"), check_vma=False
    )
```

time: 249 us -> 181 us (0.73)
  Pallas kernels: 62.4 us -> 27.2 us
  waiting for transfers between devices: 71 us -> 48.7 us
  local copies, waits for them, and re-layouts: 15.5 us -> 11.3 us
  starting transfers between devices: 84.4 us -> 80.4 us
    pallas_call x10 -> x12, Pallas kernels: 62.4 us -> 27.2 us  [the longest x3 9.33 us: normed_projection(): call(kernel, 12, in_specs=[pl.BlockSpec(memory_space=pltpu.SMEM)] + [IN_V...]
    ppermute x45 -> x43, waiting for transfers between devices: 69 us -> 44.4 us  [mp_send(): return lax.ppermute(block, 'mp', pairs)]
    unnamed x57 -> x36, local copies, waits for them, and re-layouts: 3.15 us -> 8.73 us
    another operation x6, other arithmetic: 1.91 us -> 7.06 us  [the longest x3 3.83 us: gather_mp(): jnp.stack([from_x2, left_y, right_y, y_x2])]
    ppermute x45 -> x43, starting transfers between devices: 63.8 us -> 60.8 us  [mp_send(): return lax.ppermute(block, 'mp', pairs)]
    slice x20 -> x0, local copies, waits for them, and re-layouts: 2.97 us -> none  [the longest x1 1.67 us: relay_kv(): top = ctx_send(back1[:, :half], [(1, 2), (2, 3)])]
    all_to_all x1, waiting for transfers between devices: 0.01 us -> 2.56 us  [exchange_neighbours(): lax.all_to_all(outgoing, ('pool', 'ctx'), split_axis=0, concat_axis=0, ti...]
    ppermute x5 -> x4, starting transfers between devices: 16.4 us -> 14.2 us  [ctx_send(): return lax.ppermute(block, 'ctx', pairs)]
  transfers between devices with their start and end apart: 51 -> 48, of which waited for: 29 -> 21; matrix products, arithmetic and copies ran while one was open for 10% -> 8% of each run, Pallas kernels for 17% -> 5%
where the time goes in v2:
time: 181 us; the launch traced here: 180 us
  starting transfers between devices  80.4 us (44%)
  waiting for transfers between devices  48.7 us (27%)
  Pallas kernels  27.2 us (15%)
  other arithmetic  12 us (7%)
  local copies, waits for them, and re-layouts  11.3 us (6%)
    ppermute x43, starting transfers between devices, mp_send(): return lax.ppermute(block, 'mp', pairs)  60.8 us
    ppermute x43, waiting for transfers between devices, mp_send(): return lax.ppermute(block, 'mp', pairs)  44.4 us
    ppermute x4, starting transfers between devices, ctx_send(): return lax.ppermute(block, 'ctx', pairs)  14.2 us
    pallas_call x3, Pallas kernels, normed_projection(): call(kernel, 12, in_specs=[pl.BlockSpec(memory_space=pltpu.SMEM)] + [IN_V...  9.33 us
    unnamed x36, local copies, waits for them, and re-layouts  8.73 us
    pallas_call x4, Pallas kernels, output_blocks(): call(kernel, 12, in_specs=[pl.BlockSpec(memory_space=pltpu.SMEM), IN_VMEM...  6.46 us
    all_to_all x1, starting transfers between devices, exchange_neighbours(): lax.all_to_all(outgoing, ('pool', 'ctx'), split_axis=0, concat_axis=0, ti...  5.43 us
    pallas_call x1, Pallas kernels, neighbour_projection(): call(kernel, 16, in_specs=[IN_VMEM] * (len(stacks) + 1), out_specs=IN_VME...  4.34 us
  transfers between devices with their start and end apart: 48, of which 21 were waited for; matrix products, arithmetic and copies ran while one was open for 8% of the time, Pallas kernels for 5%

profile of v2, /device:TPU:2, one launch (start us, length us, event | category | flops | bytes accessed | tf_op | source)
XLA Modules:
  0.0 180.2 jit_solution(13953873378734958886)
XLA Ops:
  2.5 3.2 %collective-permute-start.2 = (bf16[528,256]{1,0:T(8,128)(2,1)S(1)}, bf16[528,256]{1,0:T(8,128)(2,1)S(1)}, u32[]{:S(2)}, u32[]{:S(2)}) collective-permute-start(bf16[528,256]{1,0:T(8,128)(2,1)S(1)} %get-tuple-element.30), channel_id=1, source_target_pairs={{0,8},{1,9},{2,10},{3,11},{4,12},{5,13},{6,14},{7,15},{8,0},{9,1},... | collective-permute-start | bytes 811016 | tf_op jit(solution)/shard_map/ppermute | solution.py:33
  5.7 2.1 %collective-permute-start.3 = (bf16[528,256]{1,0:T(8,128)(2,1)S(1)}, bf16[528,256]{1,0:T(8,128)(2,1)S(1)}, u32[]{:S(2)}, u32[]{:S(2)}) collective-permute-start(bf16[528,256]{1,0:T(8,128)(2,1)S(1)} %get-tuple-element.30), channel_id=1, source_target_pairs={{0,4},{1,5},{2,6},{3,7},{4,0},{5,1},{6,2},{7,3},{8,12},{9,13},{10,... | collective-permute-start | bytes 811016 | tf_op jit(solution)/shard_map/ppermute | solution.py:33
  7.8 2.0 %collective-permute-start.1 = (bf16[528,256]{1,0:T(8,128)(2,1)S(1)}, bf16[528,256]{1,0:T(8,128)(2,1)}, u32[]{:S(2)}, u32[]{:S(2)}) collective-permute-start(bf16[528,256]{1,0:T(8,128)(2,1)S(1)} %get-tuple-element.30), channel_id=1, source_target_pairs={{0,6},{1,7},{2,0},{3,1},{4,2},{5,3},{6,4},{7,5},{8,14},{9,15},{10,... | collective-permute-start | bytes 811016 | tf_op jit(solution)/shard_map/ppermute | solution.py:33
  12.1 1.4 gather_fusion
  13.5 5.4 %all-to-all-start = ((bf16[8,4,8,896]{3,2,1,0:T(8,128)(2,1)}), bf16[8,4,8,896]{3,2,1,0:T(8,128)(2,1)S(1)}, u32[]{:S(2)}, u32[]{:S(2)}) async-start(bf16[8,4,8,896]{3,2,1,0:T(8,128)(2,1)} %bitcast.23), calls=%async_computation | async-start | bytes 917504 | tf_op jit(solution)/shard_map/all_to_all | solution.py:386
  19.2 2.7 %collective-permute-start.5 = (bf16[528,256]{1,0:T(8,128)(2,1)S(1)}, bf16[528,256]{1,0:T(8,128)(2,1)}, u32[]{:S(2)}, u32[]{:S(2)}) collective-permute-start(bf16[528,256]{1,0:T(8,128)(2,1)S(1)} %collective-permute-done.2), channel_id=1, source_target_pairs={{0,6},{1,7},{2,0},{3,1},{4,2},{5,3},{6,4},{7,5},{8,14},{9,15},{10,... | collective-permute-start | bytes 811016 | tf_op jit(solution)/shard_map/ppermute | solution.py:33
  21.9 1.8 %collective-permute-start.6 = (bf16[528,256]{1,0:T(8,128)(2,1)S(1)}, bf16[528,256]{1,0:T(8,128)(2,1)}, u32[]{:S(2)}, u32[]{:S(2)}) collective-permute-start(bf16[528,256]{1,0:T(8,128)(2,1)S(1)} %collective-permute-done.3), channel_id=1, source_target_pairs={{0,8},{1,9},{2,10},{3,11},{4,12},{5,13},{6,14},{7,15},{8,0},{9,1},... | collective-permute-start | bytes 811016 | tf_op jit(solution)/shard_map/ppermute | solution.py:33
  25.0 2.6 %all-to-all-done = bf16[8,4,8,896]{3,2,1,0:T(8,128)(2,1)S(1)} async-done(((bf16[8,4,8,896]{3,2,1,0:T(8,128)(2,1)}), bf16[8,4,8,896]{3,2,1,0:T(8,128)(2,1)S(1)}, u32[]{:S(2)}, u32[]{:S(2)}) %all-to-all-start) | async-done | bytes 458784 | tf_op jit(solution)/shard_map/all_to_all | solution.py:386
  28.2 2.9 %collective-permute-done.6 = bf16[528,256]{1,0:T(8,128)(2,1)} collective-permute-done((bf16[528,256]{1,0:T(8,128)(2,1)S(1)}, bf16[528,256]{1,0:T(8,128)(2,1)}, u32[]{:S(2)}, u32[]{:S(2)}) %collective-permute-start.6) | collective-permute-done | bytes 270368 | tf_op jit(solution)/shard_map/ppermute | solution.py:33
  31.1 1.3 pad_maximum_fusion.1.refs_1_
  32.8 2.6 %collective-permute-done.8.refs_3_ = bf16[4,528,256]{2,1,0:T(8,128)(2,1)} collective-permute-done((bf16[4,528,256]{2,1,0:T(8,128)(2,1)S(1)}, bf16[4,528,256]{2,1,0:T(8,128)(2,1)}, u32[]{:S(2)}, u32[]{:S(2)}) %collective-permute-start.8) | collective-permute-done | bytes 1081376 | tf_op jit(solution)/shard_map/ppermute | solution.py:33
  35.4 1.6 copy-done.3
  37.0 1.6 copy-done.4
  38.6 4.7 %shard_map.128.own_ref = bf16[2,512,256]{2,1,0:T(8,128)(2,1)} custom-call(s32[16]{0:T(128)S(1)} %stack.159.ids_ref, bf16[4,528,256]{2,1,0:T(8,128)(2,1)S(1)} %pad_maximum_fusion.refs_0_, bf16[4,528,256]{2,1,0:T(8,128)(2,1)S(1)} %pad_maximum_fusion.1.refs_1_, bf16[4,528,256]{2,1,0:T(8,128)(2,1)} %collective-permute-done.7.refs_2_, ...), custom_call_target="tpu_custom_call" | custom-call | flops 2147483648 | bytes 8388608 | tf_op jit(solution)/shard_map/pallas_call | solution.py:177
  43.3 4.9 %collective-permute-start.17 = (bf16[2,512,256]{2,1,0:T(8,128)(2,1)}, bf16[2,512,256]{2,1,0:T(8,128)(2,1)}, u32[]{:S(2)}, u32[]{:S(2)}) collective-permute-start(bf16[2,512,256]{2,1,0:T(8,128)(2,1)} %shard_map.128.own_ref), channel_id=1, source_target_pairs={{0,48},{16,0},{1,49},{17,1},{2,50},{18,2},{3,51},{19,3},{4,52},{20... | collective-permute-start | bytes 1572872 | tf_op jit(solution)/shard_map/ppermute | solution.py:391
  48.1 1.8 %collective-permute-start.10 = (bf16[128,896]{1,0:T(8,128)(2,1)S(1)}, bf16[128,896]{1,0:T(8,128)(2,1)}, u32[]{:S(2)}, u32[]{:S(2)}) collective-permute-start(bf16[128,896]{1,0:T(8,128)(2,1)S(1)} %bitcast.124), channel_id=1, source_target_pairs={{0,4},{1,5},{2,6},{3,7},{4,0},{5,1},{6,2},{7,3},{8,12},{9,13},{10,... | collective-permute-start | bytes 688136 | tf_op jit(solution)/shard_map/ppermute | solution.py:33
  50.0 2.4 %collective-permute-start.11 = (bf16[128,896]{1,0:T(8,128)(2,1)S(1)}, bf16[128,896]{1,0:T(8,128)(2,1)S(1)}, u32[]{:S(2)}, u32[]{:S(2)}) collective-permute-start(bf16[128,896]{1,0:T(8,128)(2,1)S(1)} %bitcast.125), channel_id=1, source_target_pairs={{0,2},{1,3},{2,4},{3,5},{4,6},{5,7},{6,0},{7,1},{8,10},{9,11},{10,... | collective-permute-start | bytes 688136 | tf_op jit(solution)/shard_map/ppermute | solution.py:33
  52.3 1.7 collective-permute-start.9
  54.0 4.3 %collective-permute-done.10 = bf16[128,896]{1,0:T(8,128)(2,1)} collective-permute-done((bf16[128,896]{1,0:T(8,128)(2,1)S(1)}, bf16[128,896]{1,0:T(8,128)(2,1)}, u32[]{:S(2)}, u32[]{:S(2)}) %collective-permute-start.10) | collective-permute-done | bytes 229408 | tf_op jit(solution)/shard_map/ppermute | solution.py:33
  58.4 2.4 %collective-permute-start.16 = (bf16[2,512,256]{2,1,0:T(8,128)(2,1)}, bf16[2,512,256]{2,1,0:T(8,128)(2,1)}, u32[]{:S(2)}, u32[]{:S(2)}) collective-permute-start(bf16[2,512,256]{2,1,0:T(8,128)(2,1)} %shard_map.128.own_ref), channel_id=1, source_target_pairs={{0,16},{16,32},{32,48},{1,17},{17,33},{33,49},{2,18},{18,34},{34,5... | collective-permute-start | bytes 1572872 | tf_op jit(solution)/shard_map/ppermute | solution.py:391
  60.8 5.5 %collective-permute-start.18 = (bf16[2,512,256]{2,1,0:T(8,128)(2,1)}, bf16[2,512,256]{2,1,0:T(8,128)(2,1)}, u32[]{:S(2)}, u32[]{:S(2)}) collective-permute-start(bf16[2,512,256]{2,1,0:T(8,128)(2,1)} %collective-permute-done.17.b3_ref), channel_id=1, source_target_pairs={{48,32},{0,48},{49,33},{1,49},{50,34},{2,50},{51,35},{3,51},{52,36... | collective-permute-start | bytes 1572872 | tf_op jit(solution)/shard_map/ppermute | solution.py:391
  66.6 2.5 %collective-permute-start.14 = (bf16[128,896]{1,0:T(8,128)(2,1)}, bf16[128,896]{1,0:T(8,128)(2,1)}, u32[]{:S(2)}, u32[]{:S(2)}) collective-permute-start(bf16[128,896]{1,0:T(8,128)(2,1)} %collective-permute-done.9), channel_id=1, source_target_pairs={{0,6},{1,7},{2,0},{3,1},{4,2},{5,3},{6,4},{7,5},{8,14},{9,15},{10,... | collective-permute-start | bytes 688136 | tf_op jit(solution)/shard_map/ppermute | solution.py:33
  69.2 1.7 collective-permute-start.15
  70.9 1.6 copy-done.5
  72.5 2.8 %shard_map.129 = bf16[1,512,256]{2,1,0:T(8,128)(2,1)S(1)} custom-call(s32[16]{0:T(128)S(1)} %stack.159.ids_ref, bf16[4,528,256]{2,1,0:T(8,128)(2,1)S(1)} %pad_maximum_fusion.refs_0_, bf16[4,528,256]{2,1,0:T(8,128)(2,1)S(1)} %pad_maximum_fusion.1.refs_1_, bf16[4,528,256]{2,1,0:T(8,128)(2,1)} %collective-permute-done.7.refs_2_, ...), custom_call_target="tpu_custom_call" | custom-call | flops 1073741824 | bytes 6291456 | tf_op jit(solution)/shard_map/pallas_call | solution.py:177
  75.4 1.9 %collective-permute-done.15 = bf16[128,896]{1,0:T(8,128)(2,1)} collective-permute-done((bf16[128,896]{1,0:T(8,128)(2,1)}, bf16[128,896]{1,0:T(8,128)(2,1)}, u32[]{:S(2)}, u32[]{:S(2)}) %collective-permute-start.15) | collective-permute-done | bytes 229408 | tf_op jit(solution)/shard_map/ppermute | solution.py:33
  77.2 2.4 %pad_maximum_fusion.4.refs_1_ = bf16[4,128,896]{2,1,0:T(8,128)(2,1)} fusion(bf16[1,128,896]{2,1,0:T(8,128)(2,1)} %bitcast.38, bf16[1,128,896]{2,1,0:T(8,128)(2,1)} %bitcast.37, bf16[1,128,896]{2,1,0:T(8,128)(2,1)} %bitcast.36, bf16[1,128,896]{2,1,0:T(8,128)(2,1)} %bitcast.35), kind=kLoop, calls=%fused_computation.6 | loop fusion | flops 1376256 | bytes 1835008 | tf_op jit(solution)/shard_map/stack | solution.py:69
  79.6 3.3 %shard_map.130.in_ref = bf16[512,256]{1,0:T(8,128)(2,1)S(1)} custom-call(s32[1]{0:T(128)} %bitcast.39.ctx_ref, bf16[512,256]{1,0:T(8,128)(2,1)S(1)} %bitcast.120, bf16[2,512,256]{2,1,0:T(8,128)(2,1)} %shard_map.128.own_ref, bf16[2,512,256]{2,1,0:T(8,128)(2,1)} %collective-permute-done.16.b1_ref, bf16[2,512,256]{2,1,0:T(8,128)(2,1)} %collective-permute-done.18.b2_ref, ...), custom_call_target="tpu_custom_call" | custom-call | flops 1073741824 | bytes 1310720 | tf_op jit(solution)/shard_map/pallas_call | solution.py:234
  83.0 2.6 %shard_map.132 = bf16[8,512,256]{2,1,0:T(8,128)(2,1)} custom-call(s32[8]{0:T(128)S(1)} %stack.175.ids_ref, bf16[512,256]{1,0:T(8,128)(2,1)S(1)} %shard_map.130.in_ref, bf16[256,4096]{1,0:T(8,128)(2,1)S(1)} %copy-done.1), custom_call_target="tpu_custom_call" | custom-call | flops 536870912 | bytes 2097152 | tf_op jit(solution)/shard_map/pallas_call | solution.py:261
  85.7 2.0 %pad_maximum_fusion.5.refs_0_ = bf16[4,128,896]{2,1,0:T(8,128)(2,1)} fusion(bf16[1,128,896]{2,1,0:T(8,128)(2,1)} %bitcast.50, bf16[1,128,896]{2,1,0:T(8,128)(2,1)S(1)} %bitcast.140, bf16[1,128,896]{2,1,0:T(8,128)(2,1)S(1)} %bitcast.139, bf16[1,128,896]{2,1,0:T(8,128)(2,1)S(1)} %bitcast.128), kind=kLoop, calls=%fused_computation.7 | loop fusion | flops 1376256 | bytes 1835008 | tf_op jit(solution)/shard_map/stack | solution.py:64
  88.3 1.3 shard_map.131.refs_1_
  90.2 1.6 fusion.15
  91.7 1.8 collective-permute-start.22
  93.5 2.9 %collective-permute-start.24 = (bf16[512,256]{1,0:T(8,128)(2,1)S(1)}, bf16[512,256]{1,0:T(8,128)(2,1)S(1)}, u32[]{:S(2)}, u32[]{:S(2)}) collective-permute-start(bf16[512,256]{1,0:T(8,128)(2,1)S(1)} %get-tuple-element.64), channel_id=1, source_target_pairs={{0,6},{1,7},{2,0},{3,1},{4,2},{5,3},{6,4},{7,5},{8,14},{9,15},{10,... | collective-permute-start | bytes 786440 | tf_op jit(solution)/shard_map/ppermute | solution.py:33
  96.4 4.3 %shard_map.133.kv_ref = bf16[2,8,16,16,256]{4,3,2,1,0:T(8,128)(2,1)S(1)} custom-call(bf16[4,128,896]{2,1,0:T(8,128)(2,1)} %pad_maximum_fusion.5.refs_0_, bf16[4,128,896]{2,1,0:T(8,128)(2,1)} %pad_maximum_fusion.4.refs_1_, bf16[4,128,896]{2,1,0:T(8,128)(2,1)} %collective-permute-done.25.refs_2_, bf16[4,128,896]{2,1,0:T(8,128)(2,1)} %collective-permute-done.26.refs_3_, ...), custom_call_target="tpu_custom_call" | custom-call | flops 1879048192 | bytes 3670016 | tf_op jit(solution)/shard_map/pallas_call | solution.py:290
  100.9 3.5 %collective-permute-start.21 = (bf16[512,256]{1,0:T(8,128)(2,1)S(1)}, bf16[512,256]{1,0:T(8,128)(2,1)S(1)}, u32[]{:S(2)}, u32[]{:S(2)}) collective-permute-start(bf16[512,256]{1,0:T(8,128)(2,1)S(1)} %get-tuple-element.67), channel_id=1, source_target_pairs={{0,6},{1,7},{2,0},{3,1},{4,2},{5,3},{6,4},{7,5},{8,14},{9,15},{10,... | collective-permute-start | bytes 786440 | tf_op jit(solution)/shard_map/ppermute | solution.py:33
  104.4 1.3 fusion.9
  105.7 3.2 %collective-permute-start.27 = (bf16[512,256]{1,0:T(8,128)(2,1)S(1)}, bf16[512,256]{1,0:T(8,128)(2,1)S(1)}, u32[]{:S(2)}, u32[]{:S(2)}) collective-permute-start(bf16[512,256]{1,0:T(8,128)(2,1)S(1)} %get-tuple-element.63), channel_id=1, source_target_pairs={{0,4},{1,5},{2,6},{3,7},{4,0},{5,1},{6,2},{7,3},{8,12},{9,13},{10,... | collective-permute-start | bytes 786440 | tf_op jit(solution)/shard_map/ppermute | solution.py:33
  108.8 1.8 %collective-permute-start.28 = (bf16[512,256]{1,0:T(8,128)(2,1)S(1)}, bf16[512,256]{1,0:T(8,128)(2,1)S(1)}, u32[]{:S(2)}, u32[]{:S(2)}) collective-permute-start(bf16[512,256]{1,0:T(8,128)(2,1)S(1)} %get-tuple-element.62), channel_id=1, source_target_pairs={{0,8},{1,9},{2,10},{3,11},{4,12},{5,13},{6,14},{7,15},{8,0},{9,1},... | collective-permute-start | bytes 786440 | tf_op jit(solution)/shard_map/ppermute | solution.py:33
  111.3 6.0 %collective-permute-done.27.refs_5_ = bf16[512,256]{1,0:T(8,128)(2,1)S(1)} collective-permute-done((bf16[512,256]{1,0:T(8,128)(2,1)S(1)}, bf16[512,256]{1,0:T(8,128)(2,1)S(1)}, u32[]{:S(2)}, u32[]{:S(2)}) %collective-permute-start.27) | collective-permute-done | bytes 262176 | tf_op jit(solution)/shard_map/ppermute | solution.py:33
  117.3 2.0 %shard_map.134 = (bf16[512,256]{1,0:T(8,128)(2,1)S(1)}, bf16[528,256]{1,0:T(8,128)(2,1)S(1)}) custom-call(s32[1]{0:T(128)} %bitcast.ids_ref, f32[16,1,256]{2,1,0:T(1,128)S(1)} %bitcast.121, bf16[512,256]{1,0:T(8,128)(2,1)S(1)} %bitcast.116, bf16[8,512,256]{2,1,0:T(8,128)(2,1)S(1)} %shard_map.131.refs_1_, ...), custom_call_target="tpu_custom_call" | custom-call | tf_op jit(solution)/shard_map/pallas_call | solution.py:133
  119.3 1.9 %collective-permute-start.31 = (bf16[528,256]{1,0:T(8,128)(2,1)S(1)}, bf16[528,256]{1,0:T(8,128)(2,1)S(1)}, u32[]{:S(2)}, u32[]{:S(2)}) collective-permute-start(bf16[528,256]{1,0:T(8,128)(2,1)S(1)} %get-tuple-element.47), channel_id=1, source_target_pairs={{0,8},{1,9},{2,10},{3,11},{4,12},{5,13},{6,14},{7,15},{8,0},{9,1},... | collective-permute-start | bytes 811016 | tf_op jit(solution)/shard_map/ppermute | solution.py:33
  121.3 3.0 %collective-permute-start.32 = (bf16[528,256]{1,0:T(8,128)(2,1)S(1)}, bf16[528,256]{1,0:T(8,128)(2,1)S(1)}, u32[]{:S(2)}, u32[]{:S(2)}) collective-permute-start(bf16[528,256]{1,0:T(8,128)(2,1)S(1)} %get-tuple-element.47), channel_id=1, source_target_pairs={{0,4},{1,5},{2,6},{3,7},{4,0},{5,1},{6,2},{7,3},{8,12},{9,13},{10,... | collective-permute-start | bytes 811016 | tf_op jit(solution)/shard_map/ppermute | solution.py:33
  124.2 1.3 collective-permute-start.33
  125.6 2.0 %collective-permute-start.30 = (bf16[528,256]{1,0:T(8,128)(2,1)S(1)}, bf16[528,256]{1,0:T(8,128)(2,1)S(1)}, u32[]{:S(2)}, u32[]{:S(2)}) collective-permute-start(bf16[528,256]{1,0:T(8,128)(2,1)S(1)} %get-tuple-element.47), channel_id=1, source_target_pairs={{0,6},{1,7},{2,0},{3,1},{4,2},{5,3},{6,4},{7,5},{8,14},{9,15},{10,... | collective-permute-start | bytes 811016 | tf_op jit(solution)/shard_map/ppermute | solution.py:33
  127.7 1.8 collective-permute-done.33.earlier_ref
  129.4 2.8 %collective-permute-done.32 = bf16[528,256]{1,0:T(8,128)(2,1)S(1)} collective-permute-done((bf16[528,256]{1,0:T(8,128)(2,1)S(1)}, bf16[528,256]{1,0:T(8,128)(2,1)S(1)}, u32[]{:S(2)}, u32[]{:S(2)}) %collective-permute-start.32) | collective-permute-done | bytes 270368 | tf_op jit(solution)/shard_map/ppermute | solution.py:33
  134.2 1.7 collective-permute-start.36
  136.9 2.7 %collective-permute-done.34 = bf16[528,256]{1,0:T(8,128)(2,1)S(1)} collective-permute-done((bf16[528,256]{1,0:T(8,128)(2,1)S(1)}, bf16[528,256]{1,0:T(8,128)(2,1)S(1)}, u32[]{:S(2)}, u32[]{:S(2)}) %collective-permute-start.34) | collective-permute-done | bytes 270368 | tf_op jit(solution)/shard_map/ppermute | solution.py:33
  139.6 1.3 collective-permute-done.35
  140.9 1.3 collective-permute-done.36
  142.4 2.7 %collective-permute-done.38.refs_3_ = bf16[4,528,256]{2,1,0:T(8,128)(2,1)S(1)} collective-permute-done((bf16[4,528,256]{2,1,0:T(8,128)(2,1)S(1)}, bf16[4,528,256]{2,1,0:T(8,128)(2,1)S(1)}, u32[]{:S(2)}, u32[]{:S(2)}) %collective-permute-start.38) | collective-permute-done | bytes 1081376 | tf_op jit(solution)/shard_map/ppermute | solution.py:33
  145.1 1.8 shard_map.135
  148.5 1.3 shard_map.138
  150.0 1.3 shard_map.137
  151.3 2.7 %collective-permute-done.39 = bf16[8,512,256]{2,1,0:T(8,128)(2,1)S(1)} collective-permute-done((bf16[8,512,256]{2,1,0:T(8,128)(2,1)S(1)}, bf16[8,512,256]{2,1,0:T(8,128)(2,1)S(1)}, u32[]{:S(2)}, u32[]{:S(2)}) %collective-permute-start.39) | collective-permute-done | bytes 2097184 | tf_op jit(solution)/shard_map/ppermute | solution.py:33
  154.4 1.8 collective-permute-start.42
  156.2 1.5 collective-permute-start.43
  159.7 2.0 %collective-permute-start.41 = (bf16[512,256]{1,0:T(8,128)(2,1)S(1)}, bf16[512,256]{1,0:T(8,128)(2,1)S(1)}, u32[]{:S(2)}, u32[]{:S(2)}) collective-permute-start(bf16[512,256]{1,0:T(8,128)(2,1)S(1)} %get-tuple-element.59), channel_id=1, source_target_pairs={{0,6},{1,7},{2,0},{3,1},{4,2},{5,3},{6,4},{7,5},{8,14},{9,15},{10,... | collective-permute-start | bytes 786440 | tf_op jit(solution)/shard_map/ppermute | solution.py:33
  161.7 2.6 %collective-permute-done.42 = bf16[512,256]{1,0:T(8,128)(2,1)S(1)} collective-permute-done((bf16[512,256]{1,0:T(8,128)(2,1)S(1)}, bf16[512,256]{1,0:T(8,128)(2,1)S(1)}, u32[]{:S(2)}, u32[]{:S(2)}) %collective-permute-start.42) | collective-permute-done | bytes 262176 | tf_op jit(solution)/shard_map/ppermute | solution.py:33
  164.3 1.3 collective-permute-done.43
  167.1 4.2 %collective-permute-start.45 = (bf16[512,256]{1,0:T(8,128)(2,1)S(1)}, bf16[512,256]{1,0:T(8,128)(2,1)S(1)}, u32[]{:S(2)}, u32[]{:S(2)}) collective-permute-start(bf16[512,256]{1,0:T(8,128)(2,1)S(1)} %get-tuple-element.60), channel_id=1, source_target_pairs={{0,4},{1,5},{2,6},{3,7},{4,0},{5,1},{6,2},{7,3},{8,12},{9,13},{10,... | collective-permute-start | bytes 786440 | tf_op jit(solution)/shard_map/ppermute | solution.py:33
  171.3 1.8 %collective-permute-start.46 = (bf16[512,256]{1,0:T(8,128)(2,1)S(1)}, bf16[512,256]{1,0:T(8,128)(2,1)S(1)}, u32[]{:S(2)}, u32[]{:S(2)}) collective-permute-start(bf16[512,256]{1,0:T(8,128)(2,1)S(1)} %get-tuple-element.61), channel_id=1, source_target_pairs={{0,8},{1,9},{2,10},{3,11},{4,12},{5,13},{6,14},{7,15},{8,0},{9,1},... | collective-permute-start | bytes 786440 | tf_op jit(solution)/shard_map/ppermute | solution.py:33
  173.2 5.0 %collective-permute-done.45 = bf16[512,256]{1,0:T(8,128)(2,1)S(1)} collective-permute-done((bf16[512,256]{1,0:T(8,128)(2,1)S(1)}, bf16[512,256]{1,0:T(8,128)(2,1)S(1)}, u32[]{:S(2)}, u32[]{:S(2)}) %collective-permute-start.45) | collective-permute-done | bytes 262176 | tf_op jit(solution)/shard_map/ppermute | solution.py:33
  (111 shorter events, 20.4 us)
Async XLA Ops:
  0.0 12.1 %copy-start = (bf16[64,8,896]{2,1,0:T(8,128)(2,1)S(1)}, bf16[64,8,896]{2,1,0:T(8,128)(2,1)}, u32[]{:S(2)}) copy-start(bf16[64,8,896]{2,1,0:T(8,128)(2,1)} %param.23) | copy-start | bytes 2752516
  0.0 1.0 copy-start.7
  2.5 16.6 %collective-permute-start.2 = (bf16[528,256]{1,0:T(8,128)(2,1)S(1)}, bf16[528,256]{1,0:T(8,128)(2,1)S(1)}, u32[]{:S(2)}, u32[]{:S(2)}) collective-permute-start(bf16[528,256]{1,0:T(8,128)(2,1)S(1)} %get-tuple-element.30), channel_id=1, source_target_pairs={{0,8},{1,9},{2,10},{3,11},{4,12},{5,13},{6,14},{7,15},{8,0},{9,1},... | collective-permute-start | bytes 811016 | tf_op jit(solution)/shard_map/ppermute | solution.py:33
  5.7 13.4 %collective-permute-start.3 = (bf16[528,256]{1,0:T(8,128)(2,1)S(1)}, bf16[528,256]{1,0:T(8,128)(2,1)S(1)}, u32[]{:S(2)}, u32[]{:S(2)}) collective-permute-start(bf16[528,256]{1,0:T(8,128)(2,1)S(1)} %get-tuple-element.30), channel_id=1, source_target_pairs={{0,4},{1,5},{2,6},{3,7},{4,0},{5,1},{6,2},{7,3},{8,12},{9,13},{10,... | collective-permute-start | bytes 811016 | tf_op jit(solution)/shard_map/ppermute | solution.py:33
  7.8 16.0 %collective-permute-start = (bf16[528,256]{1,0:T(8,128)(2,1)S(1)}, bf16[528,256]{1,0:T(8,128)(2,1)S(1)}, u32[]{:S(2)}, u32[]{:S(2)}) collective-permute-start(bf16[528,256]{1,0:T(8,128)(2,1)S(1)} %get-tuple-element.30), channel_id=1, source_target_pairs={{0,2},{1,3},{2,4},{3,5},{4,6},{5,7},{6,0},{7,1},{8,10},{9,11},{10,... | collective-permute-start | bytes 811016 | tf_op jit(solution)/shard_map/ppermute | solution.py:33
  7.8 16.0 %collective-permute-start.1 = (bf16[528,256]{1,0:T(8,128)(2,1)S(1)}, bf16[528,256]{1,0:T(8,128)(2,1)}, u32[]{:S(2)}, u32[]{:S(2)}) collective-permute-start(bf16[528,256]{1,0:T(8,128)(2,1)S(1)} %get-tuple-element.30), channel_id=1, source_target_pairs={{0,6},{1,7},{2,0},{3,1},{4,2},{5,3},{6,4},{7,5},{8,14},{9,15},{10,... | collective-permute-start | bytes 811016 | tf_op jit(solution)/shard_map/ppermute | solution.py:33
  13.5 14.1 %all-to-all-start = ((bf16[8,4,8,896]{3,2,1,0:T(8,128)(2,1)}), bf16[8,4,8,896]{3,2,1,0:T(8,128)(2,1)S(1)}, u32[]{:S(2)}, u32[]{:S(2)}) async-start(bf16[8,4,8,896]{3,2,1,0:T(8,128)(2,1)} %bitcast.23), calls=%async_computation | async-start | bytes 917504 | tf_op jit(solution)/shard_map/all_to_all | solution.py:386
  19.1 12.0 %copy-start.12 = (bf16[528,256]{1,0:T(8,128)(2,1)}, bf16[528,256]{1,0:T(8,128)(2,1)S(1)}, u32[]{:S(2)}) copy-start(bf16[528,256]{1,0:T(8,128)(2,1)S(1)} %collective-permute-done.3) | copy-start | bytes 811012
  19.1 9.0 %collective-permute-start.4 = (bf16[528,256]{1,0:T(8,128)(2,1)S(1)}, bf16[528,256]{1,0:T(8,128)(2,1)}, u32[]{:S(2)}, u32[]{:S(2)}) collective-permute-start(bf16[528,256]{1,0:T(8,128)(2,1)S(1)} %collective-permute-done.2), channel_id=1, source_target_pairs={{0,2},{1,3},{2,4},{3,5},{4,6},{5,7},{6,0},{7,1},{8,10},{9,11},{10,... | collective-permute-start | bytes 811016 | tf_op jit(solution)/shard_map/ppermute | solution.py:33
  19.2 8.9 %collective-permute-start.5 = (bf16[528,256]{1,0:T(8,128)(2,1)S(1)}, bf16[528,256]{1,0:T(8,128)(2,1)}, u32[]{:S(2)}, u32[]{:S(2)}) collective-permute-start(bf16[528,256]{1,0:T(8,128)(2,1)S(1)} %collective-permute-done.2), channel_id=1, source_target_pairs={{0,6},{1,7},{2,0},{3,1},{4,2},{5,3},{6,4},{7,5},{8,14},{9,15},{10,... | collective-permute-start | bytes 811016 | tf_op jit(solution)/shard_map/ppermute | solution.py:33
  21.9 9.2 %collective-permute-start.6 = (bf16[528,256]{1,0:T(8,128)(2,1)S(1)}, bf16[528,256]{1,0:T(8,128)(2,1)}, u32[]{:S(2)}, u32[]{:S(2)}) collective-permute-start(bf16[528,256]{1,0:T(8,128)(2,1)S(1)} %collective-permute-done.3), channel_id=1, source_target_pairs={{0,8},{1,9},{2,10},{3,11},{4,12},{5,13},{6,14},{7,15},{8,0},{9,1},... | collective-permute-start | bytes 811016 | tf_op jit(solution)/shard_map/ppermute | solution.py:33
  24.9 7.9 %collective-permute-start.7 = (bf16[4,528,256]{2,1,0:T(8,128)(2,1)S(1)}, bf16[4,528,256]{2,1,0:T(8,128)(2,1)}, u32[]{:S(2)}, u32[]{:S(2)}) collective-permute-start(bf16[4,528,256]{2,1,0:T(8,128)(2,1)S(1)} %pad_maximum_fusion.refs_0_), channel_id=1, source_target_pairs={{0,1},{1,0},{2,3},{3,2},{4,5},{5,4},{6,7},{7,6},{8,9},{9,8},{10,11... | collective-permute-start | bytes 3244040 | tf_op jit(solution)/shard_map/ppermute | solution.py:33
  32.5 2.9 %collective-permute-start.8 = (bf16[4,528,256]{2,1,0:T(8,128)(2,1)S(1)}, bf16[4,528,256]{2,1,0:T(8,128)(2,1)}, u32[]{:S(2)}, u32[]{:S(2)}) collective-permute-start(bf16[4,528,256]{2,1,0:T(8,128)(2,1)S(1)} %pad_maximum_fusion.1.refs_1_), channel_id=1, source_target_pairs={{0,1},{1,0},{2,3},{3,2},{4,5},{5,4},{6,7},{7,6},{8,9},{9,8},{10,11... | collective-permute-start | bytes 3244040 | tf_op jit(solution)/shard_map/ppermute | solution.py:33
  35.4 1.6 copy-start.3
  37.0 1.6 copy-start.4
  43.3 17.6 %collective-permute-start.17 = (bf16[2,512,256]{2,1,0:T(8,128)(2,1)}, bf16[2,512,256]{2,1,0:T(8,128)(2,1)}, u32[]{:S(2)}, u32[]{:S(2)}) collective-permute-start(bf16[2,512,256]{2,1,0:T(8,128)(2,1)} %shard_map.128.own_ref), channel_id=1, source_target_pairs={{0,48},{16,0},{1,49},{17,1},{2,50},{18,2},{3,51},{19,3},{4,52},{20... | collective-permute-start | bytes 1572872 | tf_op jit(solution)/shard_map/ppermute | solution.py:391
  48.1 10.2 %collective-permute-start.10 = (bf16[128,896]{1,0:T(8,128)(2,1)S(1)}, bf16[128,896]{1,0:T(8,128)(2,1)}, u32[]{:S(2)}, u32[]{:S(2)}) collective-permute-start(bf16[128,896]{1,0:T(8,128)(2,1)S(1)} %bitcast.124), channel_id=1, source_target_pairs={{0,4},{1,5},{2,6},{3,7},{4,0},{5,1},{6,2},{7,3},{8,12},{9,13},{10,... | collective-permute-start | bytes 688136 | tf_op jit(solution)/shard_map/ppermute | solution.py:33
  50.0 16.4 %collective-permute-start.11 = (bf16[128,896]{1,0:T(8,128)(2,1)S(1)}, bf16[128,896]{1,0:T(8,128)(2,1)S(1)}, u32[]{:S(2)}, u32[]{:S(2)}) collective-permute-start(bf16[128,896]{1,0:T(8,128)(2,1)S(1)} %bitcast.125), channel_id=1, source_target_pairs={{0,2},{1,3},{2,4},{3,5},{4,6},{5,7},{6,0},{7,1},{8,10},{9,11},{10,... | collective-permute-start | bytes 688136 | tf_op jit(solution)/shard_map/ppermute | solution.py:33
  52.3 14.0 %collective-permute-start.12 = (bf16[128,896]{1,0:T(8,128)(2,1)S(1)}, bf16[128,896]{1,0:T(8,128)(2,1)S(1)}, u32[]{:S(2)}, u32[]{:S(2)}) collective-permute-start(bf16[128,896]{1,0:T(8,128)(2,1)S(1)} %bitcast.126), channel_id=1, source_target_pairs={{0,6},{1,7},{2,0},{3,1},{4,2},{5,3},{6,4},{7,5},{8,14},{9,15},{10,... | collective-permute-start | bytes 688136 | tf_op jit(solution)/shard_map/ppermute | solution.py:33
  52.3 14.0 %collective-permute-start.9 = (bf16[128,896]{1,0:T(8,128)(2,1)S(1)}, bf16[128,896]{1,0:T(8,128)(2,1)}, u32[]{:S(2)}, u32[]{:S(2)}) collective-permute-start(bf16[128,896]{1,0:T(8,128)(2,1)S(1)} %bitcast.127), channel_id=1, source_target_pairs={{0,8},{1,9},{2,10},{3,11},{4,12},{5,13},{6,14},{7,15},{8,0},{9,1},... | collective-permute-start | bytes 688136 | tf_op jit(solution)/shard_map/ppermute | solution.py:33
  58.4 21.3 %collective-permute-start.16 = (bf16[2,512,256]{2,1,0:T(8,128)(2,1)}, bf16[2,512,256]{2,1,0:T(8,128)(2,1)}, u32[]{:S(2)}, u32[]{:S(2)}) collective-permute-start(bf16[2,512,256]{2,1,0:T(8,128)(2,1)} %shard_map.128.own_ref), channel_id=1, source_target_pairs={{0,16},{16,32},{32,48},{1,17},{17,33},{33,49},{2,18},{18,34},{34,5... | collective-permute-start | bytes 1572872 | tf_op jit(solution)/shard_map/ppermute | solution.py:391
  60.8 18.8 %collective-permute-start.18 = (bf16[2,512,256]{2,1,0:T(8,128)(2,1)}, bf16[2,512,256]{2,1,0:T(8,128)(2,1)}, u32[]{:S(2)}, u32[]{:S(2)}) collective-permute-start(bf16[2,512,256]{2,1,0:T(8,128)(2,1)} %collective-permute-done.17.b3_ref), channel_id=1, source_target_pairs={{48,32},{0,48},{49,33},{1,49},{50,34},{2,50},{51,35},{3,51},{52,36... | collective-permute-start | bytes 1572872 | tf_op jit(solution)/shard_map/ppermute | solution.py:391
  66.3 2.8 %copy-start.13 = (bf16[128,896]{1,0:T(8,128)(2,1)}, bf16[128,896]{1,0:T(8,128)(2,1)S(1)}, u32[]{:S(2)}) copy-start(bf16[128,896]{1,0:T(8,128)(2,1)S(1)} %collective-permute-done.11) | copy-start | bytes 688132
  66.3 2.8 %copy-start.15 = (bf16[128,896]{1,0:T(8,128)(2,1)}, bf16[128,896]{1,0:T(8,128)(2,1)S(1)}, u32[]{:S(2)}) copy-start(bf16[128,896]{1,0:T(8,128)(2,1)S(1)} %collective-permute-done.12) | copy-start | bytes 688132
  66.4 9.0 %collective-permute-start.13 = (bf16[128,896]{1,0:T(8,128)(2,1)}, bf16[128,896]{1,0:T(8,128)(2,1)}, u32[]{:S(2)}, u32[]{:S(2)}) collective-permute-start(bf16[128,896]{1,0:T(8,128)(2,1)} %collective-permute-done.9), channel_id=1, source_target_pairs={{0,2},{1,3},{2,4},{3,5},{4,6},{5,7},{6,0},{7,1},{8,10},{9,11},{10,... | collective-permute-start | bytes 688136 | tf_op jit(solution)/shard_map/ppermute | solution.py:33
  66.6 8.7 %collective-permute-start.14 = (bf16[128,896]{1,0:T(8,128)(2,1)}, bf16[128,896]{1,0:T(8,128)(2,1)}, u32[]{:S(2)}, u32[]{:S(2)}) collective-permute-start(bf16[128,896]{1,0:T(8,128)(2,1)} %collective-permute-done.9), channel_id=1, source_target_pairs={{0,6},{1,7},{2,0},{3,1},{4,2},{5,3},{6,4},{7,5},{8,14},{9,15},{10,... | collective-permute-start | bytes 688136 | tf_op jit(solution)/shard_map/ppermute | solution.py:33
  69.2 8.1 %collective-permute-start.15 = (bf16[128,896]{1,0:T(8,128)(2,1)}, bf16[128,896]{1,0:T(8,128)(2,1)}, u32[]{:S(2)}, u32[]{:S(2)}) collective-permute-start(bf16[128,896]{1,0:T(8,128)(2,1)} %collective-permute-done.10), channel_id=1, source_target_pairs={{0,8},{1,9},{2,10},{3,11},{4,12},{5,13},{6,14},{7,15},{8,0},{9,1},... | collective-permute-start | bytes 688136 | tf_op jit(solution)/shard_map/ppermute | solution.py:33
  70.9 1.6 copy-start.5
  79.6 3.4 %copy-start.1 = (bf16[256,4096]{1,0:T(8,128)(2,1)S(1)}, bf16[256,4096]{1,0:T(8,128)(2,1)}, u32[]{:S(2)}) copy-start(bf16[256,4096]{1,0:T(8,128)(2,1)} %w_ref.5) | copy-start | bytes 6291460
  83.0 2.7 %copy-start.14 = (bf16[128,896]{1,0:T(8,128)(2,1)S(1)}, bf16[128,896]{1,0:T(8,128)(2,1)}, u32[]{:S(2)}) copy-start(bf16[128,896]{1,0:T(8,128)(2,1)} %copy-done.13) | copy-start | bytes 688132
  83.0 2.7 %copy-start.16 = (bf16[128,896]{1,0:T(8,128)(2,1)S(1)}, bf16[128,896]{1,0:T(8,128)(2,1)}, u32[]{:S(2)}) copy-start(bf16[128,896]{1,0:T(8,128)(2,1)} %copy-done.15) | copy-start | bytes 688132
  85.6 4.5 %collective-permute-start.19 = (bf16[8,512,256]{2,1,0:T(8,128)(2,1)}, bf16[8,512,256]{2,1,0:T(8,128)(2,1)}, u32[]{:S(2)}, u32[]{:S(2)}) collective-permute-start(bf16[8,512,256]{2,1,0:T(8,128)(2,1)} %shard_map.132), channel_id=1, source_target_pairs={{0,1},{1,0},{2,3},{3,2},{4,5},{5,4},{6,7},{7,6},{8,9},{9,8},{10,11... | collective-permute-start | bytes 6291464 | tf_op jit(solution)/shard_map/ppermute | solution.py:33
  87.7 8.8 %collective-permute-start.25 = (bf16[4,128,896]{2,1,0:T(8,128)(2,1)}, bf16[4,128,896]{2,1,0:T(8,128)(2,1)}, u32[]{:S(2)}, u32[]{:S(2)}) collective-permute-start(bf16[4,128,896]{2,1,0:T(8,128)(2,1)} %pad_maximum_fusion.5.refs_0_), channel_id=1, source_target_pairs={{0,1},{1,0},{2,3},{3,2},{4,5},{5,4},{6,7},{7,6},{8,9},{9,8},{10,11... | collective-permute-start | bytes 2752520 | tf_op jit(solution)/shard_map/ppermute | solution.py:33
  88.2 8.3 %collective-permute-start.26 = (bf16[4,128,896]{2,1,0:T(8,128)(2,1)}, bf16[4,128,896]{2,1,0:T(8,128)(2,1)}, u32[]{:S(2)}, u32[]{:S(2)}) collective-permute-start(bf16[4,128,896]{2,1,0:T(8,128)(2,1)} %pad_maximum_fusion.4.refs_1_), channel_id=1, source_target_pairs={{0,1},{1,0},{2,3},{3,2},{4,5},{5,4},{6,7},{7,6},{8,9},{9,8},{10,11... | collective-permute-start | bytes 2752520 | tf_op jit(solution)/shard_map/ppermute | solution.py:33
  89.5 6.9 %copy-start.11 = (bf16[2,896,256]{2,1,0:T(8,128)(2,1)S(1)}, bf16[2,896,256]{2,1,0:T(8,128)(2,1)}, u32[]{:S(2)}) copy-start(bf16[2,896,256]{2,1,0:T(8,128)(2,1)} %refs_4_.6) | copy-start | bytes 2752516
  91.7 12.7 %collective-permute-start.22 = (bf16[512,256]{1,0:T(8,128)(2,1)S(1)}, bf16[512,256]{1,0:T(8,128)(2,1)S(1)}, u32[]{:S(2)}, u32[]{:S(2)}) collective-permute-start(bf16[512,256]{1,0:T(8,128)(2,1)S(1)} %get-tuple-element.66), channel_id=1, source_target_pairs={{0,8},{1,9},{2,10},{3,11},{4,12},{5,13},{6,14},{7,15},{8,0},{9,1},... | collective-permute-start | bytes 786440 | tf_op jit(solution)/shard_map/ppermute | solution.py:33
  93.5 10.9 %collective-permute-start.23 = (bf16[512,256]{1,0:T(8,128)(2,1)S(1)}, bf16[512,256]{1,0:T(8,128)(2,1)S(1)}, u32[]{:S(2)}, u32[]{:S(2)}) collective-permute-start(bf16[512,256]{1,0:T(8,128)(2,1)S(1)} %get-tuple-element.65), channel_id=1, source_target_pairs={{0,2},{1,3},{2,4},{3,5},{4,6},{5,7},{6,0},{7,1},{8,10},{9,11},{10,... | collective-permute-start | bytes 786440 | tf_op jit(solution)/shard_map/ppermute | solution.py:33
  93.5 10.9 %collective-permute-start.24 = (bf16[512,256]{1,0:T(8,128)(2,1)S(1)}, bf16[512,256]{1,0:T(8,128)(2,1)S(1)}, u32[]{:S(2)}, u32[]{:S(2)}) collective-permute-start(bf16[512,256]{1,0:T(8,128)(2,1)S(1)} %get-tuple-element.64), channel_id=1, source_target_pairs={{0,6},{1,7},{2,0},{3,1},{4,2},{5,3},{6,4},{7,5},{8,14},{9,15},{10,... | collective-permute-start | bytes 786440 | tf_op jit(solution)/shard_map/ppermute | solution.py:33
  100.8 10.5 %collective-permute-start.20 = (bf16[512,256]{1,0:T(8,128)(2,1)S(1)}, bf16[512,256]{1,0:T(8,128)(2,1)S(1)}, u32[]{:S(2)}, u32[]{:S(2)}) collective-permute-start(bf16[512,256]{1,0:T(8,128)(2,1)S(1)} %get-tuple-element.68), channel_id=1, source_target_pairs={{0,2},{1,3},{2,4},{3,5},{4,6},{5,7},{6,0},{7,1},{8,10},{9,11},{10,... | collective-permute-start | bytes 786440 | tf_op jit(solution)/shard_map/ppermute | solution.py:33
  100.9 16.4 %copy-start.8 = (bf16[1,512,256]{2,1,0:T(8,128)(2,1)S(1)}, bf16[1,512,256]{2,1,0:T(8,128)(2,1)}, u32[]{:S(2)}) copy-start(bf16[1,512,256]{2,1,0:T(8,128)(2,1)} %param.13) | copy-start | bytes 786436
  100.9 16.4 %copy-start.9 = (f32[4096]{0:T(1024)S(1)}, f32[4096]{0:T(1024)}, u32[]{:S(2)}) copy-start(f32[4096]{0:T(1024)} %param.15) | copy-start | bytes 49156
  100.9 10.4 %collective-permute-start.21 = (bf16[512,256]{1,0:T(8,128)(2,1)S(1)}, bf16[512,256]{1,0:T(8,128)(2,1)S(1)}, u32[]{:S(2)}, u32[]{:S(2)}) collective-permute-start(bf16[512,256]{1,0:T(8,128)(2,1)S(1)} %get-tuple-element.67), channel_id=1, source_target_pairs={{0,6},{1,7},{2,0},{3,1},{4,2},{5,3},{6,4},{7,5},{8,14},{9,15},{10,... | collective-permute-start | bytes 786440 | tf_op jit(solution)/shard_map/ppermute | solution.py:33
  105.7 11.6 %collective-permute-start.27 = (bf16[512,256]{1,0:T(8,128)(2,1)S(1)}, bf16[512,256]{1,0:T(8,128)(2,1)S(1)}, u32[]{:S(2)}, u32[]{:S(2)}) collective-permute-start(bf16[512,256]{1,0:T(8,128)(2,1)S(1)} %get-tuple-element.63), channel_id=1, source_target_pairs={{0,4},{1,5},{2,6},{3,7},{4,0},{5,1},{6,2},{7,3},{8,12},{9,13},{10,... | collective-permute-start | bytes 786440 | tf_op jit(solution)/shard_map/ppermute | solution.py:33
  108.8 8.4 %collective-permute-start.28 = (bf16[512,256]{1,0:T(8,128)(2,1)S(1)}, bf16[512,256]{1,0:T(8,128)(2,1)S(1)}, u32[]{:S(2)}, u32[]{:S(2)}) collective-permute-start(bf16[512,256]{1,0:T(8,128)(2,1)S(1)} %get-tuple-element.62), channel_id=1, source_target_pairs={{0,8},{1,9},{2,10},{3,11},{4,12},{5,13},{6,14},{7,15},{8,0},{9,1},... | collective-permute-start | bytes 786440 | tf_op jit(solution)/shard_map/ppermute | solution.py:33
  119.3 10.1 %collective-permute-start.31 = (bf16[528,256]{1,0:T(8,128)(2,1)S(1)}, bf16[528,256]{1,0:T(8,128)(2,1)S(1)}, u32[]{:S(2)}, u32[]{:S(2)}) collective-permute-start(bf16[528,256]{1,0:T(8,128)(2,1)S(1)} %get-tuple-element.47), channel_id=1, source_target_pairs={{0,8},{1,9},{2,10},{3,11},{4,12},{5,13},{6,14},{7,15},{8,0},{9,1},... | collective-permute-start | bytes 811016 | tf_op jit(solution)/shard_map/ppermute | solution.py:33
  121.3 10.9 %collective-permute-start.32 = (bf16[528,256]{1,0:T(8,128)(2,1)S(1)}, bf16[528,256]{1,0:T(8,128)(2,1)S(1)}, u32[]{:S(2)}, u32[]{:S(2)}) collective-permute-start(bf16[528,256]{1,0:T(8,128)(2,1)S(1)} %get-tuple-element.47), channel_id=1, source_target_pairs={{0,4},{1,5},{2,6},{3,7},{4,0},{5,1},{6,2},{7,3},{8,12},{9,13},{10,... | collective-permute-start | bytes 811016 | tf_op jit(solution)/shard_map/ppermute | solution.py:33
  124.2 5.2 %collective-permute-start.33 = (bf16[2,16,16,256]{3,2,1,0:T(8,128)(2,1)S(1)}, bf16[2,16,16,256]{3,2,1,0:T(8,128)(2,1)S(1)}, u32[]{:S(2)}, u32[]{:S(2)}) collective-permute-start(bf16[2,16,16,256]{3,2,1,0:T(8,128)(2,1)S(1)} %slice_bitcast_fusion.2), channel_id=1, source_target_pairs={{0,16},{16,32},{32,48},{1,17},{17,33},{33,49},{2,18},{18,34},{34,5... | collective-permute-start | bytes 786440 | tf_op jit(solution)/shard_map/ppermute | solution.py:391
  125.6 11.2 %collective-permute-start.29 = (bf16[528,256]{1,0:T(8,128)(2,1)S(1)}, bf16[528,256]{1,0:T(8,128)(2,1)S(1)}, u32[]{:S(2)}, u32[]{:S(2)}) collective-permute-start(bf16[528,256]{1,0:T(8,128)(2,1)S(1)} %get-tuple-element.47), channel_id=1, source_target_pairs={{0,2},{1,3},{2,4},{3,5},{4,6},{5,7},{6,0},{7,1},{8,10},{9,11},{10,... | collective-permute-start | bytes 811016 | tf_op jit(solution)/shard_map/ppermute | solution.py:33
  125.6 11.1 %collective-permute-start.30 = (bf16[528,256]{1,0:T(8,128)(2,1)S(1)}, bf16[528,256]{1,0:T(8,128)(2,1)S(1)}, u32[]{:S(2)}, u32[]{:S(2)}) collective-permute-start(bf16[528,256]{1,0:T(8,128)(2,1)S(1)} %get-tuple-element.47), channel_id=1, source_target_pairs={{0,6},{1,7},{2,0},{3,1},{4,2},{5,3},{6,4},{7,5},{8,14},{9,15},{10,... | collective-permute-start | bytes 811016 | tf_op jit(solution)/shard_map/ppermute | solution.py:33
  132.2 7.4 %collective-permute-start.34 = (bf16[528,256]{1,0:T(8,128)(2,1)S(1)}, bf16[528,256]{1,0:T(8,128)(2,1)S(1)}, u32[]{:S(2)}, u32[]{:S(2)}) collective-permute-start(bf16[528,256]{1,0:T(8,128)(2,1)S(1)} %collective-permute-done.31), channel_id=1, source_target_pairs={{0,2},{1,3},{2,4},{3,5},{4,6},{5,7},{6,0},{7,1},{8,10},{9,11},{10,... | collective-permute-start | bytes 811016 | tf_op jit(solution)/shard_map/ppermute | solution.py:33
  133.2 7.6 %collective-permute-start.35 = (bf16[528,256]{1,0:T(8,128)(2,1)S(1)}, bf16[528,256]{1,0:T(8,128)(2,1)S(1)}, u32[]{:S(2)}, u32[]{:S(2)}) collective-permute-start(bf16[528,256]{1,0:T(8,128)(2,1)S(1)} %collective-permute-done.31), channel_id=1, source_target_pairs={{0,6},{1,7},{2,0},{3,1},{4,2},{5,3},{6,4},{7,5},{8,14},{9,15},{10,... | collective-permute-start | bytes 811016 | tf_op jit(solution)/shard_map/ppermute | solution.py:33
  134.2 8.0 %collective-permute-start.36 = (bf16[528,256]{1,0:T(8,128)(2,1)S(1)}, bf16[528,256]{1,0:T(8,128)(2,1)S(1)}, u32[]{:S(2)}, u32[]{:S(2)}) collective-permute-start(bf16[528,256]{1,0:T(8,128)(2,1)S(1)} %collective-permute-done.32), channel_id=1, source_target_pairs={{0,8},{1,9},{2,10},{3,11},{4,12},{5,13},{6,14},{7,15},{8,0},{9,1},... | collective-permute-start | bytes 811016 | tf_op jit(solution)/shard_map/ppermute | solution.py:33
  136.9 5.6 %collective-permute-start.37 = (bf16[4,528,256]{2,1,0:T(8,128)(2,1)S(1)}, bf16[4,528,256]{2,1,0:T(8,128)(2,1)S(1)}, u32[]{:S(2)}, u32[]{:S(2)}) collective-permute-start(bf16[4,528,256]{2,1,0:T(8,128)(2,1)S(1)} %pad_maximum_fusion.2.refs_0_), channel_id=1, source_target_pairs={{0,1},{1,0},{2,3},{3,2},{4,5},{5,4},{6,7},{7,6},{8,9},{9,8},{10,11... | collective-permute-start | bytes 3244040 | tf_op jit(solution)/shard_map/ppermute | solution.py:33
  142.2 2.9 %copy-start.6 = (bf16[4096,256]{1,0:T(8,128)(2,1)S(1)}, bf16[4096,256]{1,0:T(8,128)(2,1)}, u32[]{:S(2)}) copy-start(bf16[4096,256]{1,0:T(8,128)(2,1)} %refs_4_.7) | copy-start | bytes 6291460
  142.3 2.8 %collective-permute-start.38 = (bf16[4,528,256]{2,1,0:T(8,128)(2,1)S(1)}, bf16[4,528,256]{2,1,0:T(8,128)(2,1)S(1)}, u32[]{:S(2)}, u32[]{:S(2)}) collective-permute-start(bf16[4,528,256]{2,1,0:T(8,128)(2,1)S(1)} %pad_maximum_fusion.3.refs_1_), channel_id=1, source_target_pairs={{0,1},{1,0},{2,3},{3,2},{4,5},{5,4},{6,7},{7,6},{8,9},{9,8},{10,11... | collective-permute-start | bytes 3244040 | tf_op jit(solution)/shard_map/ppermute | solution.py:33
  146.9 1.6 copy-start.2
  149.8 4.2 %collective-permute-start.39 = (bf16[8,512,256]{2,1,0:T(8,128)(2,1)S(1)}, bf16[8,512,256]{2,1,0:T(8,128)(2,1)S(1)}, u32[]{:S(2)}, u32[]{:S(2)}) collective-permute-start(bf16[8,512,256]{2,1,0:T(8,128)(2,1)S(1)} %shard_map.138), channel_id=1, source_target_pairs={{0,1},{1,0},{2,3},{3,2},{4,5},{5,4},{6,7},{7,6},{8,9},{9,8},{10,11... | collective-permute-start | bytes 6291464 | tf_op jit(solution)/shard_map/ppermute | solution.py:33
  154.4 9.9 %collective-permute-start.42 = (bf16[512,256]{1,0:T(8,128)(2,1)S(1)}, bf16[512,256]{1,0:T(8,128)(2,1)S(1)}, u32[]{:S(2)}, u32[]{:S(2)}) collective-permute-start(bf16[512,256]{1,0:T(8,128)(2,1)S(1)} %get-tuple-element.58), channel_id=1, source_target_pairs={{0,8},{1,9},{2,10},{3,11},{4,12},{5,13},{6,14},{7,15},{8,0},{9,1},... | collective-permute-start | bytes 786440 | tf_op jit(solution)/shard_map/ppermute | solution.py:33
  156.2 9.5 %collective-permute-start.43 = (bf16[512,256]{1,0:T(8,128)(2,1)S(1)}, bf16[512,256]{1,0:T(8,128)(2,1)S(1)}, u32[]{:S(2)}, u32[]{:S(2)}) collective-permute-start(bf16[512,256]{1,0:T(8,128)(2,1)S(1)} %get-tuple-element.57), channel_id=1, source_target_pairs={{0,2},{1,3},{2,4},{3,5},{4,6},{5,7},{6,0},{7,1},{8,10},{9,11},{10,... | collective-permute-start | bytes 786440 | tf_op jit(solution)/shard_map/ppermute | solution.py:33
  157.7 9.2 %collective-permute-start.44 = (bf16[512,256]{1,0:T(8,128)(2,1)S(1)}, bf16[512,256]{1,0:T(8,128)(2,1)S(1)}, u32[]{:S(2)}, u32[]{:S(2)}) collective-permute-start(bf16[512,256]{1,0:T(8,128)(2,1)S(1)} %get-tuple-element.56), channel_id=1, source_target_pairs={{0,6},{1,7},{2,0},{3,1},{4,2},{5,3},{6,4},{7,5},{8,14},{9,15},{10,... | collective-permute-start | bytes 786440 | tf_op jit(solution)/shard_map/ppermute | solution.py:33
  158.5 14.7 %collective-permute-start.40 = (bf16[512,256]{1,0:T(8,128)(2,1)S(1)}, bf16[512,256]{1,0:T(8,128)(2,1)S(1)}, u32[]{:S(2)}, u32[]{:S(2)}) collective-permute-start(bf16[512,256]{1,0:T(8,128)(2,1)S(1)} %get-tuple-element.55), channel_id=1, source_target_pairs={{0,2},{1,3},{2,4},{3,5},{4,6},{5,7},{6,0},{7,1},{8,10},{9,11},{10,... | collective-permute-start | bytes 786440 | tf_op jit(solution)/shard_map/ppermute | solution.py:33
  159.7 13.5 %collective-permute-start.41 = (bf16[512,256]{1,0:T(8,128)(2,1)S(1)}, bf16[512,256]{1,0:T(8,128)(2,1)S(1)}, u32[]{:S(2)}, u32[]{:S(2)}) collective-permute-start(bf16[512,256]{1,0:T(8,128)(2,1)S(1)} %get-tuple-element.59), channel_id=1, source_target_pairs={{0,6},{1,7},{2,0},{3,1},{4,2},{5,3},{6,4},{7,5},{8,14},{9,15},{10,... | collective-permute-start | bytes 786440 | tf_op jit(solution)/shard_map/ppermute | solution.py:33
  167.1 11.0 %collective-permute-start.45 = (bf16[512,256]{1,0:T(8,128)(2,1)S(1)}, bf16[512,256]{1,0:T(8,128)(2,1)S(1)}, u32[]{:S(2)}, u32[]{:S(2)}) collective-permute-start(bf16[512,256]{1,0:T(8,128)(2,1)S(1)} %get-tuple-element.60), channel_id=1, source_target_pairs={{0,4},{1,5},{2,6},{3,7},{4,0},{5,1},{6,2},{7,3},{8,12},{9,13},{10,... | collective-permute-start | bytes 786440 | tf_op jit(solution)/shard_map/ppermute | solution.py:33
  171.3 7.9 %collective-permute-start.46 = (bf16[512,256]{1,0:T(8,128)(2,1)S(1)}, bf16[512,256]{1,0:T(8,128)(2,1)S(1)}, u32[]{:S(2)}, u32[]{:S(2)}) collective-permute-start(bf16[512,256]{1,0:T(8,128)(2,1)S(1)} %get-tuple-element.61), channel_id=1, source_target_pairs={{0,8},{1,9},{2,10},{3,11},{4,12},{5,13},{6,14},{7,15},{8,0},{9,1},... | collective-permute-start | bytes 786440 | tf_op jit(solution)/shard_map/ppermute | solution.py:33
  (1 other events, 0.7 us)

commit v3 on v2

--- a/solution.py
+++ b/solution.py
@@ -13,7 +13,7 @@
 norm_eps = 1e-05
 mask_floor = -1e30
 
-CHIPS = ((0, 0), (0, -1), (0, 1), (1, 0), (0, 2), (1, -1), (1, 1), (1, 2))
+CHIPS = ((0, 0), (0, -1), (0, 1), (0, 2), (1, 0), (1, -1), (1, 1), (1, 2))
 
 
 def route(dy, dx, dc):
@@ -61,12 +61,12 @@
         (from_y, from_x2), during_first = tie(((from_y, from_x2), during_first))
     left_y, right_y = mp_send(from_y, TO_RIGHT), mp_send(from_y, TO_LEFT)
     y_x2 = mp_send(from_x2, TO_Y)
-    near = jnp.stack([shard, from_left, from_right, from_y])
+    near = jnp.stack([shard, from_left, from_right, from_x2])
     near_partner = mp_send(near, TO_CORE)
     if callable(during_second):
         during_second = during_second(during_first)
     far, during_second, _ = tie(
-        (jnp.stack([from_x2, left_y, right_y, y_x2]), during_second, corner(near))
+        (jnp.stack([from_y, left_y, right_y, y_x2]), during_second, corner(near))
     )
     return (near, far, near_partner, mp_send(far, TO_CORE)), during_first, during_second
 
@@ -78,7 +78,7 @@
         return mine[i].astype(jnp.float32) + partner[i].astype(jnp.float32)
 
     b16, f32 = jnp.bfloat16, jnp.float32
-    _, left, right, y, x2, y_left, y_right, y2 = range(8)
+    _, left, right, x2, y, y_left, y_right, y2 = range(8)
     far = mp_send(part(y2).astype(b16), TO_Y)
     from_left = mp_send(part(y_right).astype(b16), TO_RIGHT)
     from_right = mp_send(part(y_left).astype(b16), TO_LEFT)
@@ -179,6 +179,77 @@
         12,
         in_specs=[pl.BlockSpec(memory_space=pltpu.SMEM)] + [IN_VMEM] * (len(stacks) + count),
         out_specs=IN_VMEM,
+        out_shape=jax.ShapeDtypeStruct((count, rows, width), jnp.bfloat16),
+        cost_estimate=pl.CostEstimate(
+            flops=2 * rows * depth * width * count,
+            bytes_accessed=2 * (rows + width * count) * depth,
+            transcendentals=0,
+        ),
+    )(ids, *stacks, *weights)
+
+
+def halved_projection(ids, stacks, weights):
+    near, far, near_partner, far_partner = stacks
+    each, rows, feats = near.shape
+    rows = rows - STAT_ROWS
+    depth = 4 * each * feats
+    count = len(weights)
+    width = weights[0].shape[1]
+    lines = rows // feats
+
+    def kernel(ids_ref, near_ref, far_ref, near_partner_ref, far_partner_ref, *refs):
+        w_refs, out_ref, acc_ref = refs[:count], refs[count], refs[count + 1]
+        step = pl.program_id(0)
+
+        def product(first, second, at, w_ref):
+            x = jnp.concatenate([r[i, :rows] for r in (first, second) for i in range(each)], axis=1)
+            w = jnp.concatenate(
+                [
+                    w_ref[pl.ds(pl.multiple_of((ids_ref[k] % (2 * each)) * feats, feats), feats)]
+                    for part in (at, at + 2 * each)
+                    for k in range(part, part + each)
+                ]
+            )
+            return jnp.dot(x, w, preferred_element_type=jnp.float32)
+
+        @pl.when(step == 0)
+        def _():
+            for i, w_ref in enumerate(w_refs):
+                acc_ref[i] = product(near_ref, near_partner_ref, 0, w_ref)
+
+        @pl.when(step == 1)
+        def _():
+            stat = jnp.zeros((STAT_ROWS, feats), jnp.float32)
+            for x_ref in (near_ref, far_ref, near_partner_ref, far_partner_ref):
+                for i in range(each):
+                    stat = stat + x_ref[i, rows:].astype(jnp.float32)
+            stat = stat[:lines] + stat[lines : 2 * lines]
+            inv_line = lax.rsqrt(stat * (1.0 / depth) + norm_eps)
+            inv = jnp.concatenate(
+                [jnp.broadcast_to(inv_line[i : i + 1], (128, feats)).T for i in range(lines)]
+            )
+            inv = jnp.concatenate([inv] * (width // 128), axis=1)
+            for i, w_ref in enumerate(w_refs):
+                total = acc_ref[i] + product(far_ref, far_partner_ref, each, w_ref)
+                out_ref[i] = (total * inv).astype(jnp.bfloat16)
+
+    whole = pl.BlockSpec(near.shape, lambda g, ids: (0, 0, 0))
+    return call(
+        kernel,
+        48,
+        grid_spec=pltpu.PrefetchScalarGridSpec(
+            num_scalar_prefetch=1,
+            grid=(2,),
+            in_specs=[whole] * 4
+            + [
+                pl.BlockSpec(
+                    (2 * each * feats, width), lambda g, ids: ((ids[0] // (2 * each) + g) % 2, 0)
+                )
+            ]
+            * count,
+            out_specs=pl.BlockSpec((count, rows, width), lambda g, ids: (0, 0, 0)),
+            scratch_shapes=[pltpu.VMEM((count, rows, width), jnp.float32)],
+        ),
         out_shape=jax.ShapeDtypeStruct((count, rows, width), jnp.bfloat16),
         cost_estimate=pl.CostEstimate(
             flops=2 * rows * depth * width * count,
@@ -417,7 +488,7 @@
     picked = pick_neighbours(encoded, owners, slots)
     fetched = exchange_neighbours(*picked)
     stacks, _, fetched = gather_mp(shard, picked, fetched)
-    kv = normed_projection(ids, stacks, (w_key, w_value))
+    kv = halved_projection(ids, stacks, (w_key, w_value))
     kv, fetched = tie((kv, fetched))
     back1, back3 = send_kv(kv)
     queries = normed_projection(ids, stacks, (w_query,))[0]

time: 181 us -> 179 us (0.989)
  local copies, waits for them, and re-layouts: 11.3 us -> 8.11 us
    pallas_call x0 -> x1, Pallas kernels: none -> 6.11 us  [halved_projection(): call(kernel, 48, grid_spec=pltpu.PrefetchScalarGridSpec(num_scalar_prefet...]
    pallas_call x3 -> x2, Pallas kernels: 9.33 us -> 4.62 us  [normed_projection(): call(kernel, 12, in_specs=[pl.BlockSpec(memory_space=pltpu.SMEM)] + [IN_V...]
    unnamed x36 -> x32, local copies, waits for them, and re-layouts: 8.73 us -> 5.56 us
where the time goes in v3:
time: 179 us; the launch traced here: 178 us
  starting transfers between devices  80.4 us (45%)
  waiting for transfers between devices  48.7 us (27%)
  Pallas kernels  28.6 us (16%)
  other arithmetic  12.1 us (7%)
  local copies, waits for them, and re-layouts  8.11 us (5%)
    ppermute x43, starting transfers between devices, mp_send(): return lax.ppermute(block, 'mp', pairs)  60.8 us
    ppermute x43, waiting for transfers between devices, mp_send(): return lax.ppermute(block, 'mp', pairs)  44.4 us
    ppermute x4, starting transfers between devices, ctx_send(): return lax.ppermute(block, 'ctx', pairs)  14.2 us
    pallas_call x4, Pallas kernels, output_blocks(): call(kernel, 12, in_specs=[pl.BlockSpec(memory_space=pltpu.SMEM), IN_VMEM...  6.45 us
    pallas_call x1, Pallas kernels, halved_projection(): call(kernel, 48, grid_spec=pltpu.PrefetchScalarGridSpec(num_scalar_prefet...  6.11 us
    unnamed x32, local copies, waits for them, and re-layouts  5.56 us
    all_to_all x1, starting transfers between devices, exchange_neighbours(): lax.all_to_all(outgoing, ('pool', 'ctx'), split_axis=0, concat_axis=0, ti...  5.42 us
    pallas_call x2, Pallas kernels, normed_projection(): call(kernel, 12, in_specs=[pl.BlockSpec(memory_space=pltpu.SMEM)] + [IN_V...  4.62 us
  transfers between devices with their start and end apart: 48, of which 21 were waited for; matrix products, arithmetic and copies ran while one was open for 8% of the time, Pallas kernels for 5%

profile of v3, /device:TPU:2, one launch (start us, length us, event | category | flops | bytes accessed | tf_op | source)
XLA Modules:
  0.0 178.4 jit_solution(17564201926154017058)
XLA Ops:
  2.5 3.2 %collective-permute-start.2 = (bf16[528,256]{1,0:T(8,128)(2,1)S(1)}, bf16[528,256]{1,0:T(8,128)(2,1)S(1)}, u32[]{:S(2)}, u32[]{:S(2)}) collective-permute-start(bf16[528,256]{1,0:T(8,128)(2,1)S(1)} %get-tuple-element.30), channel_id=1, source_target_pairs={{0,8},{1,9},{2,10},{3,11},{4,12},{5,13},{6,14},{7,15},{8,0},{9,1},... | collective-permute-start | bytes 811016 | tf_op jit(solution)/shard_map/ppermute | solution.py:33
  5.7 2.1 %collective-permute-start.3 = (bf16[528,256]{1,0:T(8,128)(2,1)S(1)}, bf16[528,256]{1,0:T(8,128)(2,1)S(1)}, u32[]{:S(2)}, u32[]{:S(2)}) collective-permute-start(bf16[528,256]{1,0:T(8,128)(2,1)S(1)} %get-tuple-element.30), channel_id=1, source_target_pairs={{0,4},{1,5},{2,6},{3,7},{4,0},{5,1},{6,2},{7,3},{8,12},{9,13},{10,... | collective-permute-start | bytes 811016 | tf_op jit(solution)/shard_map/ppermute | solution.py:33
  7.8 2.0 %collective-permute-start.1 = (bf16[528,256]{1,0:T(8,128)(2,1)S(1)}, bf16[528,256]{1,0:T(8,128)(2,1)}, u32[]{:S(2)}, u32[]{:S(2)}) collective-permute-start(bf16[528,256]{1,0:T(8,128)(2,1)S(1)} %get-tuple-element.30), channel_id=1, source_target_pairs={{0,6},{1,7},{2,0},{3,1},{4,2},{5,3},{6,4},{7,5},{8,14},{9,15},{10,... | collective-permute-start | bytes 811016 | tf_op jit(solution)/shard_map/ppermute | solution.py:33
  12.1 1.4 gather_fusion
  13.5 5.4 %all-to-all-start = ((bf16[8,4,8,896]{3,2,1,0:T(8,128)(2,1)}), bf16[8,4,8,896]{3,2,1,0:T(8,128)(2,1)S(1)}, u32[]{:S(2)}, u32[]{:S(2)}) async-start(bf16[8,4,8,896]{3,2,1,0:T(8,128)(2,1)} %bitcast.23), calls=%async_computation | async-start | bytes 917504 | tf_op jit(solution)/shard_map/all_to_all | solution.py:457
  19.2 2.7 %collective-permute-start.5 = (bf16[528,256]{1,0:T(8,128)(2,1)S(1)}, bf16[528,256]{1,0:T(8,128)(2,1)}, u32[]{:S(2)}, u32[]{:S(2)}) collective-permute-start(bf16[528,256]{1,0:T(8,128)(2,1)S(1)} %collective-permute-done.2), channel_id=1, source_target_pairs={{0,6},{1,7},{2,0},{3,1},{4,2},{5,3},{6,4},{7,5},{8,14},{9,15},{10,... | collective-permute-start | bytes 811016 | tf_op jit(solution)/shard_map/ppermute | solution.py:33
  21.9 1.8 %collective-permute-start.6 = (bf16[528,256]{1,0:T(8,128)(2,1)S(1)}, bf16[528,256]{1,0:T(8,128)(2,1)}, u32[]{:S(2)}, u32[]{:S(2)}) collective-permute-start(bf16[528,256]{1,0:T(8,128)(2,1)S(1)} %collective-permute-done.3), channel_id=1, source_target_pairs={{0,8},{1,9},{2,10},{3,11},{4,12},{5,13},{6,14},{7,15},{8,0},{9,1},... | collective-permute-start | bytes 811016 | tf_op jit(solution)/shard_map/ppermute | solution.py:33
  25.0 2.6 %all-to-all-done = bf16[8,4,8,896]{3,2,1,0:T(8,128)(2,1)S(1)} async-done(((bf16[8,4,8,896]{3,2,1,0:T(8,128)(2,1)}), bf16[8,4,8,896]{3,2,1,0:T(8,128)(2,1)S(1)}, u32[]{:S(2)}, u32[]{:S(2)}) %all-to-all-start) | async-done | bytes 458784 | tf_op jit(solution)/shard_map/all_to_all | solution.py:457
  28.2 2.9 %collective-permute-done.6 = bf16[528,256]{1,0:T(8,128)(2,1)} collective-permute-done((bf16[528,256]{1,0:T(8,128)(2,1)S(1)}, bf16[528,256]{1,0:T(8,128)(2,1)}, u32[]{:S(2)}, u32[]{:S(2)}) %collective-permute-start.6) | collective-permute-done | bytes 270368 | tf_op jit(solution)/shard_map/ppermute | solution.py:33
  31.1 1.3 pad_maximum_fusion.1.far_ref.refs_1_
  32.8 2.6 %collective-permute-done.8.far_partner_ref.refs_3_ = bf16[4,528,256]{2,1,0:T(8,128)(2,1)} collective-permute-done((bf16[4,528,256]{2,1,0:T(8,128)(2,1)S(1)}, bf16[4,528,256]{2,1,0:T(8,128)(2,1)}, u32[]{:S(2)}, u32[]{:S(2)}) %collective-permute-start.8) | collective-permute-done | bytes 1081376 | tf_op jit(solution)/shard_map/ppermute | solution.py:33
  35.4 6.1 %shard_map.128.own_ref = bf16[2,512,256]{2,1,0:T(8,128)(2,1)} custom-call(s32[16]{0:T(128)S(1)} %stack.159.ids_ref, bf16[4,528,256]{2,1,0:T(8,128)(2,1)S(1)} %pad_maximum_fusion.near_ref.refs_0_, bf16[4,528,256]{2,1,0:T(8,128)(2,1)S(1)} %pad_maximum_fusion.1.far_ref.refs_1_, bf16[4,528,256]{2,1,0:T(8,128)(2,1)} %collective-permute-done.7.near_partner_ref.refs_2_, ...), custom_call_target="tpu_custom_call" | custom-call | flops 2147483648 | bytes 8388608 | tf_op jit(solution)/shard_map/pallas_call | solution.py:237
  41.5 4.9 %collective-permute-start.17 = (bf16[2,512,256]{2,1,0:T(8,128)(2,1)}, bf16[2,512,256]{2,1,0:T(8,128)(2,1)}, u32[]{:S(2)}, u32[]{:S(2)}) collective-permute-start(bf16[2,512,256]{2,1,0:T(8,128)(2,1)} %shard_map.128.own_ref), channel_id=1, source_target_pairs={{0,48},{16,0},{1,49},{17,1},{2,50},{18,2},{3,51},{19,3},{4,52},{20... | collective-permute-start | bytes 1572872 | tf_op jit(solution)/shard_map/ppermute | solution.py:462
  46.4 1.8 %collective-permute-start.10 = (bf16[128,896]{1,0:T(8,128)(2,1)S(1)}, bf16[128,896]{1,0:T(8,128)(2,1)}, u32[]{:S(2)}, u32[]{:S(2)}) collective-permute-start(bf16[128,896]{1,0:T(8,128)(2,1)S(1)} %bitcast.124), channel_id=1, source_target_pairs={{0,4},{1,5},{2,6},{3,7},{4,0},{5,1},{6,2},{7,3},{8,12},{9,13},{10,... | collective-permute-start | bytes 688136 | tf_op jit(solution)/shard_map/ppermute | solution.py:33
  48.2 2.4 %collective-permute-start.11 = (bf16[128,896]{1,0:T(8,128)(2,1)S(1)}, bf16[128,896]{1,0:T(8,128)(2,1)S(1)}, u32[]{:S(2)}, u32[]{:S(2)}) collective-permute-start(bf16[128,896]{1,0:T(8,128)(2,1)S(1)} %bitcast.125), channel_id=1, source_target_pairs={{0,2},{1,3},{2,4},{3,5},{4,6},{5,7},{6,0},{7,1},{8,10},{9,11},{10,... | collective-permute-start | bytes 688136 | tf_op jit(solution)/shard_map/ppermute | solution.py:33
  50.6 1.7 collective-permute-start.9
  52.3 4.3 %collective-permute-done.10 = bf16[128,896]{1,0:T(8,128)(2,1)} collective-permute-done((bf16[128,896]{1,0:T(8,128)(2,1)S(1)}, bf16[128,896]{1,0:T(8,128)(2,1)}, u32[]{:S(2)}, u32[]{:S(2)}) %collective-permute-start.10) | collective-permute-done | bytes 229408 | tf_op jit(solution)/shard_map/ppermute | solution.py:33
  56.6 2.4 %collective-permute-start.16 = (bf16[2,512,256]{2,1,0:T(8,128)(2,1)}, bf16[2,512,256]{2,1,0:T(8,128)(2,1)}, u32[]{:S(2)}, u32[]{:S(2)}) collective-permute-start(bf16[2,512,256]{2,1,0:T(8,128)(2,1)} %shard_map.128.own_ref), channel_id=1, source_target_pairs={{0,16},{16,32},{32,48},{1,17},{17,33},{33,49},{2,18},{18,34},{34,5... | collective-permute-start | bytes 1572872 | tf_op jit(solution)/shard_map/ppermute | solution.py:462
  59.0 5.5 %collective-permute-start.18 = (bf16[2,512,256]{2,1,0:T(8,128)(2,1)}, bf16[2,512,256]{2,1,0:T(8,128)(2,1)}, u32[]{:S(2)}, u32[]{:S(2)}) collective-permute-start(bf16[2,512,256]{2,1,0:T(8,128)(2,1)} %collective-permute-done.17.b3_ref), channel_id=1, source_target_pairs={{48,32},{0,48},{49,33},{1,49},{50,34},{2,50},{51,35},{3,51},{52,36... | collective-permute-start | bytes 1572872 | tf_op jit(solution)/shard_map/ppermute | solution.py:462
  64.9 2.5 %collective-permute-start.14 = (bf16[128,896]{1,0:T(8,128)(2,1)}, bf16[128,896]{1,0:T(8,128)(2,1)}, u32[]{:S(2)}, u32[]{:S(2)}) collective-permute-start(bf16[128,896]{1,0:T(8,128)(2,1)} %collective-permute-done.9), channel_id=1, source_target_pairs={{0,6},{1,7},{2,0},{3,1},{4,2},{5,3},{6,4},{7,5},{8,14},{9,15},{10,... | collective-permute-start | bytes 688136 | tf_op jit(solution)/shard_map/ppermute | solution.py:33
  67.4 1.7 collective-permute-start.15
  69.2 1.6 copy-done.3
  70.8 2.8 %shard_map.129 = bf16[1,512,256]{2,1,0:T(8,128)(2,1)S(1)} custom-call(s32[16]{0:T(128)S(1)} %stack.159.ids_ref, bf16[4,528,256]{2,1,0:T(8,128)(2,1)S(1)} %pad_maximum_fusion.near_ref.refs_0_, bf16[4,528,256]{2,1,0:T(8,128)(2,1)S(1)} %pad_maximum_fusion.1.far_ref.refs_1_, bf16[4,528,256]{2,1,0:T(8,128)(2,1)} %collective-permute-done.7.near_partner_ref.refs_2_, ...), custom_call_target="tpu_custom_call" | custom-call | flops 1073741824 | bytes 6291456 | tf_op jit(solution)/shard_map/pallas_call | solution.py:177
  73.6 1.8 %collective-permute-done.15 = bf16[128,896]{1,0:T(8,128)(2,1)} collective-permute-done((bf16[128,896]{1,0:T(8,128)(2,1)}, bf16[128,896]{1,0:T(8,128)(2,1)}, u32[]{:S(2)}, u32[]{:S(2)}) %collective-permute-start.15) | collective-permute-done | bytes 229408 | tf_op jit(solution)/shard_map/ppermute | solution.py:33
  75.5 2.4 %pad_maximum_fusion.4.refs_1_ = bf16[4,128,896]{2,1,0:T(8,128)(2,1)} fusion(bf16[1,128,896]{2,1,0:T(8,128)(2,1)} %bitcast.38, bf16[1,128,896]{2,1,0:T(8,128)(2,1)} %bitcast.37, bf16[1,128,896]{2,1,0:T(8,128)(2,1)} %bitcast.36, bf16[1,128,896]{2,1,0:T(8,128)(2,1)} %bitcast.35), kind=kLoop, calls=%fused_computation.6 | loop fusion | flops 1376256 | bytes 1835008 | tf_op jit(solution)/shard_map/stack | solution.py:69
  77.8 3.3 %shard_map.130.in_ref = bf16[512,256]{1,0:T(8,128)(2,1)S(1)} custom-call(s32[1]{0:T(128)} %bitcast.39.ctx_ref, bf16[512,256]{1,0:T(8,128)(2,1)S(1)} %bitcast.120, bf16[2,512,256]{2,1,0:T(8,128)(2,1)} %shard_map.128.own_ref, bf16[2,512,256]{2,1,0:T(8,128)(2,1)} %collective-permute-done.16.b1_ref, bf16[2,512,256]{2,1,0:T(8,128)(2,1)} %collective-permute-done.18.b2_ref, ...), custom_call_target="tpu_custom_call" | custom-call | flops 1073741824 | bytes 1310720 | tf_op jit(solution)/shard_map/pallas_call | solution.py:305
  81.2 2.6 %shard_map.132 = bf16[8,512,256]{2,1,0:T(8,128)(2,1)} custom-call(s32[8]{0:T(128)S(1)} %stack.175.ids_ref, bf16[512,256]{1,0:T(8,128)(2,1)S(1)} %shard_map.130.in_ref, bf16[256,4096]{1,0:T(8,128)(2,1)S(1)} %copy-done.1), custom_call_target="tpu_custom_call" | custom-call | flops 536870912 | bytes 2097152 | tf_op jit(solution)/shard_map/pallas_call | solution.py:332
  83.9 2.0 %pad_maximum_fusion.5.refs_0_ = bf16[4,128,896]{2,1,0:T(8,128)(2,1)} fusion(bf16[1,128,896]{2,1,0:T(8,128)(2,1)} %bitcast.50, bf16[1,128,896]{2,1,0:T(8,128)(2,1)S(1)} %bitcast.140, bf16[1,128,896]{2,1,0:T(8,128)(2,1)S(1)} %bitcast.139, bf16[1,128,896]{2,1,0:T(8,128)(2,1)S(1)} %bitcast.128), kind=kLoop, calls=%fused_computation.7 | loop fusion | flops 1376256 | bytes 1835008 | tf_op jit(solution)/shard_map/stack | solution.py:64
  86.5 1.3 shard_map.131.refs_1_
  88.4 1.6 fusion.15
  89.9 1.8 collective-permute-start.22
  91.7 2.9 %collective-permute-start.24 = (bf16[512,256]{1,0:T(8,128)(2,1)S(1)}, bf16[512,256]{1,0:T(8,128)(2,1)S(1)}, u32[]{:S(2)}, u32[]{:S(2)}) collective-permute-start(bf16[512,256]{1,0:T(8,128)(2,1)S(1)} %get-tuple-element.64), channel_id=1, source_target_pairs={{0,6},{1,7},{2,0},{3,1},{4,2},{5,3},{6,4},{7,5},{8,14},{9,15},{10,... | collective-permute-start | bytes 786440 | tf_op jit(solution)/shard_map/ppermute | solution.py:33
  94.7 4.3 %shard_map.133.kv_ref = bf16[2,8,16,16,256]{4,3,2,1,0:T(8,128)(2,1)S(1)} custom-call(bf16[4,128,896]{2,1,0:T(8,128)(2,1)} %pad_maximum_fusion.5.refs_0_, bf16[4,128,896]{2,1,0:T(8,128)(2,1)} %pad_maximum_fusion.4.refs_1_, bf16[4,128,896]{2,1,0:T(8,128)(2,1)} %collective-permute-done.25.refs_2_, bf16[4,128,896]{2,1,0:T(8,128)(2,1)} %collective-permute-done.26.refs_3_, ...), custom_call_target="tpu_custom_call" | custom-call | flops 1879048192 | bytes 3670016 | tf_op jit(solution)/shard_map/pallas_call | solution.py:361
  99.1 3.5 %collective-permute-start.21 = (bf16[512,256]{1,0:T(8,128)(2,1)S(1)}, bf16[512,256]{1,0:T(8,128)(2,1)S(1)}, u32[]{:S(2)}, u32[]{:S(2)}) collective-permute-start(bf16[512,256]{1,0:T(8,128)(2,1)S(1)} %get-tuple-element.67), channel_id=1, source_target_pairs={{0,6},{1,7},{2,0},{3,1},{4,2},{5,3},{6,4},{7,5},{8,14},{9,15},{10,... | collective-permute-start | bytes 786440 | tf_op jit(solution)/shard_map/ppermute | solution.py:33
  102.6 1.3 fusion.9
  103.9 3.2 %collective-permute-start.27 = (bf16[512,256]{1,0:T(8,128)(2,1)S(1)}, bf16[512,256]{1,0:T(8,128)(2,1)S(1)}, u32[]{:S(2)}, u32[]{:S(2)}) collective-permute-start(bf16[512,256]{1,0:T(8,128)(2,1)S(1)} %get-tuple-element.63), channel_id=1, source_target_pairs={{0,4},{1,5},{2,6},{3,7},{4,0},{5,1},{6,2},{7,3},{8,12},{9,13},{10,... | collective-permute-start | bytes 786440 | tf_op jit(solution)/shard_map/ppermute | solution.py:33
  107.1 1.8 %collective-permute-start.28 = (bf16[512,256]{1,0:T(8,128)(2,1)S(1)}, bf16[512,256]{1,0:T(8,128)(2,1)S(1)}, u32[]{:S(2)}, u32[]{:S(2)}) collective-permute-start(bf16[512,256]{1,0:T(8,128)(2,1)S(1)} %get-tuple-element.62), channel_id=1, source_target_pairs={{0,8},{1,9},{2,10},{3,11},{4,12},{5,13},{6,14},{7,15},{8,0},{9,1},... | collective-permute-start | bytes 786440 | tf_op jit(solution)/shard_map/ppermute | solution.py:33
  109.5 6.0 %collective-permute-done.27.refs_5_ = bf16[512,256]{1,0:T(8,128)(2,1)S(1)} collective-permute-done((bf16[512,256]{1,0:T(8,128)(2,1)S(1)}, bf16[512,256]{1,0:T(8,128)(2,1)S(1)}, u32[]{:S(2)}, u32[]{:S(2)}) %collective-permute-start.27) | collective-permute-done | bytes 262176 | tf_op jit(solution)/shard_map/ppermute | solution.py:33
  115.5 2.0 %shard_map.134 = (bf16[512,256]{1,0:T(8,128)(2,1)S(1)}, bf16[528,256]{1,0:T(8,128)(2,1)S(1)}) custom-call(s32[1]{0:T(128)} %bitcast.ids_ref, f32[16,1,256]{2,1,0:T(1,128)S(1)} %bitcast.121, bf16[512,256]{1,0:T(8,128)(2,1)S(1)} %bitcast.116, bf16[8,512,256]{2,1,0:T(8,128)(2,1)S(1)} %shard_map.131.refs_1_, ...), custom_call_target="tpu_custom_call" | custom-call | tf_op jit(solution)/shard_map/pallas_call | solution.py:133
  117.6 1.9 %collective-permute-start.31 = (bf16[528,256]{1,0:T(8,128)(2,1)S(1)}, bf16[528,256]{1,0:T(8,128)(2,1)S(1)}, u32[]{:S(2)}, u32[]{:S(2)}) collective-permute-start(bf16[528,256]{1,0:T(8,128)(2,1)S(1)} %get-tuple-element.47), channel_id=1, source_target_pairs={{0,8},{1,9},{2,10},{3,11},{4,12},{5,13},{6,14},{7,15},{8,0},{9,1},... | collective-permute-start | bytes 811016 | tf_op jit(solution)/shard_map/ppermute | solution.py:33
  119.5 3.0 %collective-permute-start.32 = (bf16[528,256]{1,0:T(8,128)(2,1)S(1)}, bf16[528,256]{1,0:T(8,128)(2,1)S(1)}, u32[]{:S(2)}, u32[]{:S(2)}) collective-permute-start(bf16[528,256]{1,0:T(8,128)(2,1)S(1)} %get-tuple-element.47), channel_id=1, source_target_pairs={{0,4},{1,5},{2,6},{3,7},{4,0},{5,1},{6,2},{7,3},{8,12},{9,13},{10,... | collective-permute-start | bytes 811016 | tf_op jit(solution)/shard_map/ppermute | solution.py:33
  122.5 1.3 collective-permute-start.33
  123.9 2.0 %collective-permute-start.30 = (bf16[528,256]{1,0:T(8,128)(2,1)S(1)}, bf16[528,256]{1,0:T(8,128)(2,1)S(1)}, u32[]{:S(2)}, u32[]{:S(2)}) collective-permute-start(bf16[528,256]{1,0:T(8,128)(2,1)S(1)} %get-tuple-element.47), channel_id=1, source_target_pairs={{0,6},{1,7},{2,0},{3,1},{4,2},{5,3},{6,4},{7,5},{8,14},{9,15},{10,... | collective-permute-start | bytes 811016 | tf_op jit(solution)/shard_map/ppermute | solution.py:33
  125.9 1.8 collective-permute-done.33.earlier_ref
  127.6 2.8 %collective-permute-done.32 = bf16[528,256]{1,0:T(8,128)(2,1)S(1)} collective-permute-done((bf16[528,256]{1,0:T(8,128)(2,1)S(1)}, bf16[528,256]{1,0:T(8,128)(2,1)S(1)}, u32[]{:S(2)}, u32[]{:S(2)}) %collective-permute-start.32) | collective-permute-done | bytes 270368 | tf_op jit(solution)/shard_map/ppermute | solution.py:33
  132.4 1.7 collective-permute-start.36
  135.2 2.7 %collective-permute-done.34 = bf16[528,256]{1,0:T(8,128)(2,1)S(1)} collective-permute-done((bf16[528,256]{1,0:T(8,128)(2,1)S(1)}, bf16[528,256]{1,0:T(8,128)(2,1)S(1)}, u32[]{:S(2)}, u32[]{:S(2)}) %collective-permute-start.34) | collective-permute-done | bytes 270368 | tf_op jit(solution)/shard_map/ppermute | solution.py:33
  137.8 1.3 collective-permute-done.35
  139.1 1.3 collective-permute-done.36
  140.6 2.7 %collective-permute-done.38.refs_3_ = bf16[4,528,256]{2,1,0:T(8,128)(2,1)S(1)} collective-permute-done((bf16[4,528,256]{2,1,0:T(8,128)(2,1)S(1)}, bf16[4,528,256]{2,1,0:T(8,128)(2,1)S(1)}, u32[]{:S(2)}, u32[]{:S(2)}) %collective-permute-start.38) | collective-permute-done | bytes 1081376 | tf_op jit(solution)/shard_map/ppermute | solution.py:33
  143.3 1.8 %shard_map.135 = bf16[1,512,256]{2,1,0:T(8,128)(2,1)S(1)} custom-call(s32[16]{0:T(128)S(1)} %stack.159.ids_ref, bf16[4,528,256]{2,1,0:T(8,128)(2,1)S(1)} %pad_maximum_fusion.2.refs_0_, bf16[4,528,256]{2,1,0:T(8,128)(2,1)S(1)} %pad_maximum_fusion.3.refs_1_, bf16[4,528,256]{2,1,0:T(8,128)(2,1)S(1)} %collective-permute-done.37.refs_2_, ...), custom_call_target="tpu_custom_call" | custom-call | flops 1073741824 | bytes 6291456 | tf_op jit(solution)/shard_map/pallas_call | solution.py:177
  146.7 1.3 shard_map.138
  148.2 1.3 shard_map.137
  149.5 2.7 %collective-permute-done.39 = bf16[8,512,256]{2,1,0:T(8,128)(2,1)S(1)} collective-permute-done((bf16[8,512,256]{2,1,0:T(8,128)(2,1)S(1)}, bf16[8,512,256]{2,1,0:T(8,128)(2,1)S(1)}, u32[]{:S(2)}, u32[]{:S(2)}) %collective-permute-start.39) | collective-permute-done | bytes 2097184 | tf_op jit(solution)/shard_map/ppermute | solution.py:33
  152.6 1.8 collective-permute-start.42
  154.4 1.5 collective-permute-start.43
  156.7 1.2 collective-permute-start.40
  157.9 2.0 %collective-permute-start.41 = (bf16[512,256]{1,0:T(8,128)(2,1)S(1)}, bf16[512,256]{1,0:T(8,128)(2,1)S(1)}, u32[]{:S(2)}, u32[]{:S(2)}) collective-permute-start(bf16[512,256]{1,0:T(8,128)(2,1)S(1)} %get-tuple-element.59), channel_id=1, source_target_pairs={{0,6},{1,7},{2,0},{3,1},{4,2},{5,3},{6,4},{7,5},{8,14},{9,15},{10,... | collective-permute-start | bytes 786440 | tf_op jit(solution)/shard_map/ppermute | solution.py:33
  160.0 2.6 %collective-permute-done.42 = bf16[512,256]{1,0:T(8,128)(2,1)S(1)} collective-permute-done((bf16[512,256]{1,0:T(8,128)(2,1)S(1)}, bf16[512,256]{1,0:T(8,128)(2,1)S(1)}, u32[]{:S(2)}, u32[]{:S(2)}) %collective-permute-start.42) | collective-permute-done | bytes 262176 | tf_op jit(solution)/shard_map/ppermute | solution.py:33
  162.5 1.3 collective-permute-done.43
  163.8 1.2 collective-permute-done.44
  165.3 4.2 %collective-permute-start.45 = (bf16[512,256]{1,0:T(8,128)(2,1)S(1)}, bf16[512,256]{1,0:T(8,128)(2,1)S(1)}, u32[]{:S(2)}, u32[]{:S(2)}) collective-permute-start(bf16[512,256]{1,0:T(8,128)(2,1)S(1)} %get-tuple-element.60), channel_id=1, source_target_pairs={{0,4},{1,5},{2,6},{3,7},{4,0},{5,1},{6,2},{7,3},{8,12},{9,13},{10,... | collective-permute-start | bytes 786440 | tf_op jit(solution)/shard_map/ppermute | solution.py:33
  169.6 1.8 %collective-permute-start.46 = (bf16[512,256]{1,0:T(8,128)(2,1)S(1)}, bf16[512,256]{1,0:T(8,128)(2,1)S(1)}, u32[]{:S(2)}, u32[]{:S(2)}) collective-permute-start(bf16[512,256]{1,0:T(8,128)(2,1)S(1)} %get-tuple-element.61), channel_id=1, source_target_pairs={{0,8},{1,9},{2,10},{3,11},{4,12},{5,13},{6,14},{7,15},{8,0},{9,1},... | collective-permute-start | bytes 786440 | tf_op jit(solution)/shard_map/ppermute | solution.py:33
  171.4 5.0 %collective-permute-done.45 = bf16[512,256]{1,0:T(8,128)(2,1)S(1)} collective-permute-done((bf16[512,256]{1,0:T(8,128)(2,1)S(1)}, bf16[512,256]{1,0:T(8,128)(2,1)S(1)}, u32[]{:S(2)}, u32[]{:S(2)}) %collective-permute-start.45) | collective-permute-done | bytes 262176 | tf_op jit(solution)/shard_map/ppermute | solution.py:33
  (107 shorter events, 17.9 us)
Async XLA Ops:
  0.0 12.1 %copy-start = (bf16[64,8,896]{2,1,0:T(8,128)(2,1)S(1)}, bf16[64,8,896]{2,1,0:T(8,128)(2,1)}, u32[]{:S(2)}) copy-start(bf16[64,8,896]{2,1,0:T(8,128)(2,1)} %param.23) | copy-start | bytes 2752516
  0.0 1.0 copy-start.5
  1.0 0.7 copy-start.8
  2.5 16.6 %collective-permute-start.2 = (bf16[528,256]{1,0:T(8,128)(2,1)S(1)}, bf16[528,256]{1,0:T(8,128)(2,1)S(1)}, u32[]{:S(2)}, u32[]{:S(2)}) collective-permute-start(bf16[528,256]{1,0:T(8,128)(2,1)S(1)} %get-tuple-element.30), channel_id=1, source_target_pairs={{0,8},{1,9},{2,10},{3,11},{4,12},{5,13},{6,14},{7,15},{8,0},{9,1},... | collective-permute-start | bytes 811016 | tf_op jit(solution)/shard_map/ppermute | solution.py:33
  5.7 13.4 %collective-permute-start.3 = (bf16[528,256]{1,0:T(8,128)(2,1)S(1)}, bf16[528,256]{1,0:T(8,128)(2,1)S(1)}, u32[]{:S(2)}, u32[]{:S(2)}) collective-permute-start(bf16[528,256]{1,0:T(8,128)(2,1)S(1)} %get-tuple-element.30), channel_id=1, source_target_pairs={{0,4},{1,5},{2,6},{3,7},{4,0},{5,1},{6,2},{7,3},{8,12},{9,13},{10,... | collective-permute-start | bytes 811016 | tf_op jit(solution)/shard_map/ppermute | solution.py:33
  7.8 16.0 %collective-permute-start = (bf16[528,256]{1,0:T(8,128)(2,1)S(1)}, bf16[528,256]{1,0:T(8,128)(2,1)S(1)}, u32[]{:S(2)}, u32[]{:S(2)}) collective-permute-start(bf16[528,256]{1,0:T(8,128)(2,1)S(1)} %get-tuple-element.30), channel_id=1, source_target_pairs={{0,2},{1,3},{2,4},{3,5},{4,6},{5,7},{6,0},{7,1},{8,10},{9,11},{10,... | collective-permute-start | bytes 811016 | tf_op jit(solution)/shard_map/ppermute | solution.py:33
  7.8 16.0 %collective-permute-start.1 = (bf16[528,256]{1,0:T(8,128)(2,1)S(1)}, bf16[528,256]{1,0:T(8,128)(2,1)}, u32[]{:S(2)}, u32[]{:S(2)}) collective-permute-start(bf16[528,256]{1,0:T(8,128)(2,1)S(1)} %get-tuple-element.30), channel_id=1, source_target_pairs={{0,6},{1,7},{2,0},{3,1},{4,2},{5,3},{6,4},{7,5},{8,14},{9,15},{10,... | collective-permute-start | bytes 811016 | tf_op jit(solution)/shard_map/ppermute | solution.py:33
  13.5 14.1 %all-to-all-start = ((bf16[8,4,8,896]{3,2,1,0:T(8,128)(2,1)}), bf16[8,4,8,896]{3,2,1,0:T(8,128)(2,1)S(1)}, u32[]{:S(2)}, u32[]{:S(2)}) async-start(bf16[8,4,8,896]{3,2,1,0:T(8,128)(2,1)} %bitcast.23), calls=%async_computation | async-start | bytes 917504 | tf_op jit(solution)/shard_map/all_to_all | solution.py:457
  19.1 12.0 %copy-start.10 = (bf16[528,256]{1,0:T(8,128)(2,1)}, bf16[528,256]{1,0:T(8,128)(2,1)S(1)}, u32[]{:S(2)}) copy-start(bf16[528,256]{1,0:T(8,128)(2,1)S(1)} %collective-permute-done.2) | copy-start | bytes 811012
  19.1 9.0 %collective-permute-start.4 = (bf16[528,256]{1,0:T(8,128)(2,1)S(1)}, bf16[528,256]{1,0:T(8,128)(2,1)}, u32[]{:S(2)}, u32[]{:S(2)}) collective-permute-start(bf16[528,256]{1,0:T(8,128)(2,1)S(1)} %collective-permute-done.2), channel_id=1, source_target_pairs={{0,2},{1,3},{2,4},{3,5},{4,6},{5,7},{6,0},{7,1},{8,10},{9,11},{10,... | collective-permute-start | bytes 811016 | tf_op jit(solution)/shard_map/ppermute | solution.py:33
  19.2 8.9 %collective-permute-start.5 = (bf16[528,256]{1,0:T(8,128)(2,1)S(1)}, bf16[528,256]{1,0:T(8,128)(2,1)}, u32[]{:S(2)}, u32[]{:S(2)}) collective-permute-start(bf16[528,256]{1,0:T(8,128)(2,1)S(1)} %collective-permute-done.2), channel_id=1, source_target_pairs={{0,6},{1,7},{2,0},{3,1},{4,2},{5,3},{6,4},{7,5},{8,14},{9,15},{10,... | collective-permute-start | bytes 811016 | tf_op jit(solution)/shard_map/ppermute | solution.py:33
  21.9 9.2 %collective-permute-start.6 = (bf16[528,256]{1,0:T(8,128)(2,1)S(1)}, bf16[528,256]{1,0:T(8,128)(2,1)}, u32[]{:S(2)}, u32[]{:S(2)}) collective-permute-start(bf16[528,256]{1,0:T(8,128)(2,1)S(1)} %collective-permute-done.3), channel_id=1, source_target_pairs={{0,8},{1,9},{2,10},{3,11},{4,12},{5,13},{6,14},{7,15},{8,0},{9,1},... | collective-permute-start | bytes 811016 | tf_op jit(solution)/shard_map/ppermute | solution.py:33
  24.9 7.9 %collective-permute-start.7 = (bf16[4,528,256]{2,1,0:T(8,128)(2,1)S(1)}, bf16[4,528,256]{2,1,0:T(8,128)(2,1)}, u32[]{:S(2)}, u32[]{:S(2)}) collective-permute-start(bf16[4,528,256]{2,1,0:T(8,128)(2,1)S(1)} %pad_maximum_fusion.near_ref.refs_0_), channel_id=1, source_target_pairs={{0,1},{1,0},{2,3},{3,2},{4,5},{5,4},{6,7},{7,6},{8,9},{9,8},{10,11... | collective-permute-start | bytes 3244040 | tf_op jit(solution)/shard_map/ppermute | solution.py:33
  32.4 2.9 %collective-permute-start.8 = (bf16[4,528,256]{2,1,0:T(8,128)(2,1)S(1)}, bf16[4,528,256]{2,1,0:T(8,128)(2,1)}, u32[]{:S(2)}, u32[]{:S(2)}) collective-permute-start(bf16[4,528,256]{2,1,0:T(8,128)(2,1)S(1)} %pad_maximum_fusion.1.far_ref.refs_1_), channel_id=1, source_target_pairs={{0,1},{1,0},{2,3},{3,2},{4,5},{5,4},{6,7},{7,6},{8,9},{9,8},{10,11... | collective-permute-start | bytes 3244040 | tf_op jit(solution)/shard_map/ppermute | solution.py:33
  41.5 17.5 %collective-permute-start.17 = (bf16[2,512,256]{2,1,0:T(8,128)(2,1)}, bf16[2,512,256]{2,1,0:T(8,128)(2,1)}, u32[]{:S(2)}, u32[]{:S(2)}) collective-permute-start(bf16[2,512,256]{2,1,0:T(8,128)(2,1)} %shard_map.128.own_ref), channel_id=1, source_target_pairs={{0,48},{16,0},{1,49},{17,1},{2,50},{18,2},{3,51},{19,3},{4,52},{20... | collective-permute-start | bytes 1572872 | tf_op jit(solution)/shard_map/ppermute | solution.py:462
  46.4 10.2 %collective-permute-start.10 = (bf16[128,896]{1,0:T(8,128)(2,1)S(1)}, bf16[128,896]{1,0:T(8,128)(2,1)}, u32[]{:S(2)}, u32[]{:S(2)}) collective-permute-start(bf16[128,896]{1,0:T(8,128)(2,1)S(1)} %bitcast.124), channel_id=1, source_target_pairs={{0,4},{1,5},{2,6},{3,7},{4,0},{5,1},{6,2},{7,3},{8,12},{9,13},{10,... | collective-permute-start | bytes 688136 | tf_op jit(solution)/shard_map/ppermute | solution.py:33
  48.2 16.4 %collective-permute-start.11 = (bf16[128,896]{1,0:T(8,128)(2,1)S(1)}, bf16[128,896]{1,0:T(8,128)(2,1)S(1)}, u32[]{:S(2)}, u32[]{:S(2)}) collective-permute-start(bf16[128,896]{1,0:T(8,128)(2,1)S(1)} %bitcast.125), channel_id=1, source_target_pairs={{0,2},{1,3},{2,4},{3,5},{4,6},{5,7},{6,0},{7,1},{8,10},{9,11},{10,... | collective-permute-start | bytes 688136 | tf_op jit(solution)/shard_map/ppermute | solution.py:33
  50.6 14.0 %collective-permute-start.12 = (bf16[128,896]{1,0:T(8,128)(2,1)S(1)}, bf16[128,896]{1,0:T(8,128)(2,1)S(1)}, u32[]{:S(2)}, u32[]{:S(2)}) collective-permute-start(bf16[128,896]{1,0:T(8,128)(2,1)S(1)} %bitcast.126), channel_id=1, source_target_pairs={{0,6},{1,7},{2,0},{3,1},{4,2},{5,3},{6,4},{7,5},{8,14},{9,15},{10,... | collective-permute-start | bytes 688136 | tf_op jit(solution)/shard_map/ppermute | solution.py:33
  50.6 14.0 %collective-permute-start.9 = (bf16[128,896]{1,0:T(8,128)(2,1)S(1)}, bf16[128,896]{1,0:T(8,128)(2,1)}, u32[]{:S(2)}, u32[]{:S(2)}) collective-permute-start(bf16[128,896]{1,0:T(8,128)(2,1)S(1)} %bitcast.127), channel_id=1, source_target_pairs={{0,8},{1,9},{2,10},{3,11},{4,12},{5,13},{6,14},{7,15},{8,0},{9,1},... | collective-permute-start | bytes 688136 | tf_op jit(solution)/shard_map/ppermute | solution.py:33
  56.6 21.2 %collective-permute-start.16 = (bf16[2,512,256]{2,1,0:T(8,128)(2,1)}, bf16[2,512,256]{2,1,0:T(8,128)(2,1)}, u32[]{:S(2)}, u32[]{:S(2)}) collective-permute-start(bf16[2,512,256]{2,1,0:T(8,128)(2,1)} %shard_map.128.own_ref), channel_id=1, source_target_pairs={{0,16},{16,32},{32,48},{1,17},{17,33},{33,49},{2,18},{18,34},{34,5... | collective-permute-start | bytes 1572872 | tf_op jit(solution)/shard_map/ppermute | solution.py:462
  59.0 18.8 %collective-permute-start.18 = (bf16[2,512,256]{2,1,0:T(8,128)(2,1)}, bf16[2,512,256]{2,1,0:T(8,128)(2,1)}, u32[]{:S(2)}, u32[]{:S(2)}) collective-permute-start(bf16[2,512,256]{2,1,0:T(8,128)(2,1)} %collective-permute-done.17.b3_ref), channel_id=1, source_target_pairs={{48,32},{0,48},{49,33},{1,49},{50,34},{2,50},{51,35},{3,51},{52,36... | collective-permute-start | bytes 1572872 | tf_op jit(solution)/shard_map/ppermute | solution.py:462
  64.6 2.8 %copy-start.11 = (bf16[128,896]{1,0:T(8,128)(2,1)}, bf16[128,896]{1,0:T(8,128)(2,1)S(1)}, u32[]{:S(2)}) copy-start(bf16[128,896]{1,0:T(8,128)(2,1)S(1)} %collective-permute-done.11) | copy-start | bytes 688132
  64.6 2.8 %copy-start.13 = (bf16[128,896]{1,0:T(8,128)(2,1)}, bf16[128,896]{1,0:T(8,128)(2,1)S(1)}, u32[]{:S(2)}) copy-start(bf16[128,896]{1,0:T(8,128)(2,1)S(1)} %collective-permute-done.12) | copy-start | bytes 688132
  64.6 9.0 %collective-permute-start.13 = (bf16[128,896]{1,0:T(8,128)(2,1)}, bf16[128,896]{1,0:T(8,128)(2,1)}, u32[]{:S(2)}, u32[]{:S(2)}) collective-permute-start(bf16[128,896]{1,0:T(8,128)(2,1)} %collective-permute-done.9), channel_id=1, source_target_pairs={{0,2},{1,3},{2,4},{3,5},{4,6},{5,7},{6,0},{7,1},{8,10},{9,11},{10,... | collective-permute-start | bytes 688136 | tf_op jit(solution)/shard_map/ppermute | solution.py:33
  64.9 8.7 %collective-permute-start.14 = (bf16[128,896]{1,0:T(8,128)(2,1)}, bf16[128,896]{1,0:T(8,128)(2,1)}, u32[]{:S(2)}, u32[]{:S(2)}) collective-permute-start(bf16[128,896]{1,0:T(8,128)(2,1)} %collective-permute-done.9), channel_id=1, source_target_pairs={{0,6},{1,7},{2,0},{3,1},{4,2},{5,3},{6,4},{7,5},{8,14},{9,15},{10,... | collective-permute-start | bytes 688136 | tf_op jit(solution)/shard_map/ppermute | solution.py:33
  67.4 8.1 %collective-permute-start.15 = (bf16[128,896]{1,0:T(8,128)(2,1)}, bf16[128,896]{1,0:T(8,128)(2,1)}, u32[]{:S(2)}, u32[]{:S(2)}) collective-permute-start(bf16[128,896]{1,0:T(8,128)(2,1)} %collective-permute-done.10), channel_id=1, source_target_pairs={{0,8},{1,9},{2,10},{3,11},{4,12},{5,13},{6,14},{7,15},{8,0},{9,1},... | collective-permute-start | bytes 688136 | tf_op jit(solution)/shard_map/ppermute | solution.py:33
  69.2 1.6 copy-start.3
  77.8 3.4 %copy-start.1 = (bf16[256,4096]{1,0:T(8,128)(2,1)S(1)}, bf16[256,4096]{1,0:T(8,128)(2,1)}, u32[]{:S(2)}) copy-start(bf16[256,4096]{1,0:T(8,128)(2,1)} %w_ref.5) | copy-start | bytes 6291460
  81.2 2.7 %copy-start.12 = (bf16[128,896]{1,0:T(8,128)(2,1)S(1)}, bf16[128,896]{1,0:T(8,128)(2,1)}, u32[]{:S(2)}) copy-start(bf16[128,896]{1,0:T(8,128)(2,1)} %copy-done.11) | copy-start | bytes 688132
  81.2 2.7 %copy-start.14 = (bf16[128,896]{1,0:T(8,128)(2,1)S(1)}, bf16[128,896]{1,0:T(8,128)(2,1)}, u32[]{:S(2)}) copy-start(bf16[128,896]{1,0:T(8,128)(2,1)} %copy-done.13) | copy-start | bytes 688132
  83.9 4.5 %collective-permute-start.19 = (bf16[8,512,256]{2,1,0:T(8,128)(2,1)}, bf16[8,512,256]{2,1,0:T(8,128)(2,1)}, u32[]{:S(2)}, u32[]{:S(2)}) collective-permute-start(bf16[8,512,256]{2,1,0:T(8,128)(2,1)} %shard_map.132), channel_id=1, source_target_pairs={{0,1},{1,0},{2,3},{3,2},{4,5},{5,4},{6,7},{7,6},{8,9},{9,8},{10,11... | collective-permute-start | bytes 6291464 | tf_op jit(solution)/shard_map/ppermute | solution.py:33
  85.9 8.8 %collective-permute-start.25 = (bf16[4,128,896]{2,1,0:T(8,128)(2,1)}, bf16[4,128,896]{2,1,0:T(8,128)(2,1)}, u32[]{:S(2)}, u32[]{:S(2)}) collective-permute-start(bf16[4,128,896]{2,1,0:T(8,128)(2,1)} %pad_maximum_fusion.5.refs_0_), channel_id=1, source_target_pairs={{0,1},{1,0},{2,3},{3,2},{4,5},{5,4},{6,7},{7,6},{8,9},{9,8},{10,11... | collective-permute-start | bytes 2752520 | tf_op jit(solution)/shard_map/ppermute | solution.py:33
  86.4 8.3 %collective-permute-start.26 = (bf16[4,128,896]{2,1,0:T(8,128)(2,1)}, bf16[4,128,896]{2,1,0:T(8,128)(2,1)}, u32[]{:S(2)}, u32[]{:S(2)}) collective-permute-start(bf16[4,128,896]{2,1,0:T(8,128)(2,1)} %pad_maximum_fusion.4.refs_1_), channel_id=1, source_target_pairs={{0,1},{1,0},{2,3},{3,2},{4,5},{5,4},{6,7},{7,6},{8,9},{9,8},{10,11... | collective-permute-start | bytes 2752520 | tf_op jit(solution)/shard_map/ppermute | solution.py:33
  87.8 6.9 %copy-start.9 = (bf16[2,896,256]{2,1,0:T(8,128)(2,1)S(1)}, bf16[2,896,256]{2,1,0:T(8,128)(2,1)}, u32[]{:S(2)}) copy-start(bf16[2,896,256]{2,1,0:T(8,128)(2,1)} %refs_4_.4) | copy-start | bytes 2752516
  89.9 12.7 %collective-permute-start.22 = (bf16[512,256]{1,0:T(8,128)(2,1)S(1)}, bf16[512,256]{1,0:T(8,128)(2,1)S(1)}, u32[]{:S(2)}, u32[]{:S(2)}) collective-permute-start(bf16[512,256]{1,0:T(8,128)(2,1)S(1)} %get-tuple-element.66), channel_id=1, source_target_pairs={{0,8},{1,9},{2,10},{3,11},{4,12},{5,13},{6,14},{7,15},{8,0},{9,1},... | collective-permute-start | bytes 786440 | tf_op jit(solution)/shard_map/ppermute | solution.py:33
  91.7 10.9 %collective-permute-start.23 = (bf16[512,256]{1,0:T(8,128)(2,1)S(1)}, bf16[512,256]{1,0:T(8,128)(2,1)S(1)}, u32[]{:S(2)}, u32[]{:S(2)}) collective-permute-start(bf16[512,256]{1,0:T(8,128)(2,1)S(1)} %get-tuple-element.65), channel_id=1, source_target_pairs={{0,2},{1,3},{2,4},{3,5},{4,6},{5,7},{6,0},{7,1},{8,10},{9,11},{10,... | collective-permute-start | bytes 786440 | tf_op jit(solution)/shard_map/ppermute | solution.py:33
  91.7 10.9 %collective-permute-start.24 = (bf16[512,256]{1,0:T(8,128)(2,1)S(1)}, bf16[512,256]{1,0:T(8,128)(2,1)S(1)}, u32[]{:S(2)}, u32[]{:S(2)}) collective-permute-start(bf16[512,256]{1,0:T(8,128)(2,1)S(1)} %get-tuple-element.64), channel_id=1, source_target_pairs={{0,6},{1,7},{2,0},{3,1},{4,2},{5,3},{6,4},{7,5},{8,14},{9,15},{10,... | collective-permute-start | bytes 786440 | tf_op jit(solution)/shard_map/ppermute | solution.py:33
  99.0 10.5 %collective-permute-start.20 = (bf16[512,256]{1,0:T(8,128)(2,1)S(1)}, bf16[512,256]{1,0:T(8,128)(2,1)S(1)}, u32[]{:S(2)}, u32[]{:S(2)}) collective-permute-start(bf16[512,256]{1,0:T(8,128)(2,1)S(1)} %get-tuple-element.68), channel_id=1, source_target_pairs={{0,2},{1,3},{2,4},{3,5},{4,6},{5,7},{6,0},{7,1},{8,10},{9,11},{10,... | collective-permute-start | bytes 786440 | tf_op jit(solution)/shard_map/ppermute | solution.py:33
  99.1 16.4 %copy-start.6 = (bf16[1,512,256]{2,1,0:T(8,128)(2,1)S(1)}, bf16[1,512,256]{2,1,0:T(8,128)(2,1)}, u32[]{:S(2)}) copy-start(bf16[1,512,256]{2,1,0:T(8,128)(2,1)} %param.13) | copy-start | bytes 786436
  99.1 16.4 %copy-start.7 = (f32[4096]{0:T(1024)S(1)}, f32[4096]{0:T(1024)}, u32[]{:S(2)}) copy-start(f32[4096]{0:T(1024)} %param.15) | copy-start | bytes 49156
  99.1 10.4 %collective-permute-start.21 = (bf16[512,256]{1,0:T(8,128)(2,1)S(1)}, bf16[512,256]{1,0:T(8,128)(2,1)S(1)}, u32[]{:S(2)}, u32[]{:S(2)}) collective-permute-start(bf16[512,256]{1,0:T(8,128)(2,1)S(1)} %get-tuple-element.67), channel_id=1, source_target_pairs={{0,6},{1,7},{2,0},{3,1},{4,2},{5,3},{6,4},{7,5},{8,14},{9,15},{10,... | collective-permute-start | bytes 786440 | tf_op jit(solution)/shard_map/ppermute | solution.py:33
  103.9 11.6 %collective-permute-start.27 = (bf16[512,256]{1,0:T(8,128)(2,1)S(1)}, bf16[512,256]{1,0:T(8,128)(2,1)S(1)}, u32[]{:S(2)}, u32[]{:S(2)}) collective-permute-start(bf16[512,256]{1,0:T(8,128)(2,1)S(1)} %get-tuple-element.63), channel_id=1, source_target_pairs={{0,4},{1,5},{2,6},{3,7},{4,0},{5,1},{6,2},{7,3},{8,12},{9,13},{10,... | collective-permute-start | bytes 786440 | tf_op jit(solution)/shard_map/ppermute | solution.py:33
  107.1 8.4 %collective-permute-start.28 = (bf16[512,256]{1,0:T(8,128)(2,1)S(1)}, bf16[512,256]{1,0:T(8,128)(2,1)S(1)}, u32[]{:S(2)}, u32[]{:S(2)}) collective-permute-start(bf16[512,256]{1,0:T(8,128)(2,1)S(1)} %get-tuple-element.62), channel_id=1, source_target_pairs={{0,8},{1,9},{2,10},{3,11},{4,12},{5,13},{6,14},{7,15},{8,0},{9,1},... | collective-permute-start | bytes 786440 | tf_op jit(solution)/shard_map/ppermute | solution.py:33
  117.6 10.1 %collective-permute-start.31 = (bf16[528,256]{1,0:T(8,128)(2,1)S(1)}, bf16[528,256]{1,0:T(8,128)(2,1)S(1)}, u32[]{:S(2)}, u32[]{:S(2)}) collective-permute-start(bf16[528,256]{1,0:T(8,128)(2,1)S(1)} %get-tuple-element.47), channel_id=1, source_target_pairs={{0,8},{1,9},{2,10},{3,11},{4,12},{5,13},{6,14},{7,15},{8,0},{9,1},... | collective-permute-start | bytes 811016 | tf_op jit(solution)/shard_map/ppermute | solution.py:33
  119.5 10.9 %collective-permute-start.32 = (bf16[528,256]{1,0:T(8,128)(2,1)S(1)}, bf16[528,256]{1,0:T(8,128)(2,1)S(1)}, u32[]{:S(2)}, u32[]{:S(2)}) collective-permute-start(bf16[528,256]{1,0:T(8,128)(2,1)S(1)} %get-tuple-element.47), channel_id=1, source_target_pairs={{0,4},{1,5},{2,6},{3,7},{4,0},{5,1},{6,2},{7,3},{8,12},{9,13},{10,... | collective-permute-start | bytes 811016 | tf_op jit(solution)/shard_map/ppermute | solution.py:33
  122.5 5.2 %collective-permute-start.33 = (bf16[2,16,16,256]{3,2,1,0:T(8,128)(2,1)S(1)}, bf16[2,16,16,256]{3,2,1,0:T(8,128)(2,1)S(1)}, u32[]{:S(2)}, u32[]{:S(2)}) collective-permute-start(bf16[2,16,16,256]{3,2,1,0:T(8,128)(2,1)S(1)} %slice_bitcast_fusion.2), channel_id=1, source_target_pairs={{0,16},{16,32},{32,48},{1,17},{17,33},{33,49},{2,18},{18,34},{34,5... | collective-permute-start | bytes 786440 | tf_op jit(solution)/shard_map/ppermute | solution.py:462
  123.8 11.2 %collective-permute-start.29 = (bf16[528,256]{1,0:T(8,128)(2,1)S(1)}, bf16[528,256]{1,0:T(8,128)(2,1)S(1)}, u32[]{:S(2)}, u32[]{:S(2)}) collective-permute-start(bf16[528,256]{1,0:T(8,128)(2,1)S(1)} %get-tuple-element.47), channel_id=1, source_target_pairs={{0,2},{1,3},{2,4},{3,5},{4,6},{5,7},{6,0},{7,1},{8,10},{9,11},{10,... | collective-permute-start | bytes 811016 | tf_op jit(solution)/shard_map/ppermute | solution.py:33
  123.9 11.1 %collective-permute-start.30 = (bf16[528,256]{1,0:T(8,128)(2,1)S(1)}, bf16[528,256]{1,0:T(8,128)(2,1)S(1)}, u32[]{:S(2)}, u32[]{:S(2)}) collective-permute-start(bf16[528,256]{1,0:T(8,128)(2,1)S(1)} %get-tuple-element.47), channel_id=1, source_target_pairs={{0,6},{1,7},{2,0},{3,1},{4,2},{5,3},{6,4},{7,5},{8,14},{9,15},{10,... | collective-permute-start | bytes 811016 | tf_op jit(solution)/shard_map/ppermute | solution.py:33
  130.4 7.4 %collective-permute-start.34 = (bf16[528,256]{1,0:T(8,128)(2,1)S(1)}, bf16[528,256]{1,0:T(8,128)(2,1)S(1)}, u32[]{:S(2)}, u32[]{:S(2)}) collective-permute-start(bf16[528,256]{1,0:T(8,128)(2,1)S(1)} %collective-permute-done.31), channel_id=1, source_target_pairs={{0,2},{1,3},{2,4},{3,5},{4,6},{5,7},{6,0},{7,1},{8,10},{9,11},{10,... | collective-permute-start | bytes 811016 | tf_op jit(solution)/shard_map/ppermute | solution.py:33
  131.4 7.6 %collective-permute-start.35 = (bf16[528,256]{1,0:T(8,128)(2,1)S(1)}, bf16[528,256]{1,0:T(8,128)(2,1)S(1)}, u32[]{:S(2)}, u32[]{:S(2)}) collective-permute-start(bf16[528,256]{1,0:T(8,128)(2,1)S(1)} %collective-permute-done.31), channel_id=1, source_target_pairs={{0,6},{1,7},{2,0},{3,1},{4,2},{5,3},{6,4},{7,5},{8,14},{9,15},{10,... | collective-permute-start | bytes 811016 | tf_op jit(solution)/shard_map/ppermute | solution.py:33
  132.4 8.0 %collective-permute-start.36 = (bf16[528,256]{1,0:T(8,128)(2,1)S(1)}, bf16[528,256]{1,0:T(8,128)(2,1)S(1)}, u32[]{:S(2)}, u32[]{:S(2)}) collective-permute-start(bf16[528,256]{1,0:T(8,128)(2,1)S(1)} %collective-permute-done.32), channel_id=1, source_target_pairs={{0,8},{1,9},{2,10},{3,11},{4,12},{5,13},{6,14},{7,15},{8,0},{9,1},... | collective-permute-start | bytes 811016 | tf_op jit(solution)/shard_map/ppermute | solution.py:33
  135.1 5.6 %collective-permute-start.37 = (bf16[4,528,256]{2,1,0:T(8,128)(2,1)S(1)}, bf16[4,528,256]{2,1,0:T(8,128)(2,1)S(1)}, u32[]{:S(2)}, u32[]{:S(2)}) collective-permute-start(bf16[4,528,256]{2,1,0:T(8,128)(2,1)S(1)} %pad_maximum_fusion.2.refs_0_), channel_id=1, source_target_pairs={{0,1},{1,0},{2,3},{3,2},{4,5},{5,4},{6,7},{7,6},{8,9},{9,8},{10,11... | collective-permute-start | bytes 3244040 | tf_op jit(solution)/shard_map/ppermute | solution.py:33
  140.4 2.9 %copy-start.4 = (bf16[4096,256]{1,0:T(8,128)(2,1)S(1)}, bf16[4096,256]{1,0:T(8,128)(2,1)}, u32[]{:S(2)}) copy-start(bf16[4096,256]{1,0:T(8,128)(2,1)} %refs_4_.5) | copy-start | bytes 6291460
  140.5 2.8 %collective-permute-start.38 = (bf16[4,528,256]{2,1,0:T(8,128)(2,1)S(1)}, bf16[4,528,256]{2,1,0:T(8,128)(2,1)S(1)}, u32[]{:S(2)}, u32[]{:S(2)}) collective-permute-start(bf16[4,528,256]{2,1,0:T(8,128)(2,1)S(1)} %pad_maximum_fusion.3.refs_1_), channel_id=1, source_target_pairs={{0,1},{1,0},{2,3},{3,2},{4,5},{5,4},{6,7},{7,6},{8,9},{9,8},{10,11... | collective-permute-start | bytes 3244040 | tf_op jit(solution)/shard_map/ppermute | solution.py:33
  145.1 1.6 copy-start.2
  148.0 4.2 %collective-permute-start.39 = (bf16[8,512,256]{2,1,0:T(8,128)(2,1)S(1)}, bf16[8,512,256]{2,1,0:T(8,128)(2,1)S(1)}, u32[]{:S(2)}, u32[]{:S(2)}) collective-permute-start(bf16[8,512,256]{2,1,0:T(8,128)(2,1)S(1)} %shard_map.138), channel_id=1, source_target_pairs={{0,1},{1,0},{2,3},{3,2},{4,5},{5,4},{6,7},{7,6},{8,9},{9,8},{10,11... | collective-permute-start | bytes 6291464 | tf_op jit(solution)/shard_map/ppermute | solution.py:33
  152.6 9.9 %collective-permute-start.42 = (bf16[512,256]{1,0:T(8,128)(2,1)S(1)}, bf16[512,256]{1,0:T(8,128)(2,1)S(1)}, u32[]{:S(2)}, u32[]{:S(2)}) collective-permute-start(bf16[512,256]{1,0:T(8,128)(2,1)S(1)} %get-tuple-element.58), channel_id=1, source_target_pairs={{0,8},{1,9},{2,10},{3,11},{4,12},{5,13},{6,14},{7,15},{8,0},{9,1},... | collective-permute-start | bytes 786440 | tf_op jit(solution)/shard_map/ppermute | solution.py:33
  154.4 9.5 %collective-permute-start.43 = (bf16[512,256]{1,0:T(8,128)(2,1)S(1)}, bf16[512,256]{1,0:T(8,128)(2,1)S(1)}, u32[]{:S(2)}, u32[]{:S(2)}) collective-permute-start(bf16[512,256]{1,0:T(8,128)(2,1)S(1)} %get-tuple-element.57), channel_id=1, source_target_pairs={{0,2},{1,3},{2,4},{3,5},{4,6},{5,7},{6,0},{7,1},{8,10},{9,11},{10,... | collective-permute-start | bytes 786440 | tf_op jit(solution)/shard_map/ppermute | solution.py:33
  155.9 9.2 %collective-permute-start.44 = (bf16[512,256]{1,0:T(8,128)(2,1)S(1)}, bf16[512,256]{1,0:T(8,128)(2,1)S(1)}, u32[]{:S(2)}, u32[]{:S(2)}) collective-permute-start(bf16[512,256]{1,0:T(8,128)(2,1)S(1)} %get-tuple-element.56), channel_id=1, source_target_pairs={{0,6},{1,7},{2,0},{3,1},{4,2},{5,3},{6,4},{7,5},{8,14},{9,15},{10,... | collective-permute-start | bytes 786440 | tf_op jit(solution)/shard_map/ppermute | solution.py:33
  156.7 14.7 %collective-permute-start.40 = (bf16[512,256]{1,0:T(8,128)(2,1)S(1)}, bf16[512,256]{1,0:T(8,128)(2,1)S(1)}, u32[]{:S(2)}, u32[]{:S(2)}) collective-permute-start(bf16[512,256]{1,0:T(8,128)(2,1)S(1)} %get-tuple-element.55), channel_id=1, source_target_pairs={{0,2},{1,3},{2,4},{3,5},{4,6},{5,7},{6,0},{7,1},{8,10},{9,11},{10,... | collective-permute-start | bytes 786440 | tf_op jit(solution)/shard_map/ppermute | solution.py:33
  157.9 13.5 %collective-permute-start.41 = (bf16[512,256]{1,0:T(8,128)(2,1)S(1)}, bf16[512,256]{1,0:T(8,128)(2,1)S(1)}, u32[]{:S(2)}, u32[]{:S(2)}) collective-permute-start(bf16[512,256]{1,0:T(8,128)(2,1)S(1)} %get-tuple-element.59), channel_id=1, source_target_pairs={{0,6},{1,7},{2,0},{3,1},{4,2},{5,3},{6,4},{7,5},{8,14},{9,15},{10,... | collective-permute-start | bytes 786440 | tf_op jit(solution)/shard_map/ppermute | solution.py:33
  165.3 11.0 %collective-permute-start.45 = (bf16[512,256]{1,0:T(8,128)(2,1)S(1)}, bf16[512,256]{1,0:T(8,128)(2,1)S(1)}, u32[]{:S(2)}, u32[]{:S(2)}) collective-permute-start(bf16[512,256]{1,0:T(8,128)(2,1)S(1)} %get-tuple-element.60), channel_id=1, source_target_pairs={{0,4},{1,5},{2,6},{3,7},{4,0},{5,1},{6,2},{7,3},{8,12},{9,13},{10,... | collective-permute-start | bytes 786440 | tf_op jit(solution)/shard_map/ppermute | solution.py:33
  169.6 7.9 %collective-permute-start.46 = (bf16[512,256]{1,0:T(8,128)(2,1)S(1)}, bf16[512,256]{1,0:T(8,128)(2,1)S(1)}, u32[]{:S(2)}, u32[]{:S(2)}) collective-permute-start(bf16[512,256]{1,0:T(8,128)(2,1)S(1)} %get-tuple-element.61), channel_id=1, source_target_pairs={{0,8},{1,9},{2,10},{3,11},{4,12},{5,13},{6,14},{7,15},{8,0},{9,1},... | collective-permute-start | bytes 786440 | tf_op jit(solution)/shard_map/ppermute | solution.py:33

commit v4 on v3

--- a/solution.py
+++ b/solution.py
@@ -72,24 +72,26 @@
 
 
 def scatter_mp(mine, partner, during_first=None):
-    partner = mp_send(partner, TO_CORE)
+    near, far = mp_send(partner[0], TO_CORE), mp_send(partner[1], TO_CORE)
+    count = near.shape[0]
 
     def part(i):
-        return mine[i].astype(jnp.float32) + partner[i].astype(jnp.float32)
+        other = near[i] if i < count else far[i - count]
+        return mine[i].astype(jnp.float32) + other.astype(jnp.float32)
 
     b16, f32 = jnp.bfloat16, jnp.float32
     _, left, right, x2, y, y_left, y_right, y2 = range(8)
-    far = mp_send(part(y2).astype(b16), TO_Y)
+    via_y = mp_send(part(y2).astype(b16), TO_Y)
     from_left = mp_send(part(y_right).astype(b16), TO_RIGHT)
     from_right = mp_send(part(y_left).astype(b16), TO_LEFT)
     near_left = mp_send(part(right).astype(b16), TO_RIGHT)
     near_right = mp_send(part(left).astype(b16), TO_LEFT)
-    (far, from_left, from_right), during_first = lax.optimization_barrier(
-        ((far, from_left, from_right), during_first)
-    )
-    from_x2 = mp_send((part(x2) + far.astype(f32)).astype(b16), TO_X2)
+    (via_y, from_left, from_right), during_first = lax.optimization_barrier(
+        ((via_y, from_left, from_right), during_first)
+    )
+    from_x2 = mp_send((part(x2) + via_y.astype(f32)).astype(b16), TO_X2)
     from_y = mp_send((part(y) + from_left.astype(f32) + from_right.astype(f32)).astype(b16), TO_Y)
-    return [mine, partner, near_left, near_right, from_x2, from_y], during_first
+    return [mine, near, near_left, near_right, from_x2, from_y], during_first
 
 
 IN_VMEM = pl.BlockSpec(memory_space=pltpu.VMEM)
@@ -500,7 +502,9 @@
         ),
         all_first=True,
     )
-    for_partner = output_blocks(ids[half:], attended, w_out)
+    far_partner = output_blocks(ids[half + half // 2 :], attended, w_out)
+    near_partner = output_blocks(ids[half : half + half // 2], attended, w_out)
+    for_partner = (near_partner, far_partner)
     for_mine = output_blocks(ids[:half], attended, w_out)
     neighbour_kv = neighbour_projection(nb_stacks, w_cross_kv)
     summands, neighbour_kv = scatter_mp(for_mine, for_partner, neighbour_kv)
@@ -509,7 +513,9 @@
     stacks, earlier, _ = gather_mp(shard, earlier)
     cross_queries = normed_projection(ids, stacks, (w_cross_query,))[0]
     crossed = cross_attention(cross_queries, neighbour_kv, earlier)
-    for_partner = output_blocks(ids[half:], crossed, w_cross_out)
+    far_partner = output_blocks(ids[half + half // 2 :], crossed, w_cross_out)
+    near_partner = output_blocks(ids[half : half + half // 2], crossed, w_cross_out)
+    for_partner = (near_partner, far_partner)
     for_mine = output_blocks(ids[:half], crossed, w_cross_out)
     summands, _ = scatter_mp(for_mine, for_partner)
     total = residual.astype(jnp.float32)

time: 179 us -> 175 us (0.978)
  waiting for transfers between devices: 48.7 us -> 46.1 us
  other arithmetic: 12.1 us -> 10 us
    ppermute x43 -> x45, waiting for transfers between devices: 44.4 us -> 37.5 us  [mp_send(): return lax.ppermute(block, 'mp', pairs)]
    ppermute x4, waiting for transfers between devices: 1.77 us -> 4.29 us  [ctx_send(): return lax.ppermute(block, 'ctx', pairs)]
    ppermute x43 -> x45, starting transfers between devices: 60.8 us -> 63.2 us  [mp_send(): return lax.ppermute(block, 'mp', pairs)]
    pallas_call x4 -> x6, Pallas kernels: 6.45 us -> 8.46 us  [output_blocks(): call(kernel, 12, in_specs=[pl.BlockSpec(memory_space=pltpu.SMEM), IN_VMEM...]
    unnamed x32 -> x24, local copies, waits for them, and re-layouts: 5.56 us -> 3.94 us
  transfers between devices with their start and end apart: 48 -> 50, of which waited for: 21 -> 23; matrix products, arithmetic and copies ran while one was open for 8% -> 7% of each run, Pallas kernels for 5% -> 6%
where the time goes in v4:
time: 175 us; the launch traced here: 173 us
  starting transfers between devices  81.8 us (47%)
  waiting for transfers between devices  46.1 us (26%)
  Pallas kernels  27.9 us (16%)
  other arithmetic  10 us (6%)
  local copies, waits for them, and re-layouts  6.42 us (4%)
    ppermute x45, starting transfers between devices, mp_send(): return lax.ppermute(block, 'mp', pairs)  63.2 us
    ppermute x45, waiting for transfers between devices, mp_send(): return lax.ppermute(block, 'mp', pairs)  37.5 us
    ppermute x4, starting transfers between devices, ctx_send(): return lax.ppermute(block, 'ctx', pairs)  13.1 us
    pallas_call x6, Pallas kernels, output_blocks(): call(kernel, 12, in_specs=[pl.BlockSpec(memory_space=pltpu.SMEM), IN_VMEM...  8.46 us
    all_to_all x1, starting transfers between devices, exchange_neighbours(): lax.all_to_all(outgoing, ('pool', 'ctx'), split_axis=0, concat_axis=0, ti...  5.43 us
    pallas_call x1, Pallas kernels, halved_projection(): call(kernel, 48, grid_spec=pltpu.PrefetchScalarGridSpec(num_scalar_prefet...  5.42 us
    pallas_call x2, Pallas kernels, normed_projection(): call(kernel, 12, in_specs=[pl.BlockSpec(memory_space=pltpu.SMEM)] + [IN_V...  4.63 us
    pallas_call x1, Pallas kernels, neighbour_projection(): call(kernel, 16, in_specs=[IN_VMEM] * (len(stacks) + 1), out_specs=IN_VME...  4.34 us
  transfers between devices with their start and end apart: 50, of which 23 were waited for; matrix products, arithmetic and copies ran while one was open for 7% of the time, Pallas kernels for 6%

profile of v4, /device:TPU:2, one launch (start us, length us, event | category | flops | bytes accessed | tf_op | source)
XLA Modules:
  0.0 172.7 jit_solution(14719685786688771382)
XLA Ops:
  2.5 2.1 %collective-permute-start.3 = (bf16[528,256]{1,0:T(8,128)(2,1)S(1)}, bf16[528,256]{1,0:T(8,128)(2,1)S(1)}, u32[]{:S(2)}, u32[]{:S(2)}) collective-permute-start(bf16[528,256]{1,0:T(8,128)(2,1)S(1)} %get-tuple-element.30), channel_id=1, source_target_pairs={{0,4},{1,5},{2,6},{3,7},{4,0},{5,1},{6,2},{7,3},{8,12},{9,13},{10,... | collective-permute-start | bytes 811016 | tf_op jit(solution)/shard_map/ppermute | solution.py:33
  4.6 3.2 %collective-permute-start.2 = (bf16[528,256]{1,0:T(8,128)(2,1)S(1)}, bf16[528,256]{1,0:T(8,128)(2,1)S(1)}, u32[]{:S(2)}, u32[]{:S(2)}) collective-permute-start(bf16[528,256]{1,0:T(8,128)(2,1)S(1)} %get-tuple-element.30), channel_id=1, source_target_pairs={{0,8},{1,9},{2,10},{3,11},{4,12},{5,13},{6,14},{7,15},{8,0},{9,1},... | collective-permute-start | bytes 811016 | tf_op jit(solution)/shard_map/ppermute | solution.py:33
  7.8 1.4 collective-permute-start.1
  12.1 1.4 gather_fusion
  13.5 5.4 %all-to-all-start = ((bf16[8,4,8,896]{3,2,1,0:T(8,128)(2,1)}), bf16[8,4,8,896]{3,2,1,0:T(8,128)(2,1)S(1)}, u32[]{:S(2)}, u32[]{:S(2)}) async-start(bf16[8,4,8,896]{3,2,1,0:T(8,128)(2,1)} %bitcast.23), calls=%async_computation | async-start | bytes 917504 | tf_op jit(solution)/shard_map/all_to_all | solution.py:459
  19.1 1.5 collective-permute-start.5
  21.2 1.8 %collective-permute-start.6 = (bf16[528,256]{1,0:T(8,128)(2,1)S(1)}, bf16[528,256]{1,0:T(8,128)(2,1)}, u32[]{:S(2)}, u32[]{:S(2)}) collective-permute-start(bf16[528,256]{1,0:T(8,128)(2,1)S(1)} %collective-permute-done.3), channel_id=1, source_target_pairs={{0,8},{1,9},{2,10},{3,11},{4,12},{5,13},{6,14},{7,15},{8,0},{9,1},... | collective-permute-start | bytes 811016 | tf_op jit(solution)/shard_map/ppermute | solution.py:33
  23.1 1.1 pad_maximum_fusion.near_ref.refs_0_
  24.3 4.3 %all-to-all-done = bf16[8,4,8,896]{3,2,1,0:T(8,128)(2,1)S(1)} async-done(((bf16[8,4,8,896]{3,2,1,0:T(8,128)(2,1)}), bf16[8,4,8,896]{3,2,1,0:T(8,128)(2,1)S(1)}, u32[]{:S(2)}, u32[]{:S(2)}) %all-to-all-start) | async-done | bytes 458784 | tf_op jit(solution)/shard_map/all_to_all | solution.py:459
  29.2 2.0 %collective-permute-done.6 = bf16[528,256]{1,0:T(8,128)(2,1)} collective-permute-done((bf16[528,256]{1,0:T(8,128)(2,1)S(1)}, bf16[528,256]{1,0:T(8,128)(2,1)}, u32[]{:S(2)}, u32[]{:S(2)}) %collective-permute-start.6) | collective-permute-done | bytes 270368 | tf_op jit(solution)/shard_map/ppermute | solution.py:33
  31.1 1.3 pad_maximum_fusion.1.far_ref.refs_1_
  32.8 2.6 %collective-permute-done.8.far_partner_ref.refs_3_ = bf16[4,528,256]{2,1,0:T(8,128)(2,1)} collective-permute-done((bf16[4,528,256]{2,1,0:T(8,128)(2,1)S(1)}, bf16[4,528,256]{2,1,0:T(8,128)(2,1)}, u32[]{:S(2)}, u32[]{:S(2)}) %collective-permute-start.8) | collective-permute-done | bytes 1081376 | tf_op jit(solution)/shard_map/ppermute | solution.py:33
  35.4 5.4 %shard_map.128.own_ref = bf16[2,512,256]{2,1,0:T(8,128)(2,1)S(1)} custom-call(s32[16]{0:T(128)S(1)} %stack.161.ids_ref, bf16[4,528,256]{2,1,0:T(8,128)(2,1)S(1)} %pad_maximum_fusion.near_ref.refs_0_, bf16[4,528,256]{2,1,0:T(8,128)(2,1)S(1)} %pad_maximum_fusion.1.far_ref.refs_1_, bf16[4,528,256]{2,1,0:T(8,128)(2,1)} %collective-permute-done.7.near_partner_ref.refs_2_, ...), custom_call_target="tpu_custom_call" | custom-call | flops 2147483648 | bytes 8388608 | tf_op jit(solution)/shard_map/pallas_call | solution.py:239
  40.8 4.9 %collective-permute-start.17 = (bf16[2,512,256]{2,1,0:T(8,128)(2,1)S(1)}, bf16[2,512,256]{2,1,0:T(8,128)(2,1)S(1)}, u32[]{:S(2)}, u32[]{:S(2)}) collective-permute-start(bf16[2,512,256]{2,1,0:T(8,128)(2,1)S(1)} %shard_map.128.own_ref), channel_id=1, source_target_pairs={{0,48},{16,0},{1,49},{17,1},{2,50},{18,2},{3,51},{19,3},{4,52},{20... | collective-permute-start | bytes 1572872 | tf_op jit(solution)/shard_map/ppermute | solution.py:464
  45.7 1.5 collective-permute-start.12
  47.8 3.8 %collective-permute-start.10 = (bf16[128,896]{1,0:T(8,128)(2,1)S(1)}, bf16[128,896]{1,0:T(8,128)(2,1)S(1)}, u32[]{:S(2)}, u32[]{:S(2)}) collective-permute-start(bf16[128,896]{1,0:T(8,128)(2,1)S(1)} %bitcast.126), channel_id=1, source_target_pairs={{0,4},{1,5},{2,6},{3,7},{4,0},{5,1},{6,2},{7,3},{8,12},{9,13},{10,... | collective-permute-start | bytes 688136 | tf_op jit(solution)/shard_map/ppermute | solution.py:33
  51.6 1.7 collective-permute-start.9
  53.3 1.3 collective-permute-start.16
  54.7 2.5 %collective-permute-done.17.b3_ref = bf16[2,512,256]{2,1,0:T(8,128)(2,1)S(1)} collective-permute-done((bf16[2,512,256]{2,1,0:T(8,128)(2,1)S(1)}, bf16[2,512,256]{2,1,0:T(8,128)(2,1)S(1)}, u32[]{:S(2)}, u32[]{:S(2)}) %collective-permute-start.17) | collective-permute-done | bytes 524320 | tf_op jit(solution)/shard_map/ppermute | solution.py:464
  57.2 5.6 %collective-permute-start.18 = (bf16[2,512,256]{2,1,0:T(8,128)(2,1)S(1)}, bf16[2,512,256]{2,1,0:T(8,128)(2,1)S(1)}, u32[]{:S(2)}, u32[]{:S(2)}) collective-permute-start(bf16[2,512,256]{2,1,0:T(8,128)(2,1)S(1)} %collective-permute-done.17.b3_ref), channel_id=1, source_target_pairs={{48,32},{0,48},{49,33},{1,49},{50,34},{2,50},{51,35},{3,51},{52,36... | collective-permute-start | bytes 1572872 | tf_op jit(solution)/shard_map/ppermute | solution.py:464
  62.8 1.5 collective-permute-start.14
  64.9 1.7 collective-permute-start.15
  66.8 2.8 %shard_map.129 = bf16[1,512,256]{2,1,0:T(8,128)(2,1)S(1)} custom-call(s32[16]{0:T(128)S(1)} %stack.161.ids_ref, bf16[4,528,256]{2,1,0:T(8,128)(2,1)S(1)} %pad_maximum_fusion.near_ref.refs_0_, bf16[4,528,256]{2,1,0:T(8,128)(2,1)S(1)} %pad_maximum_fusion.1.far_ref.refs_1_, bf16[4,528,256]{2,1,0:T(8,128)(2,1)} %collective-permute-done.7.near_partner_ref.refs_2_, ...), custom_call_target="tpu_custom_call" | custom-call | flops 1073741824 | bytes 6291456 | tf_op jit(solution)/shard_map/pallas_call | solution.py:179
  69.6 2.8 %collective-permute-done.15 = bf16[128,896]{1,0:T(8,128)(2,1)S(1)} collective-permute-done((bf16[128,896]{1,0:T(8,128)(2,1)S(1)}, bf16[128,896]{1,0:T(8,128)(2,1)S(1)}, u32[]{:S(2)}, u32[]{:S(2)}) %collective-permute-start.15) | collective-permute-done | bytes 229408 | tf_op jit(solution)/shard_map/ppermute | solution.py:33
  72.5 1.1 pad_maximum_fusion.4.refs_1_
  73.6 1.7 shard_map.130.in_ref
  75.3 2.0 %shard_map.133 = bf16[4,512,256]{2,1,0:T(8,128)(2,1)} custom-call(s32[4]{0:T(128)S(1)} %pad_add_fusion.1.ids_ref, bf16[512,256]{1,0:T(8,128)(2,1)S(1)} %shard_map.130.in_ref, bf16[256,4096]{1,0:T(8,128)(2,1)S(1)} %copy-done.1), custom_call_target="tpu_custom_call" | custom-call | flops 268435456 | bytes 1048576 | tf_op jit(solution)/shard_map/pallas_call | solution.py:334
  77.3 2.0 %shard_map.132 = bf16[4,512,256]{2,1,0:T(8,128)(2,1)} custom-call(s32[4]{0:T(128)S(1)} %pad_add_fusion.ids_ref, bf16[512,256]{1,0:T(8,128)(2,1)S(1)} %shard_map.130.in_ref, bf16[256,4096]{1,0:T(8,128)(2,1)S(1)} %copy-done.1), custom_call_target="tpu_custom_call" | custom-call | flops 268435456 | bytes 1048576 | tf_op jit(solution)/shard_map/pallas_call | solution.py:334
  79.7 1.1 pad_maximum_fusion.5.refs_0_
  81.4 1.3 shard_map.131.refs_1_
  83.7 1.6 fusion.15
  85.3 2.1 %collective-permute-start.25 = (bf16[512,256]{1,0:T(8,128)(2,1)S(1)}, bf16[512,256]{1,0:T(8,128)(2,1)S(1)}, u32[]{:S(2)}, u32[]{:S(2)}) collective-permute-start(bf16[512,256]{1,0:T(8,128)(2,1)S(1)} %get-tuple-element.60), channel_id=1, source_target_pairs={{0,6},{1,7},{2,0},{3,1},{4,2},{5,3},{6,4},{7,5},{8,14},{9,15},{10,... | collective-permute-start | bytes 786440 | tf_op jit(solution)/shard_map/ppermute | solution.py:33
  87.4 1.7 collective-permute-start.23
  89.1 4.3 %shard_map.134.kv_ref = bf16[2,8,16,16,256]{4,3,2,1,0:T(8,128)(2,1)S(1)} custom-call(bf16[4,128,896]{2,1,0:T(8,128)(2,1)} %pad_maximum_fusion.5.refs_0_, bf16[4,128,896]{2,1,0:T(8,128)(2,1)} %pad_maximum_fusion.4.refs_1_, bf16[4,128,896]{2,1,0:T(8,128)(2,1)} %collective-permute-done.26.refs_2_, bf16[4,128,896]{2,1,0:T(8,128)(2,1)} %collective-permute-done.27.refs_3_, ...), custom_call_target="tpu_custom_call" | custom-call | flops 1879048192 | bytes 3670016 | tf_op jit(solution)/shard_map/pallas_call | solution.py:363
  93.4 2.5 %collective-permute-start.20 = (bf16[512,256]{1,0:T(8,128)(2,1)S(1)}, bf16[512,256]{1,0:T(8,128)(2,1)S(1)}, u32[]{:S(2)}, u32[]{:S(2)}) collective-permute-start(bf16[512,256]{1,0:T(8,128)(2,1)S(1)} %get-tuple-element.72), channel_id=1, source_target_pairs={{0,2},{1,3},{2,4},{3,5},{4,6},{5,7},{6,0},{7,1},{8,10},{9,11},{10,... | collective-permute-start | bytes 786440 | tf_op jit(solution)/shard_map/ppermute | solution.py:33
  96.9 1.3 fusion.9
  98.2 1.8 %collective-permute-start.29 = (bf16[512,256]{1,0:T(8,128)(2,1)S(1)}, bf16[512,256]{1,0:T(8,128)(2,1)S(1)}, u32[]{:S(2)}, u32[]{:S(2)}) collective-permute-start(bf16[512,256]{1,0:T(8,128)(2,1)S(1)} %get-tuple-element.70), channel_id=1, source_target_pairs={{0,8},{1,9},{2,10},{3,11},{4,12},{5,13},{6,14},{7,15},{8,0},{9,1},... | collective-permute-start | bytes 786440 | tf_op jit(solution)/shard_map/ppermute | solution.py:33
  100.0 4.7 %collective-permute-start.28 = (bf16[512,256]{1,0:T(8,128)(2,1)S(1)}, bf16[512,256]{1,0:T(8,128)(2,1)S(1)}, u32[]{:S(2)}, u32[]{:S(2)}) collective-permute-start(bf16[512,256]{1,0:T(8,128)(2,1)S(1)} %get-tuple-element.71), channel_id=1, source_target_pairs={{0,4},{1,5},{2,6},{3,7},{4,0},{5,1},{6,2},{7,3},{8,12},{9,13},{10,... | collective-permute-start | bytes 786440 | tf_op jit(solution)/shard_map/ppermute | solution.py:33
  105.2 2.0 %collective-permute-done.29.refs_6_ = bf16[512,256]{1,0:T(8,128)(2,1)S(1)} collective-permute-done((bf16[512,256]{1,0:T(8,128)(2,1)S(1)}, bf16[512,256]{1,0:T(8,128)(2,1)S(1)}, u32[]{:S(2)}, u32[]{:S(2)}) %collective-permute-start.29) | collective-permute-done | bytes 262176 | tf_op jit(solution)/shard_map/ppermute | solution.py:33
  107.2 4.2 %collective-permute-done.28.refs_5_ = bf16[512,256]{1,0:T(8,128)(2,1)S(1)} collective-permute-done((bf16[512,256]{1,0:T(8,128)(2,1)S(1)}, bf16[512,256]{1,0:T(8,128)(2,1)S(1)}, u32[]{:S(2)}, u32[]{:S(2)}) %collective-permute-start.28) | collective-permute-done | bytes 262176 | tf_op jit(solution)/shard_map/ppermute | solution.py:33
  111.4 1.7 shard_map.135
  113.1 1.9 %collective-permute-start.33 = (bf16[528,256]{1,0:T(8,128)(2,1)S(1)}, bf16[528,256]{1,0:T(8,128)(2,1)S(1)}, u32[]{:S(2)}, u32[]{:S(2)}) collective-permute-start(bf16[528,256]{1,0:T(8,128)(2,1)S(1)} %get-tuple-element.47), channel_id=1, source_target_pairs={{0,4},{1,5},{2,6},{3,7},{4,0},{5,1},{6,2},{7,3},{8,12},{9,13},{10,... | collective-permute-start | bytes 811016 | tf_op jit(solution)/shard_map/ppermute | solution.py:33
  115.0 1.8 %collective-permute-start.32 = (bf16[528,256]{1,0:T(8,128)(2,1)S(1)}, bf16[528,256]{1,0:T(8,128)(2,1)S(1)}, u32[]{:S(2)}, u32[]{:S(2)}) collective-permute-start(bf16[528,256]{1,0:T(8,128)(2,1)S(1)} %get-tuple-element.47), channel_id=1, source_target_pairs={{0,8},{1,9},{2,10},{3,11},{4,12},{5,13},{6,14},{7,15},{8,0},{9,1},... | collective-permute-start | bytes 811016 | tf_op jit(solution)/shard_map/ppermute | solution.py:33
  116.8 1.3 collective-permute-start.34
  118.2 2.0 %collective-permute-start.30 = (bf16[528,256]{1,0:T(8,128)(2,1)S(1)}, bf16[528,256]{1,0:T(8,128)(2,1)S(1)}, u32[]{:S(2)}, u32[]{:S(2)}) collective-permute-start(bf16[528,256]{1,0:T(8,128)(2,1)S(1)} %get-tuple-element.47), channel_id=1, source_target_pairs={{0,2},{1,3},{2,4},{3,5},{4,6},{5,7},{6,0},{7,1},{8,10},{9,11},{10,... | collective-permute-start | bytes 811016 | tf_op jit(solution)/shard_map/ppermute | solution.py:33
  120.3 1.8 %collective-permute-done.34.earlier_ref = bf16[2,16,16,256]{3,2,1,0:T(8,128)(2,1)S(1)} collective-permute-done((bf16[2,16,16,256]{3,2,1,0:T(8,128)(2,1)S(1)}, bf16[2,16,16,256]{3,2,1,0:T(8,128)(2,1)S(1)}, u32[]{:S(2)}, u32[]{:S(2)}) %collective-permute-start.34) | collective-permute-done | bytes 262176 | tf_op jit(solution)/shard_map/ppermute | solution.py:464
  122.0 2.0 %collective-permute-done.33 = bf16[528,256]{1,0:T(8,128)(2,1)S(1)} collective-permute-done((bf16[528,256]{1,0:T(8,128)(2,1)S(1)}, bf16[528,256]{1,0:T(8,128)(2,1)S(1)}, u32[]{:S(2)}, u32[]{:S(2)}) %collective-permute-start.33) | collective-permute-done | bytes 270368 | tf_op jit(solution)/shard_map/ppermute | solution.py:33
  124.1 1.9 %collective-permute-start.37 = (bf16[528,256]{1,0:T(8,128)(2,1)S(1)}, bf16[528,256]{1,0:T(8,128)(2,1)S(1)}, u32[]{:S(2)}, u32[]{:S(2)}) collective-permute-start(bf16[528,256]{1,0:T(8,128)(2,1)S(1)} %collective-permute-done.33), channel_id=1, source_target_pairs={{0,8},{1,9},{2,10},{3,11},{4,12},{5,13},{6,14},{7,15},{8,0},{9,1},... | collective-permute-start | bytes 811016 | tf_op jit(solution)/shard_map/ppermute | solution.py:33
  125.9 2.0 %collective-permute-start.35 = (bf16[528,256]{1,0:T(8,128)(2,1)S(1)}, bf16[528,256]{1,0:T(8,128)(2,1)S(1)}, u32[]{:S(2)}, u32[]{:S(2)}) collective-permute-start(bf16[528,256]{1,0:T(8,128)(2,1)S(1)} %collective-permute-done.32), channel_id=1, source_target_pairs={{0,2},{1,3},{2,4},{3,5},{4,6},{5,7},{6,0},{7,1},{8,10},{9,11},{10,... | collective-permute-start | bytes 811016 | tf_op jit(solution)/shard_map/ppermute | solution.py:33
  129.0 3.0 %collective-permute-done.37 = bf16[528,256]{1,0:T(8,128)(2,1)S(1)} collective-permute-done((bf16[528,256]{1,0:T(8,128)(2,1)S(1)}, bf16[528,256]{1,0:T(8,128)(2,1)S(1)}, u32[]{:S(2)}, u32[]{:S(2)}) %collective-permute-start.37) | collective-permute-done | bytes 270368 | tf_op jit(solution)/shard_map/ppermute | solution.py:33
  133.2 2.7 %collective-permute-done.39.refs_3_ = bf16[4,528,256]{2,1,0:T(8,128)(2,1)S(1)} collective-permute-done((bf16[4,528,256]{2,1,0:T(8,128)(2,1)S(1)}, bf16[4,528,256]{2,1,0:T(8,128)(2,1)S(1)}, u32[]{:S(2)}, u32[]{:S(2)}) %collective-permute-start.39) | collective-permute-done | bytes 1081376 | tf_op jit(solution)/shard_map/ppermute | solution.py:33
  135.9 1.8 %shard_map.136 = bf16[1,512,256]{2,1,0:T(8,128)(2,1)S(1)} custom-call(s32[16]{0:T(128)S(1)} %stack.161.ids_ref, bf16[4,528,256]{2,1,0:T(8,128)(2,1)S(1)} %pad_maximum_fusion.2.refs_0_, bf16[4,528,256]{2,1,0:T(8,128)(2,1)S(1)} %pad_maximum_fusion.3.refs_1_, bf16[4,528,256]{2,1,0:T(8,128)(2,1)S(1)} %collective-permute-done.38.refs_2_, ...), custom_call_target="tpu_custom_call" | custom-call | flops 1073741824 | bytes 6291456 | tf_op jit(solution)/shard_map/pallas_call | solution.py:179
  141.9 1.3 shard_map.138
  144.1 1.5 collective-permute-done.43
  145.9 1.9 %collective-permute-start.44 = (bf16[512,256]{1,0:T(8,128)(2,1)S(1)}, bf16[512,256]{1,0:T(8,128)(2,1)S(1)}, u32[]{:S(2)}, u32[]{:S(2)}) collective-permute-start(bf16[512,256]{1,0:T(8,128)(2,1)S(1)} %get-tuple-element.65), channel_id=1, source_target_pairs={{0,8},{1,9},{2,10},{3,11},{4,12},{5,13},{6,14},{7,15},{8,0},{9,1},... | collective-permute-start | bytes 786440 | tf_op jit(solution)/shard_map/ppermute | solution.py:33
  147.9 1.2 collective-permute-start.45
  149.1 2.0 %collective-permute-start.46 = (bf16[512,256]{1,0:T(8,128)(2,1)S(1)}, bf16[512,256]{1,0:T(8,128)(2,1)S(1)}, u32[]{:S(2)}, u32[]{:S(2)}) collective-permute-start(bf16[512,256]{1,0:T(8,128)(2,1)S(1)} %get-tuple-element.67), channel_id=1, source_target_pairs={{0,6},{1,7},{2,0},{3,1},{4,2},{5,3},{6,4},{7,5},{8,14},{9,15},{10,... | collective-permute-start | bytes 786440 | tf_op jit(solution)/shard_map/ppermute | solution.py:33
  151.1 3.2 %collective-permute-start.42 = (bf16[512,256]{1,0:T(8,128)(2,1)S(1)}, bf16[512,256]{1,0:T(8,128)(2,1)S(1)}, u32[]{:S(2)}, u32[]{:S(2)}) collective-permute-start(bf16[512,256]{1,0:T(8,128)(2,1)S(1)} %get-tuple-element.56), channel_id=1, source_target_pairs={{0,6},{1,7},{2,0},{3,1},{4,2},{5,3},{6,4},{7,5},{8,14},{9,15},{10,... | collective-permute-start | bytes 786440 | tf_op jit(solution)/shard_map/ppermute | solution.py:33
  154.3 1.6 collective-permute-done.44
  155.9 2.3 %collective-permute-done.45 = bf16[512,256]{1,0:T(8,128)(2,1)S(1)} collective-permute-done((bf16[512,256]{1,0:T(8,128)(2,1)S(1)}, bf16[512,256]{1,0:T(8,128)(2,1)S(1)}, u32[]{:S(2)}, u32[]{:S(2)}) %collective-permute-start.45) | collective-permute-done | bytes 262176 | tf_op jit(solution)/shard_map/ppermute | solution.py:33
  158.6 5.3 %collective-permute-start.47 = (bf16[512,256]{1,0:T(8,128)(2,1)S(1)}, bf16[512,256]{1,0:T(8,128)(2,1)S(1)}, u32[]{:S(2)}, u32[]{:S(2)}) collective-permute-start(bf16[512,256]{1,0:T(8,128)(2,1)S(1)} %get-tuple-element.68), channel_id=1, source_target_pairs={{0,4},{1,5},{2,6},{3,7},{4,0},{5,1},{6,2},{7,3},{8,12},{9,13},{10,... | collective-permute-start | bytes 786440 | tf_op jit(solution)/shard_map/ppermute | solution.py:33
  163.9 1.5 collective-permute-start.48
  165.4 5.0 %collective-permute-done.47 = bf16[512,256]{1,0:T(8,128)(2,1)S(1)} collective-permute-done((bf16[512,256]{1,0:T(8,128)(2,1)S(1)}, bf16[512,256]{1,0:T(8,128)(2,1)S(1)}, u32[]{:S(2)}, u32[]{:S(2)}) %collective-permute-start.47) | collective-permute-done | bytes 262176 | tf_op jit(solution)/shard_map/ppermute | solution.py:33
  170.4 1.4 collective-permute-done.48
  (106 shorter events, 21.1 us)
Async XLA Ops:
  0.0 12.1 %copy-start = (bf16[64,8,896]{2,1,0:T(8,128)(2,1)S(1)}, bf16[64,8,896]{2,1,0:T(8,128)(2,1)}, u32[]{:S(2)}) copy-start(bf16[64,8,896]{2,1,0:T(8,128)(2,1)} %param.23) | copy-start | bytes 2752516
  0.0 1.0 copy-start.5
  1.0 0.7 copy-start.8
  2.5 16.6 %collective-permute-start.3 = (bf16[528,256]{1,0:T(8,128)(2,1)S(1)}, bf16[528,256]{1,0:T(8,128)(2,1)S(1)}, u32[]{:S(2)}, u32[]{:S(2)}) collective-permute-start(bf16[528,256]{1,0:T(8,128)(2,1)S(1)} %get-tuple-element.30), channel_id=1, source_target_pairs={{0,4},{1,5},{2,6},{3,7},{4,0},{5,1},{6,2},{7,3},{8,12},{9,13},{10,... | collective-permute-start | bytes 811016 | tf_op jit(solution)/shard_map/ppermute | solution.py:33
  4.6 14.5 %collective-permute-start.2 = (bf16[528,256]{1,0:T(8,128)(2,1)S(1)}, bf16[528,256]{1,0:T(8,128)(2,1)S(1)}, u32[]{:S(2)}, u32[]{:S(2)}) collective-permute-start(bf16[528,256]{1,0:T(8,128)(2,1)S(1)} %get-tuple-element.30), channel_id=1, source_target_pairs={{0,8},{1,9},{2,10},{3,11},{4,12},{5,13},{6,14},{7,15},{8,0},{9,1},... | collective-permute-start | bytes 811016 | tf_op jit(solution)/shard_map/ppermute | solution.py:33
  7.8 15.3 %collective-permute-start.1 = (bf16[528,256]{1,0:T(8,128)(2,1)S(1)}, bf16[528,256]{1,0:T(8,128)(2,1)S(1)}, u32[]{:S(2)}, u32[]{:S(2)}) collective-permute-start(bf16[528,256]{1,0:T(8,128)(2,1)S(1)} %get-tuple-element.30), channel_id=1, source_target_pairs={{0,6},{1,7},{2,0},{3,1},{4,2},{5,3},{6,4},{7,5},{8,14},{9,15},{10,... | collective-permute-start | bytes 811016 | tf_op jit(solution)/shard_map/ppermute | solution.py:33
  9.3 13.9 %collective-permute-start = (bf16[528,256]{1,0:T(8,128)(2,1)S(1)}, bf16[528,256]{1,0:T(8,128)(2,1)}, u32[]{:S(2)}, u32[]{:S(2)}) collective-permute-start(bf16[528,256]{1,0:T(8,128)(2,1)S(1)} %get-tuple-element.30), channel_id=1, source_target_pairs={{0,2},{1,3},{2,4},{3,5},{4,6},{5,7},{6,0},{7,1},{8,10},{9,11},{10,... | collective-permute-start | bytes 811016 | tf_op jit(solution)/shard_map/ppermute | solution.py:33
  13.5 15.1 %all-to-all-start = ((bf16[8,4,8,896]{3,2,1,0:T(8,128)(2,1)}), bf16[8,4,8,896]{3,2,1,0:T(8,128)(2,1)S(1)}, u32[]{:S(2)}, u32[]{:S(2)}) async-start(bf16[8,4,8,896]{3,2,1,0:T(8,128)(2,1)} %bitcast.23), calls=%async_computation | async-start | bytes 917504 | tf_op jit(solution)/shard_map/all_to_all | solution.py:459
  19.1 12.0 %copy-start.10 = (bf16[528,256]{1,0:T(8,128)(2,1)}, bf16[528,256]{1,0:T(8,128)(2,1)S(1)}, u32[]{:S(2)}) copy-start(bf16[528,256]{1,0:T(8,128)(2,1)S(1)} %collective-permute-done.2) | copy-start | bytes 811012
  19.1 12.0 %collective-permute-start.5 = (bf16[528,256]{1,0:T(8,128)(2,1)S(1)}, bf16[528,256]{1,0:T(8,128)(2,1)}, u32[]{:S(2)}, u32[]{:S(2)}) collective-permute-start(bf16[528,256]{1,0:T(8,128)(2,1)S(1)} %collective-permute-done.2), channel_id=1, source_target_pairs={{0,6},{1,7},{2,0},{3,1},{4,2},{5,3},{6,4},{7,5},{8,14},{9,15},{10,... | collective-permute-start | bytes 811016 | tf_op jit(solution)/shard_map/ppermute | solution.py:33
  20.7 10.5 %collective-permute-start.4 = (bf16[528,256]{1,0:T(8,128)(2,1)S(1)}, bf16[528,256]{1,0:T(8,128)(2,1)}, u32[]{:S(2)}, u32[]{:S(2)}) collective-permute-start(bf16[528,256]{1,0:T(8,128)(2,1)S(1)} %collective-permute-done.2), channel_id=1, source_target_pairs={{0,2},{1,3},{2,4},{3,5},{4,6},{5,7},{6,0},{7,1},{8,10},{9,11},{10,... | collective-permute-start | bytes 811016 | tf_op jit(solution)/shard_map/ppermute | solution.py:33
  21.2 9.9 %collective-permute-start.6 = (bf16[528,256]{1,0:T(8,128)(2,1)S(1)}, bf16[528,256]{1,0:T(8,128)(2,1)}, u32[]{:S(2)}, u32[]{:S(2)}) collective-permute-start(bf16[528,256]{1,0:T(8,128)(2,1)S(1)} %collective-permute-done.3), channel_id=1, source_target_pairs={{0,8},{1,9},{2,10},{3,11},{4,12},{5,13},{6,14},{7,15},{8,0},{9,1},... | collective-permute-start | bytes 811016 | tf_op jit(solution)/shard_map/ppermute | solution.py:33
  24.2 8.6 %collective-permute-start.7 = (bf16[4,528,256]{2,1,0:T(8,128)(2,1)S(1)}, bf16[4,528,256]{2,1,0:T(8,128)(2,1)}, u32[]{:S(2)}, u32[]{:S(2)}) collective-permute-start(bf16[4,528,256]{2,1,0:T(8,128)(2,1)S(1)} %pad_maximum_fusion.near_ref.refs_0_), channel_id=1, source_target_pairs={{0,1},{1,0},{2,3},{3,2},{4,5},{5,4},{6,7},{7,6},{8,9},{9,8},{10,11... | collective-permute-start | bytes 3244040 | tf_op jit(solution)/shard_map/ppermute | solution.py:33
  32.5 2.9 %collective-permute-start.8 = (bf16[4,528,256]{2,1,0:T(8,128)(2,1)S(1)}, bf16[4,528,256]{2,1,0:T(8,128)(2,1)}, u32[]{:S(2)}, u32[]{:S(2)}) collective-permute-start(bf16[4,528,256]{2,1,0:T(8,128)(2,1)S(1)} %pad_maximum_fusion.1.far_ref.refs_1_), channel_id=1, source_target_pairs={{0,1},{1,0},{2,3},{3,2},{4,5},{5,4},{6,7},{7,6},{8,9},{9,8},{10,11... | collective-permute-start | bytes 3244040 | tf_op jit(solution)/shard_map/ppermute | solution.py:33
  35.4 31.4 %copy-start.3 = (bf16[4096,256]{1,0:T(8,128)(2,1)S(1)}, bf16[4096,256]{1,0:T(8,128)(2,1)}, u32[]{:S(2)}) copy-start(bf16[4096,256]{1,0:T(8,128)(2,1)} %refs_4_.3) | copy-start | bytes 6291460
  40.8 16.4 %collective-permute-start.17 = (bf16[2,512,256]{2,1,0:T(8,128)(2,1)S(1)}, bf16[2,512,256]{2,1,0:T(8,128)(2,1)S(1)}, u32[]{:S(2)}, u32[]{:S(2)}) collective-permute-start(bf16[2,512,256]{2,1,0:T(8,128)(2,1)S(1)} %shard_map.128.own_ref), channel_id=1, source_target_pairs={{0,48},{16,0},{1,49},{17,1},{2,50},{18,2},{3,51},{19,3},{4,52},{20... | collective-permute-start | bytes 1572872 | tf_op jit(solution)/shard_map/ppermute | solution.py:464
  45.7 7.6 %collective-permute-start.12 = (bf16[128,896]{1,0:T(8,128)(2,1)S(1)}, bf16[128,896]{1,0:T(8,128)(2,1)S(1)}, u32[]{:S(2)}, u32[]{:S(2)}) collective-permute-start(bf16[128,896]{1,0:T(8,128)(2,1)S(1)} %bitcast.124), channel_id=1, source_target_pairs={{0,6},{1,7},{2,0},{3,1},{4,2},{5,3},{6,4},{7,5},{8,14},{9,15},{10,... | collective-permute-start | bytes 688136 | tf_op jit(solution)/shard_map/ppermute | solution.py:33
  47.2 15.6 %collective-permute-start.11 = (bf16[128,896]{1,0:T(8,128)(2,1)S(1)}, bf16[128,896]{1,0:T(8,128)(2,1)S(1)}, u32[]{:S(2)}, u32[]{:S(2)}) collective-permute-start(bf16[128,896]{1,0:T(8,128)(2,1)S(1)} %bitcast.125), channel_id=1, source_target_pairs={{0,2},{1,3},{2,4},{3,5},{4,6},{5,7},{6,0},{7,1},{8,10},{9,11},{10,... | collective-permute-start | bytes 688136 | tf_op jit(solution)/shard_map/ppermute | solution.py:33
  47.8 15.0 %collective-permute-start.10 = (bf16[128,896]{1,0:T(8,128)(2,1)S(1)}, bf16[128,896]{1,0:T(8,128)(2,1)S(1)}, u32[]{:S(2)}, u32[]{:S(2)}) collective-permute-start(bf16[128,896]{1,0:T(8,128)(2,1)S(1)} %bitcast.126), channel_id=1, source_target_pairs={{0,4},{1,5},{2,6},{3,7},{4,0},{5,1},{6,2},{7,3},{8,12},{9,13},{10,... | collective-permute-start | bytes 688136 | tf_op jit(solution)/shard_map/ppermute | solution.py:33
  51.6 11.2 %collective-permute-start.9 = (bf16[128,896]{1,0:T(8,128)(2,1)S(1)}, bf16[128,896]{1,0:T(8,128)(2,1)S(1)}, u32[]{:S(2)}, u32[]{:S(2)}) collective-permute-start(bf16[128,896]{1,0:T(8,128)(2,1)S(1)} %bitcast.127), channel_id=1, source_target_pairs={{0,8},{1,9},{2,10},{3,11},{4,12},{5,13},{6,14},{7,15},{8,0},{9,1},... | collective-permute-start | bytes 688136 | tf_op jit(solution)/shard_map/ppermute | solution.py:33
  53.3 20.2 %collective-permute-start.16 = (bf16[2,512,256]{2,1,0:T(8,128)(2,1)S(1)}, bf16[2,512,256]{2,1,0:T(8,128)(2,1)S(1)}, u32[]{:S(2)}, u32[]{:S(2)}) collective-permute-start(bf16[2,512,256]{2,1,0:T(8,128)(2,1)S(1)} %shard_map.128.own_ref), channel_id=1, source_target_pairs={{0,16},{16,32},{32,48},{1,17},{17,33},{33,49},{2,18},{18,34},{34,5... | collective-permute-start | bytes 1572872 | tf_op jit(solution)/shard_map/ppermute | solution.py:464
  57.2 16.4 %collective-permute-start.18 = (bf16[2,512,256]{2,1,0:T(8,128)(2,1)S(1)}, bf16[2,512,256]{2,1,0:T(8,128)(2,1)S(1)}, u32[]{:S(2)}, u32[]{:S(2)}) collective-permute-start(bf16[2,512,256]{2,1,0:T(8,128)(2,1)S(1)} %collective-permute-done.17.b3_ref), channel_id=1, source_target_pairs={{48,32},{0,48},{49,33},{1,49},{50,34},{2,50},{51,35},{3,51},{52,36... | collective-permute-start | bytes 1572872 | tf_op jit(solution)/shard_map/ppermute | solution.py:464
  62.8 9.6 %collective-permute-start.14 = (bf16[128,896]{1,0:T(8,128)(2,1)S(1)}, bf16[128,896]{1,0:T(8,128)(2,1)S(1)}, u32[]{:S(2)}, u32[]{:S(2)}) collective-permute-start(bf16[128,896]{1,0:T(8,128)(2,1)S(1)} %collective-permute-done.9), channel_id=1, source_target_pairs={{0,6},{1,7},{2,0},{3,1},{4,2},{5,3},{6,4},{7,5},{8,14},{9,15},{10,... | collective-permute-start | bytes 688136 | tf_op jit(solution)/shard_map/ppermute | solution.py:33
  64.3 8.1 %collective-permute-start.13 = (bf16[128,896]{1,0:T(8,128)(2,1)S(1)}, bf16[128,896]{1,0:T(8,128)(2,1)S(1)}, u32[]{:S(2)}, u32[]{:S(2)}) collective-permute-start(bf16[128,896]{1,0:T(8,128)(2,1)S(1)} %collective-permute-done.9), channel_id=1, source_target_pairs={{0,2},{1,3},{2,4},{3,5},{4,6},{5,7},{6,0},{7,1},{8,10},{9,11},{10,... | collective-permute-start | bytes 688136 | tf_op jit(solution)/shard_map/ppermute | solution.py:33
  64.9 7.5 %collective-permute-start.15 = (bf16[128,896]{1,0:T(8,128)(2,1)S(1)}, bf16[128,896]{1,0:T(8,128)(2,1)S(1)}, u32[]{:S(2)}, u32[]{:S(2)}) collective-permute-start(bf16[128,896]{1,0:T(8,128)(2,1)S(1)} %collective-permute-done.10), channel_id=1, source_target_pairs={{0,8},{1,9},{2,10},{3,11},{4,12},{5,13},{6,14},{7,15},{8,0},{9,1},... | collective-permute-start | bytes 688136 | tf_op jit(solution)/shard_map/ppermute | solution.py:33
  73.6 1.7 copy-start.1
  79.2 3.5 %collective-permute-start.19 = (bf16[4,512,256]{2,1,0:T(8,128)(2,1)}, bf16[4,512,256]{2,1,0:T(8,128)(2,1)}, u32[]{:S(2)}, u32[]{:S(2)}) collective-permute-start(bf16[4,512,256]{2,1,0:T(8,128)(2,1)} %shard_map.132), channel_id=1, source_target_pairs={{0,1},{1,0},{2,3},{3,2},{4,5},{5,4},{6,7},{7,6},{8,9},{9,8},{10,11... | collective-permute-start | bytes 3145736 | tf_op jit(solution)/shard_map/ppermute | solution.py:33
  79.2 4.5 %collective-permute-start.22 = (bf16[4,512,256]{2,1,0:T(8,128)(2,1)}, bf16[4,512,256]{2,1,0:T(8,128)(2,1)}, u32[]{:S(2)}, u32[]{:S(2)}) collective-permute-start(bf16[4,512,256]{2,1,0:T(8,128)(2,1)} %shard_map.133), channel_id=1, source_target_pairs={{0,1},{1,0},{2,3},{3,2},{4,5},{5,4},{6,7},{7,6},{8,9},{9,8},{10,11... | collective-permute-start | bytes 3145736 | tf_op jit(solution)/shard_map/ppermute | solution.py:33
  80.8 8.3 %collective-permute-start.26 = (bf16[4,128,896]{2,1,0:T(8,128)(2,1)}, bf16[4,128,896]{2,1,0:T(8,128)(2,1)}, u32[]{:S(2)}, u32[]{:S(2)}) collective-permute-start(bf16[4,128,896]{2,1,0:T(8,128)(2,1)} %pad_maximum_fusion.5.refs_0_), channel_id=1, source_target_pairs={{0,1},{1,0},{2,3},{3,2},{4,5},{5,4},{6,7},{7,6},{8,9},{9,8},{10,11... | collective-permute-start | bytes 2752520 | tf_op jit(solution)/shard_map/ppermute | solution.py:33
  80.8 8.3 %collective-permute-start.27 = (bf16[4,128,896]{2,1,0:T(8,128)(2,1)}, bf16[4,128,896]{2,1,0:T(8,128)(2,1)}, u32[]{:S(2)}, u32[]{:S(2)}) collective-permute-start(bf16[4,128,896]{2,1,0:T(8,128)(2,1)} %pad_maximum_fusion.4.refs_1_), channel_id=1, source_target_pairs={{0,1},{1,0},{2,3},{3,2},{4,5},{5,4},{6,7},{7,6},{8,9},{9,8},{10,11... | collective-permute-start | bytes 2752520 | tf_op jit(solution)/shard_map/ppermute | solution.py:33
  82.7 6.4 %copy-start.9 = (bf16[2,896,256]{2,1,0:T(8,128)(2,1)S(1)}, bf16[2,896,256]{2,1,0:T(8,128)(2,1)}, u32[]{:S(2)}) copy-start(bf16[2,896,256]{2,1,0:T(8,128)(2,1)} %refs_4_.4) | copy-start | bytes 2752516
  85.3 11.5 %collective-permute-start.25 = (bf16[512,256]{1,0:T(8,128)(2,1)S(1)}, bf16[512,256]{1,0:T(8,128)(2,1)S(1)}, u32[]{:S(2)}, u32[]{:S(2)}) collective-permute-start(bf16[512,256]{1,0:T(8,128)(2,1)S(1)} %get-tuple-element.60), channel_id=1, source_target_pairs={{0,6},{1,7},{2,0},{3,1},{4,2},{5,3},{6,4},{7,5},{8,14},{9,15},{10,... | collective-permute-start | bytes 786440 | tf_op jit(solution)/shard_map/ppermute | solution.py:33
  87.4 9.4 %collective-permute-start.24 = (bf16[512,256]{1,0:T(8,128)(2,1)S(1)}, bf16[512,256]{1,0:T(8,128)(2,1)S(1)}, u32[]{:S(2)}, u32[]{:S(2)}) collective-permute-start(bf16[512,256]{1,0:T(8,128)(2,1)S(1)} %get-tuple-element.61), channel_id=1, source_target_pairs={{0,2},{1,3},{2,4},{3,5},{4,6},{5,7},{6,0},{7,1},{8,10},{9,11},{10,... | collective-permute-start | bytes 786440 | tf_op jit(solution)/shard_map/ppermute | solution.py:33
  87.4 9.6 %collective-permute-start.23 = (bf16[512,256]{1,0:T(8,128)(2,1)S(1)}, bf16[512,256]{1,0:T(8,128)(2,1)S(1)}, u32[]{:S(2)}, u32[]{:S(2)}) collective-permute-start(bf16[512,256]{1,0:T(8,128)(2,1)S(1)} %get-tuple-element.62), channel_id=1, source_target_pairs={{0,8},{1,9},{2,10},{3,11},{4,12},{5,13},{6,14},{7,15},{8,0},{9,1},... | collective-permute-start | bytes 786440 | tf_op jit(solution)/shard_map/ppermute | solution.py:33
  93.4 11.3 %collective-permute-start.20 = (bf16[512,256]{1,0:T(8,128)(2,1)S(1)}, bf16[512,256]{1,0:T(8,128)(2,1)S(1)}, u32[]{:S(2)}, u32[]{:S(2)}) collective-permute-start(bf16[512,256]{1,0:T(8,128)(2,1)S(1)} %get-tuple-element.72), channel_id=1, source_target_pairs={{0,2},{1,3},{2,4},{3,5},{4,6},{5,7},{6,0},{7,1},{8,10},{9,11},{10,... | collective-permute-start | bytes 786440 | tf_op jit(solution)/shard_map/ppermute | solution.py:33
  96.0 15.4 %copy-start.6 = (bf16[1,512,256]{2,1,0:T(8,128)(2,1)S(1)}, bf16[1,512,256]{2,1,0:T(8,128)(2,1)}, u32[]{:S(2)}) copy-start(bf16[1,512,256]{2,1,0:T(8,128)(2,1)} %param.13) | copy-start | bytes 786436
  96.0 15.4 %copy-start.7 = (f32[4096]{0:T(1024)S(1)}, f32[4096]{0:T(1024)}, u32[]{:S(2)}) copy-start(f32[4096]{0:T(1024)} %param.15) | copy-start | bytes 49156
  96.0 9.2 %collective-permute-start.21 = (bf16[512,256]{1,0:T(8,128)(2,1)S(1)}, bf16[512,256]{1,0:T(8,128)(2,1)S(1)}, u32[]{:S(2)}, u32[]{:S(2)}) collective-permute-start(bf16[512,256]{1,0:T(8,128)(2,1)S(1)} %get-tuple-element.73), channel_id=1, source_target_pairs={{0,6},{1,7},{2,0},{3,1},{4,2},{5,3},{6,4},{7,5},{8,14},{9,15},{10,... | collective-permute-start | bytes 786440 | tf_op jit(solution)/shard_map/ppermute | solution.py:33
  98.2 9.0 %collective-permute-start.29 = (bf16[512,256]{1,0:T(8,128)(2,1)S(1)}, bf16[512,256]{1,0:T(8,128)(2,1)S(1)}, u32[]{:S(2)}, u32[]{:S(2)}) collective-permute-start(bf16[512,256]{1,0:T(8,128)(2,1)S(1)} %get-tuple-element.70), channel_id=1, source_target_pairs={{0,8},{1,9},{2,10},{3,11},{4,12},{5,13},{6,14},{7,15},{8,0},{9,1},... | collective-permute-start | bytes 786440 | tf_op jit(solution)/shard_map/ppermute | solution.py:33
  100.0 11.4 %collective-permute-start.28 = (bf16[512,256]{1,0:T(8,128)(2,1)S(1)}, bf16[512,256]{1,0:T(8,128)(2,1)S(1)}, u32[]{:S(2)}, u32[]{:S(2)}) collective-permute-start(bf16[512,256]{1,0:T(8,128)(2,1)S(1)} %get-tuple-element.71), channel_id=1, source_target_pairs={{0,4},{1,5},{2,6},{3,7},{4,0},{5,1},{6,2},{7,3},{8,12},{9,13},{10,... | collective-permute-start | bytes 786440 | tf_op jit(solution)/shard_map/ppermute | solution.py:33
  113.1 11.0 %collective-permute-start.33 = (bf16[528,256]{1,0:T(8,128)(2,1)S(1)}, bf16[528,256]{1,0:T(8,128)(2,1)S(1)}, u32[]{:S(2)}, u32[]{:S(2)}) collective-permute-start(bf16[528,256]{1,0:T(8,128)(2,1)S(1)} %get-tuple-element.47), channel_id=1, source_target_pairs={{0,4},{1,5},{2,6},{3,7},{4,0},{5,1},{6,2},{7,3},{8,12},{9,13},{10,... | collective-permute-start | bytes 811016 | tf_op jit(solution)/shard_map/ppermute | solution.py:33
  115.0 9.1 %collective-permute-start.32 = (bf16[528,256]{1,0:T(8,128)(2,1)S(1)}, bf16[528,256]{1,0:T(8,128)(2,1)S(1)}, u32[]{:S(2)}, u32[]{:S(2)}) collective-permute-start(bf16[528,256]{1,0:T(8,128)(2,1)S(1)} %get-tuple-element.47), channel_id=1, source_target_pairs={{0,8},{1,9},{2,10},{3,11},{4,12},{5,13},{6,14},{7,15},{8,0},{9,1},... | collective-permute-start | bytes 811016 | tf_op jit(solution)/shard_map/ppermute | solution.py:33
  116.8 5.2 %collective-permute-start.34 = (bf16[2,16,16,256]{3,2,1,0:T(8,128)(2,1)S(1)}, bf16[2,16,16,256]{3,2,1,0:T(8,128)(2,1)S(1)}, u32[]{:S(2)}, u32[]{:S(2)}) collective-permute-start(bf16[2,16,16,256]{3,2,1,0:T(8,128)(2,1)S(1)} %slice_bitcast_fusion.2), channel_id=1, source_target_pairs={{0,16},{16,32},{32,48},{1,17},{17,33},{33,49},{2,18},{18,34},{34,5... | collective-permute-start | bytes 786440 | tf_op jit(solution)/shard_map/ppermute | solution.py:464
  118.2 10.6 %collective-permute-start.31 = (bf16[528,256]{1,0:T(8,128)(2,1)S(1)}, bf16[528,256]{1,0:T(8,128)(2,1)S(1)}, u32[]{:S(2)}, u32[]{:S(2)}) collective-permute-start(bf16[528,256]{1,0:T(8,128)(2,1)S(1)} %get-tuple-element.47), channel_id=1, source_target_pairs={{0,6},{1,7},{2,0},{3,1},{4,2},{5,3},{6,4},{7,5},{8,14},{9,15},{10,... | collective-permute-start | bytes 811016 | tf_op jit(solution)/shard_map/ppermute | solution.py:33
  118.2 10.5 %collective-permute-start.30 = (bf16[528,256]{1,0:T(8,128)(2,1)S(1)}, bf16[528,256]{1,0:T(8,128)(2,1)S(1)}, u32[]{:S(2)}, u32[]{:S(2)}) collective-permute-start(bf16[528,256]{1,0:T(8,128)(2,1)S(1)} %get-tuple-element.47), channel_id=1, source_target_pairs={{0,2},{1,3},{2,4},{3,5},{4,6},{5,7},{6,0},{7,1},{8,10},{9,11},{10,... | collective-permute-start | bytes 811016 | tf_op jit(solution)/shard_map/ppermute | solution.py:33
  124.1 8.0 %collective-permute-start.37 = (bf16[528,256]{1,0:T(8,128)(2,1)S(1)}, bf16[528,256]{1,0:T(8,128)(2,1)S(1)}, u32[]{:S(2)}, u32[]{:S(2)}) collective-permute-start(bf16[528,256]{1,0:T(8,128)(2,1)S(1)} %collective-permute-done.33), channel_id=1, source_target_pairs={{0,8},{1,9},{2,10},{3,11},{4,12},{5,13},{6,14},{7,15},{8,0},{9,1},... | collective-permute-start | bytes 811016 | tf_op jit(solution)/shard_map/ppermute | solution.py:33
  125.9 7.1 %collective-permute-start.36 = (bf16[528,256]{1,0:T(8,128)(2,1)S(1)}, bf16[528,256]{1,0:T(8,128)(2,1)S(1)}, u32[]{:S(2)}, u32[]{:S(2)}) collective-permute-start(bf16[528,256]{1,0:T(8,128)(2,1)S(1)} %collective-permute-done.32), channel_id=1, source_target_pairs={{0,6},{1,7},{2,0},{3,1},{4,2},{5,3},{6,4},{7,5},{8,14},{9,15},{10,... | collective-permute-start | bytes 811016 | tf_op jit(solution)/shard_map/ppermute | solution.py:33
  125.9 7.1 %collective-permute-start.35 = (bf16[528,256]{1,0:T(8,128)(2,1)S(1)}, bf16[528,256]{1,0:T(8,128)(2,1)S(1)}, u32[]{:S(2)}, u32[]{:S(2)}) collective-permute-start(bf16[528,256]{1,0:T(8,128)(2,1)S(1)} %collective-permute-done.32), channel_id=1, source_target_pairs={{0,2},{1,3},{2,4},{3,5},{4,6},{5,7},{6,0},{7,1},{8,10},{9,11},{10,... | collective-permute-start | bytes 811016 | tf_op jit(solution)/shard_map/ppermute | solution.py:33
  128.9 4.3 %collective-permute-start.38 = (bf16[4,528,256]{2,1,0:T(8,128)(2,1)S(1)}, bf16[4,528,256]{2,1,0:T(8,128)(2,1)S(1)}, u32[]{:S(2)}, u32[]{:S(2)}) collective-permute-start(bf16[4,528,256]{2,1,0:T(8,128)(2,1)S(1)} %pad_maximum_fusion.2.refs_0_), channel_id=1, source_target_pairs={{0,1},{1,0},{2,3},{3,2},{4,5},{5,4},{6,7},{7,6},{8,9},{9,8},{10,11... | collective-permute-start | bytes 3244040 | tf_op jit(solution)/shard_map/ppermute | solution.py:33
  133.0 2.9 %copy-start.4 = (bf16[4096,256]{1,0:T(8,128)(2,1)S(1)}, bf16[4096,256]{1,0:T(8,128)(2,1)}, u32[]{:S(2)}) copy-start(bf16[4096,256]{1,0:T(8,128)(2,1)} %refs_4_.5) | copy-start | bytes 6291460
  133.1 2.8 %collective-permute-start.39 = (bf16[4,528,256]{2,1,0:T(8,128)(2,1)S(1)}, bf16[4,528,256]{2,1,0:T(8,128)(2,1)S(1)}, u32[]{:S(2)}, u32[]{:S(2)}) collective-permute-start(bf16[4,528,256]{2,1,0:T(8,128)(2,1)S(1)} %pad_maximum_fusion.3.refs_1_), channel_id=1, source_target_pairs={{0,1},{1,0},{2,3},{3,2},{4,5},{5,4},{6,7},{7,6},{8,9},{9,8},{10,11... | collective-permute-start | bytes 3244040 | tf_op jit(solution)/shard_map/ppermute | solution.py:33
  137.7 1.6 copy-start.2
  141.3 2.7 %collective-permute-start.40 = (bf16[4,512,256]{2,1,0:T(8,128)(2,1)S(1)}, bf16[4,512,256]{2,1,0:T(8,128)(2,1)S(1)}, u32[]{:S(2)}, u32[]{:S(2)}) collective-permute-start(bf16[4,512,256]{2,1,0:T(8,128)(2,1)S(1)} %shard_map.139), channel_id=1, source_target_pairs={{0,1},{1,0},{2,3},{3,2},{4,5},{5,4},{6,7},{7,6},{8,9},{9,8},{10,11... | collective-permute-start | bytes 3145736 | tf_op jit(solution)/shard_map/ppermute | solution.py:33
  141.5 4.0 %collective-permute-start.43 = (bf16[4,512,256]{2,1,0:T(8,128)(2,1)S(1)}, bf16[4,512,256]{2,1,0:T(8,128)(2,1)S(1)}, u32[]{:S(2)}, u32[]{:S(2)}) collective-permute-start(bf16[4,512,256]{2,1,0:T(8,128)(2,1)S(1)} %shard_map.140), channel_id=1, source_target_pairs={{0,1},{1,0},{2,3},{3,2},{4,5},{5,4},{6,7},{7,6},{8,9},{9,8},{10,11... | collective-permute-start | bytes 3145736 | tf_op jit(solution)/shard_map/ppermute | solution.py:33
  145.9 9.9 %collective-permute-start.44 = (bf16[512,256]{1,0:T(8,128)(2,1)S(1)}, bf16[512,256]{1,0:T(8,128)(2,1)S(1)}, u32[]{:S(2)}, u32[]{:S(2)}) collective-permute-start(bf16[512,256]{1,0:T(8,128)(2,1)S(1)} %get-tuple-element.65), channel_id=1, source_target_pairs={{0,8},{1,9},{2,10},{3,11},{4,12},{5,13},{6,14},{7,15},{8,0},{9,1},... | collective-permute-start | bytes 786440 | tf_op jit(solution)/shard_map/ppermute | solution.py:33
  147.9 10.3 %collective-permute-start.45 = (bf16[512,256]{1,0:T(8,128)(2,1)S(1)}, bf16[512,256]{1,0:T(8,128)(2,1)S(1)}, u32[]{:S(2)}, u32[]{:S(2)}) collective-permute-start(bf16[512,256]{1,0:T(8,128)(2,1)S(1)} %get-tuple-element.66), channel_id=1, source_target_pairs={{0,2},{1,3},{2,4},{3,5},{4,6},{5,7},{6,0},{7,1},{8,10},{9,11},{10,... | collective-permute-start | bytes 786440 | tf_op jit(solution)/shard_map/ppermute | solution.py:33
  149.1 9.2 %collective-permute-start.46 = (bf16[512,256]{1,0:T(8,128)(2,1)S(1)}, bf16[512,256]{1,0:T(8,128)(2,1)S(1)}, u32[]{:S(2)}, u32[]{:S(2)}) collective-permute-start(bf16[512,256]{1,0:T(8,128)(2,1)S(1)} %get-tuple-element.67), channel_id=1, source_target_pairs={{0,6},{1,7},{2,0},{3,1},{4,2},{5,3},{6,4},{7,5},{8,14},{9,15},{10,... | collective-permute-start | bytes 786440 | tf_op jit(solution)/shard_map/ppermute | solution.py:33
  151.1 14.4 %collective-permute-start.41 = (bf16[512,256]{1,0:T(8,128)(2,1)S(1)}, bf16[512,256]{1,0:T(8,128)(2,1)S(1)}, u32[]{:S(2)}, u32[]{:S(2)}) collective-permute-start(bf16[512,256]{1,0:T(8,128)(2,1)S(1)} %get-tuple-element.55), channel_id=1, source_target_pairs={{0,2},{1,3},{2,4},{3,5},{4,6},{5,7},{6,0},{7,1},{8,10},{9,11},{10,... | collective-permute-start | bytes 786440 | tf_op jit(solution)/shard_map/ppermute | solution.py:33
  151.1 14.3 %collective-permute-start.42 = (bf16[512,256]{1,0:T(8,128)(2,1)S(1)}, bf16[512,256]{1,0:T(8,128)(2,1)S(1)}, u32[]{:S(2)}, u32[]{:S(2)}) collective-permute-start(bf16[512,256]{1,0:T(8,128)(2,1)S(1)} %get-tuple-element.56), channel_id=1, source_target_pairs={{0,6},{1,7},{2,0},{3,1},{4,2},{5,3},{6,4},{7,5},{8,14},{9,15},{10,... | collective-permute-start | bytes 786440 | tf_op jit(solution)/shard_map/ppermute | solution.py:33
  158.6 11.8 %collective-permute-start.47 = (bf16[512,256]{1,0:T(8,128)(2,1)S(1)}, bf16[512,256]{1,0:T(8,128)(2,1)S(1)}, u32[]{:S(2)}, u32[]{:S(2)}) collective-permute-start(bf16[512,256]{1,0:T(8,128)(2,1)S(1)} %get-tuple-element.68), channel_id=1, source_target_pairs={{0,4},{1,5},{2,6},{3,7},{4,0},{5,1},{6,2},{7,3},{8,12},{9,13},{10,... | collective-permute-start | bytes 786440 | tf_op jit(solution)/shard_map/ppermute | solution.py:33
  163.9 7.9 %collective-permute-start.48 = (bf16[512,256]{1,0:T(8,128)(2,1)S(1)}, bf16[512,256]{1,0:T(8,128)(2,1)S(1)}, u32[]{:S(2)}, u32[]{:S(2)}) collective-permute-start(bf16[512,256]{1,0:T(8,128)(2,1)S(1)} %get-tuple-element.69), channel_id=1, source_target_pairs={{0,8},{1,9},{2,10},{3,11},{4,12},{5,13},{6,14},{7,15},{8,0},{9,1},... | collective-permute-start | bytes 786440 | tf_op jit(solution)/shard_map/ppermute | solution.py:33
